TPU v7x, 32 devices: a whole 2x2x4 slice. The times are simulated.
32 devices in a mesh: group: 4 (over x, core), dp: 2 (over y), mp: 4 (over z).
Axes of the slice: x: 2, y: 2, z: 4, core: 2. Of those that a mesh axis runs over, the one named last changes fastest.
Arguments:
- image_tokens: bfloat16 [4, 4, 1024, 1536], P('group', 'dp', None, 'mp'), may hold values from -6 to 6
- text_tokens: bfloat16 [4, 4, 154, 1536], P('group', 'dp', None, 'mp'), may hold values from -6 to 6
- image_modulation: float32 [4, 4, 6, 1536], P('group', 'dp', None, 'mp'), may hold values from -3 to 3
- text_modulation: float32 [4, 4, 6, 1536], P('group', 'dp', None, 'mp'), may hold values from -3 to 3
- image_cotan: bfloat16 [4, 4, 1024, 1536], P('group', 'dp', None, 'mp'), may hold values from -6 to 6
- text_cotan: bfloat16 [4, 4, 154, 1536], P('group', 'dp', None, 'mp'), may hold values from -6 to 6
- group_counts: int32 [4], P('group'), may hold values from 2 to 4, as said below
- global_qkv: float32 [2, 1536, 3, 1536], P(None, ('dp', 'group'), None, 'mp'), may hold values from -1 to 1, as said below
- global_output: float32 [2, 1536, 1536], P(None, ('mp', 'dp', 'group')), may hold values from -1 to 1, as said below
- global_expand: float32 [2, 1536, 6144], P(None, ('dp', 'group'), 'mp'), may hold values from -1 to 1, as said below
- global_reduce: float32 [2, 6144, 1536], P(None, ('mp', 'dp', 'group')), may hold values from -1 to 1, as said below
- global_textqkv: float32 [2, 1536, 3, 1536], P(None, ('dp', 'group'), None, 'mp'), may hold values from -1 to 1, as said below
- global_textout: float32 [2, 1536, 1536], P(None, ('mp', 'dp', 'group')), may hold values from -1 to 1, as said below
- global_textexpand: float32 [2, 1536, 6144], P(None, ('dp', 'group'), 'mp'), may hold values from -1 to 1, as said below
- global_textreduce: float32 [2, 6144, 1536], P(None, ('mp', 'dp', 'group')), may hold values from -1 to 1, as said below
- moments_qkv: float32 [4, 2, 1536, 3, 1536], P('group', None, 'dp', None, 'mp'), may hold values from -1 to 1, as said below
- moments_output: float32 [4, 2, 1536, 1536], P('group', None, ('mp', 'dp')), may hold values from -1 to 1, as said below
- moments_expand: float32 [4, 2, 1536, 6144], P('group', None, 'dp', 'mp'), may hold values from -1 to 1, as said below
- moments_reduce: float32 [4, 2, 6144, 1536], P('group', None, ('mp', 'dp')), may hold values from -1 to 1, as said below
- moments_textqkv: float32 [4, 2, 1536, 3, 1536], P('group', None, 'dp', None, 'mp'), may hold values from -1 to 1, as said below
- moments_textout: float32 [4, 2, 1536, 1536], P('group', None, ('mp', 'dp')), may hold values from -1 to 1, as said below
- moments_textexpand: float32 [4, 2, 1536, 6144], P('group', None, 'dp', 'mp'), may hold values from -1 to 1, as said below
- moments_textreduce: float32 [4, 2, 6144, 1536], P('group', None, ('mp', 'dp')), may hold values from -1 to 1, as said below
Outputs:
- image_result: bfloat16 [4, 4, 1024, 1536], P('group', 'dp', None, 'mp')
- text_result: bfloat16 [4, 4, 154, 1536], P('group', 'dp', None, 'mp')
- image_grad: bfloat16 [4, 4, 1024, 1536], P('group', 'dp', None, 'mp')
- text_grad: bfloat16 [4, 4, 154, 1536], P('group', 'dp', None, 'mp')
- image_modgrad: float32 [4, 4, 6, 1536], P('group', 'dp', None, 'mp')
- text_modgrad: float32 [4, 4, 6, 1536], P('group', 'dp', None, 'mp')
- fresh_qkv: float32 [4, 2, 1536, 3, 1536], P('group', None, 'dp', None, 'mp')
- fresh_output: float32 [4, 2, 1536, 1536], P('group', None, ('mp', 'dp'))
- fresh_expand: float32 [4, 2, 1536, 6144], P('group', None, 'dp', 'mp')
- fresh_reduce: float32 [4, 2, 6144, 1536], P('group', None, ('mp', 'dp'))
- fresh_textqkv: float32 [4, 2, 1536, 3, 1536], P('group', None, 'dp', None, 'mp')
- fresh_textout: float32 [4, 2, 1536, 1536], P('group', None, ('mp', 'dp'))
- fresh_textexpand: float32 [4, 2, 1536, 6144], P('group', None, 'dp', 'mp')
- fresh_textreduce: float32 [4, 2, 6144, 1536], P('group', None, ('mp', 'dp'))
- outer_qkv: float32 [3, 1536, 3, 1536], P(None, ('dp', 'group'), None, 'mp')
- outer_output: float32 [3, 1536, 1536], P(None, ('mp', 'dp', 'group'))
- outer_expand: float32 [3, 1536, 6144], P(None, ('dp', 'group'), 'mp')
- outer_reduce: float32 [3, 6144, 1536], P(None, ('mp', 'dp', 'group'))
- outer_textqkv: float32 [3, 1536, 3, 1536], P(None, ('dp', 'group'), None, 'mp')
- outer_textout: float32 [3, 1536, 1536], P(None, ('mp', 'dp', 'group'))
- outer_textexpand: float32 [3, 1536, 6144], P(None, ('dp', 'group'), 'mp')
- outer_textreduce: float32 [3, 6144, 1536], P(None, ('mp', 'dp', 'group'))
Inputs may be any that keep to these rules, and one draw needn't show every extreme that they name: `group_counts`: live slots of each group; in every draw one group has all 4 live and another exactly 2. `global_qkv`: index 0 is the master weight, index 1 the outer momentum. `global_output`: as global_qkv. `global_expand`: as global_qkv. `global_reduce`: as global_qkv. `global_textqkv`: as global_qkv. `global_textout`: as global_qkv. `global_textexpand`: as global_qkv. `global_textreduce`: as global_qkv. `moments_qkv`: index 1 (second moments) is positive. `moments_output`: index 1 (second moments) is positive. `moments_expand`: index 1 (second moments) is positive. `moments_reduce`: index 1 (second moments) is positive. `moments_textqkv`: index 1 (second moments) is positive. `moments_textout`: index 1 (second moments) is positive. `moments_textexpand`: index 1 (second moments) is positive. `moments_textreduce`: index 1 (second moments) is positive.
All inputs are finite; a program needn't handle non-finite values.
Results may differ from a plain program's by a relative error of at most 0.025.
The roundings to bfloat16 on the way count: a program that leaves them out, or rounds other values in their place, can miss the bound.
Values may be sent and summed in bfloat16 or wider, within the bound.
No kernel may reach another device: no remote copies, remote signals or barrier semaphores. Data moves between devices by JAX's collectives and lax.ppermute only.
A program may use at most 576 MiB of HBM per device.

v0:
```python
from functools import partial

import jax
import jax.numpy as jnp
from jax import lax
from jax.sharding import PartitionSpec as P

HEAD_DIM = 64
STEP = 3


EPS_NORM = 1e-06
BETA_ONE = 0.9
BETA_TWO = 0.95
ADAM_EPS = 1e-08
LEARN_RATE = 0.02
DECAY_RATE = 0.1
OUTER_RATE = 0.7
OUTER_MOMENT = 0.9


def feature_sums(first, second):
    return lax.psum((first, second), "mp")


def spread_rows(rows):
    return lax.all_gather(rows, "mp", axis=1, tiled=True)


def spread_grad(rows):
    return lax.all_gather(rows, "mp", axis=1, tiled=True)


def reduce_branch(partial_rows):
    return lax.psum_scatter(
        partial_rows.astype(jnp.bfloat16), "mp", scatter_dimension=1, tiled=True
    ).astype(jnp.float32)


def reduce_input(partial_rows):
    return lax.psum_scatter(
        partial_rows.astype(jnp.bfloat16), "mp", scatter_dimension=1, tiled=True
    ).astype(jnp.float32)


def standardize(rows, width):
    total, square = feature_sums(jnp.sum(rows, 1), jnp.sum(rows * rows, 1))
    centre = total / width
    inverse = lax.rsqrt(square / width - centre * centre + EPS_NORM)
    return ((rows - centre[:, None]) * inverse[:, None], inverse)


def standardize_back(grad_hat, normed, inverse, width):
    total, cross = feature_sums(jnp.sum(grad_hat, 1), jnp.sum(grad_hat * normed, 1))
    return inverse[:, None] * (
        grad_hat - total[:, None] / width - normed * (cross[:, None] / width)
    )


def attend(inputs, scale):
    query_rows, key_rows, value_rows = inputs
    scores = (
        jnp.einsum("qe,ke->qk", query_rows, key_rows, preferred_element_type=jnp.float32) * scale
    )
    row_max = jnp.max(scores, 1, keepdims=True)
    log_total = row_max + jnp.log(jnp.sum(jnp.exp(scores - row_max), 1, keepdims=True))
    rounded = jnp.exp(scores - log_total).astype(jnp.bfloat16)
    mixed = jnp.dot(rounded, value_rows, preferred_element_type=jnp.float32).astype(jnp.bfloat16)
    return (mixed, log_total[:, 0])


def attend_back(inputs, scale):
    query_rows, key_rows, value_rows, grad_rows, log_total = inputs
    scores = (
        jnp.einsum("qe,ke->qk", query_rows, key_rows, preferred_element_type=jnp.float32) * scale
    )
    probability = jnp.exp(scores - log_total[:, None])
    rounded = probability.astype(jnp.bfloat16)
    value_grad = jnp.einsum("qk,qe->ke", rounded, grad_rows, preferred_element_type=jnp.float32)
    prob_grad = jnp.einsum("qe,ke->qk", grad_rows, value_rows, preferred_element_type=jnp.float32)
    score_grad = (
        probability * (prob_grad - jnp.sum(probability * prob_grad, 1, keepdims=True))
    ).astype(jnp.bfloat16)
    query_grad = jnp.dot(score_grad, key_rows, preferred_element_type=jnp.float32) * scale
    key_grad = (
        jnp.einsum("qk,qe->ke", score_grad, query_rows, preferred_element_type=jnp.float32) * scale
    )
    return jnp.stack([query_grad, key_grad, value_grad]).astype(jnp.bfloat16)


def one_sequence(image, text, image_mod, text_mod, image_cot, text_cot, live, weights):
    (
        qkv_weight,
        out_weight,
        expand_weight,
        reduce_weight,
        tqkv_weight,
        tout_weight,
        texpand_weight,
        treduce_weight,
    ) = weights
    image_len = image.shape[0]
    text_len = text.shape[0]
    local = image.shape[1]
    width = local * lax.axis_size("mp")
    heads = local // HEAD_DIM
    scale = HEAD_DIM ** (-0.5)

    def rows_of(index):
        return jnp.concatenate(
            [
                jnp.broadcast_to(image_mod[index], (image_len, local)),
                jnp.broadcast_to(text_mod[index], (text_len, local)),
            ],
            0,
        )

    def column_sums(values):
        return (jnp.sum(values[:image_len], 0), jnp.sum(values[image_len:], 0))

    joined = jnp.concatenate([image, text], 0).astype(jnp.float32)
    shift_one = rows_of(0)
    scale_one = rows_of(1)
    gate_one = rows_of(2)
    shift_two = rows_of(3)
    scale_two = rows_of(4)
    gate_two = rows_of(5)
    normed_one, inverse_one = standardize(joined, width)
    input_one = (normed_one * (1.0 + scale_one) + shift_one).astype(jnp.bfloat16)
    full_one = spread_rows(input_one)
    projected = jnp.concatenate(
        [
            jnp.einsum(
                "td,dcf->ctf", full_one[:image_len], qkv_weight, preferred_element_type=jnp.float32
            ),
            jnp.einsum(
                "td,dcf->ctf", full_one[image_len:], tqkv_weight, preferred_element_type=jnp.float32
            ),
        ],
        1,
    ).astype(jnp.bfloat16)
    length = projected.shape[1]
    per_head = projected.reshape(3, length, heads, HEAD_DIM).transpose(0, 2, 1, 3)
    mixed_heads, log_totals = lax.map(
        partial(attend, scale=scale), (per_head[0], per_head[1], per_head[2])
    )
    mixed = mixed_heads.transpose(1, 0, 2).reshape(length, local)
    partial_rows = jnp.concatenate(
        [
            jnp.dot(mixed[:image_len], out_weight, preferred_element_type=jnp.float32),
            jnp.dot(mixed[image_len:], tout_weight, preferred_element_type=jnp.float32),
        ],
        0,
    )
    attended = reduce_branch(partial_rows)
    after = joined + gate_one * attended
    normed_two, inverse_two = standardize(after, width)
    input_two = (normed_two * (1.0 + scale_two) + shift_two).astype(jnp.bfloat16)
    full_two = spread_rows(input_two)
    inner = jnp.concatenate(
        [
            jnp.dot(full_two[:image_len], expand_weight, preferred_element_type=jnp.float32),
            jnp.dot(full_two[image_len:], texpand_weight, preferred_element_type=jnp.float32),
        ],
        0,
    )
    activated, gelu_back = jax.vjp(partial(jax.nn.gelu, approximate=True), inner)
    activated = activated.astype(jnp.bfloat16)
    branch = reduce_branch(
        jnp.concatenate(
            [
                jnp.dot(activated[:image_len], reduce_weight, preferred_element_type=jnp.float32),
                jnp.dot(activated[image_len:], treduce_weight, preferred_element_type=jnp.float32),
            ],
            0,
        )
    )
    result = after + gate_two * branch
    image_result = result[:image_len].astype(jnp.bfloat16)
    text_result = result[image_len:].astype(jnp.bfloat16)
    grad_joined = jnp.concatenate([image_cot, text_cot], 0).astype(jnp.float32) * live
    gate_two_rows = grad_joined * branch
    branch_grad = (gate_two * grad_joined).astype(jnp.bfloat16)
    branch_full = spread_grad(branch_grad)
    reduce_grad = jnp.einsum(
        "th,td->hd",
        activated[:image_len],
        branch_full[:image_len],
        preferred_element_type=jnp.float32,
    )
    treduce_grad = jnp.einsum(
        "th,td->hd",
        activated[image_len:],
        branch_full[image_len:],
        preferred_element_type=jnp.float32,
    )
    act_grad = jnp.concatenate(
        [
            jnp.einsum(
                "td,hd->th",
                branch_full[:image_len],
                reduce_weight,
                preferred_element_type=jnp.float32,
            ),
            jnp.einsum(
                "td,hd->th",
                branch_full[image_len:],
                treduce_weight,
                preferred_element_type=jnp.float32,
            ),
        ],
        0,
    )
    inner_grad = gelu_back(act_grad)[0].astype(jnp.bfloat16)
    expand_grad = jnp.einsum(
        "td,th->dh",
        full_two[:image_len],
        inner_grad[:image_len],
        preferred_element_type=jnp.float32,
    )
    texpand_grad = jnp.einsum(
        "td,th->dh",
        full_two[image_len:],
        inner_grad[image_len:],
        preferred_element_type=jnp.float32,
    )
    two_grad = reduce_input(
        jnp.concatenate(
            [
                jnp.einsum(
                    "th,dh->td",
                    inner_grad[:image_len],
                    expand_weight,
                    preferred_element_type=jnp.float32,
                ),
                jnp.einsum(
                    "th,dh->td",
                    inner_grad[image_len:],
                    texpand_weight,
                    preferred_element_type=jnp.float32,
                ),
            ],
            0,
        )
    )
    scaled_two = two_grad * normed_two
    after_grad = grad_joined + standardize_back(
        two_grad * (1.0 + scale_two), normed_two, inverse_two, width
    )
    gate_rows_grad = after_grad * attended
    attended_grad = (gate_one * after_grad).astype(jnp.bfloat16)
    attended_full = spread_grad(attended_grad)
    out_grad = jnp.einsum(
        "tc,td->cd",
        mixed[:image_len],
        attended_full[:image_len],
        preferred_element_type=jnp.float32,
    )
    tout_grad = jnp.einsum(
        "tc,td->cd",
        mixed[image_len:],
        attended_full[image_len:],
        preferred_element_type=jnp.float32,
    )
    mixed_grad = jnp.concatenate(
        [
            jnp.einsum(
                "td,cd->tc",
                attended_full[:image_len],
                out_weight,
                preferred_element_type=jnp.float32,
            ),
            jnp.einsum(
                "td,cd->tc",
                attended_full[image_len:],
                tout_weight,
                preferred_element_type=jnp.float32,
            ),
        ],
        0,
    ).astype(jnp.bfloat16)
    grad_heads = mixed_grad.reshape(length, heads, HEAD_DIM).transpose(1, 0, 2)
    head_grads = lax.map(
        partial(attend_back, scale=scale),
        (per_head[0], per_head[1], per_head[2], grad_heads, log_totals),
    )
    projected_grad = head_grads.transpose(1, 2, 0, 3).reshape(3, length, local)
    qkv_grad = jnp.einsum(
        "td,ctf->dcf",
        full_one[:image_len],
        projected_grad[:, :image_len],
        preferred_element_type=jnp.float32,
    )
    tqkv_grad = jnp.einsum(
        "td,ctf->dcf",
        full_one[image_len:],
        projected_grad[:, image_len:],
        preferred_element_type=jnp.float32,
    )
    one_partial = jnp.concatenate(
        [
            jnp.einsum(
                "ctf,dcf->td",
                projected_grad[:, :image_len],
                qkv_weight,
                preferred_element_type=jnp.float32,
            ),
            jnp.einsum(
                "ctf,dcf->td",
                projected_grad[:, image_len:],
                tqkv_weight,
                preferred_element_type=jnp.float32,
            ),
        ],
        0,
    )
    one_grad = reduce_input(one_partial)
    scaled_grad = one_grad * normed_one
    joined_grad = after_grad + standardize_back(
        one_grad * (1.0 + scale_one), normed_one, inverse_one, width
    )
    pieces = [
        column_sums(values)
        for values in (one_grad, scaled_grad, gate_rows_grad, two_grad, scaled_two, gate_two_rows)
    ]
    image_modgrad = jnp.stack([piece[0] for piece in pieces])
    text_modgrad = jnp.stack([piece[1] for piece in pieces])
    outputs = (
        image_result,
        text_result,
        joined_grad[:image_len].astype(jnp.bfloat16),
        joined_grad[image_len:].astype(jnp.bfloat16),
        image_modgrad,
        text_modgrad,
    )
    return (
        outputs,
        (
            qkv_grad,
            out_grad,
            expand_grad,
            reduce_grad,
            tqkv_grad,
            tout_grad,
            texpand_grad,
            treduce_grad,
        ),
    )


def body(
    image_tokens,
    text_tokens,
    image_modulation,
    text_modulation,
    image_cotan,
    text_cotan,
    group_counts,
    global_qkv,
    global_output,
    global_expand,
    global_reduce,
    global_textqkv,
    global_textout,
    global_textexpand,
    global_textreduce,
    moments_qkv,
    moments_output,
    moments_expand,
    moments_reduce,
    moments_textqkv,
    moments_textout,
    moments_textexpand,
    moments_textreduce,
):
    states = (
        global_qkv,
        global_output,
        global_expand,
        global_reduce,
        global_textqkv,
        global_textout,
        global_textexpand,
        global_textreduce,
    )
    moments = (
        moments_qkv,
        moments_output,
        moments_expand,
        moments_reduce,
        moments_textqkv,
        moments_textout,
        moments_textexpand,
        moments_textreduce,
    )
    owned = (
        lax.all_gather(states[0][0].astype(jnp.bfloat16), "group", axis=0, tiled=True).astype(
            jnp.float32
        ),
        lax.all_gather(states[1][0].astype(jnp.bfloat16), "group", axis=0, tiled=True).astype(
            jnp.float32
        ),
        lax.all_gather(states[2][0].astype(jnp.bfloat16), "group", axis=0, tiled=True).astype(
            jnp.float32
        ),
        lax.all_gather(states[3][0].astype(jnp.bfloat16), "group", axis=0, tiled=True).astype(
            jnp.float32
        ),
        lax.all_gather(states[4][0].astype(jnp.bfloat16), "group", axis=0, tiled=True).astype(
            jnp.float32
        ),
        lax.all_gather(states[5][0].astype(jnp.bfloat16), "group", axis=0, tiled=True).astype(
            jnp.float32
        ),
        lax.all_gather(states[6][0].astype(jnp.bfloat16), "group", axis=0, tiled=True).astype(
            jnp.float32
        ),
        lax.all_gather(states[7][0].astype(jnp.bfloat16), "group", axis=0, tiled=True).astype(
            jnp.float32
        ),
    )
    masters = [piece.astype(jnp.bfloat16) for piece in owned]
    weights = (
        lax.all_gather(masters[0], "dp", axis=0, tiled=True),
        lax.all_gather(masters[1], "dp", axis=0, tiled=True),
        lax.all_gather(masters[2], "dp", axis=0, tiled=True),
        lax.all_gather(masters[3], "dp", axis=0, tiled=True),
        lax.all_gather(masters[4], "dp", axis=0, tiled=True),
        lax.all_gather(masters[5], "dp", axis=0, tiled=True),
        lax.all_gather(masters[6], "dp", axis=0, tiled=True),
        lax.all_gather(masters[7], "dp", axis=0, tiled=True),
    )
    micro_count = image_tokens.shape[1]
    dp_size = lax.axis_size("dp")
    position = lax.axis_index("dp")
    collected = [[], [], [], [], [], []]
    totals = None
    for micro in range(micro_count):
        live = (micro * dp_size + position < group_counts[0]).astype(jnp.float32)
        outputs, grads = one_sequence(
            image_tokens[0, micro],
            text_tokens[0, micro],
            image_modulation[0, micro],
            text_modulation[0, micro],
            image_cotan[0, micro],
            text_cotan[0, micro],
            live,
            weights,
        )
        for place in range(6):
            collected[place].append(outputs[place])
        if totals is None:
            totals = grads
        else:
            totals = tuple((held + more for held, more in zip(totals, grads)))
    totals = (
        lax.psum_scatter(
            totals[0].astype(jnp.bfloat16), "dp", scatter_dimension=0, tiled=True
        ).astype(jnp.float32),
        lax.psum_scatter(
            totals[1].astype(jnp.bfloat16), "dp", scatter_dimension=0, tiled=True
        ).astype(jnp.float32),
        lax.psum_scatter(
            totals[2].astype(jnp.bfloat16), "dp", scatter_dimension=0, tiled=True
        ).astype(jnp.float32),
        lax.psum_scatter(
            totals[3].astype(jnp.bfloat16), "dp", scatter_dimension=0, tiled=True
        ).astype(jnp.float32),
        lax.psum_scatter(
            totals[4].astype(jnp.bfloat16), "dp", scatter_dimension=0, tiled=True
        ).astype(jnp.float32),
        lax.psum_scatter(
            totals[5].astype(jnp.bfloat16), "dp", scatter_dimension=0, tiled=True
        ).astype(jnp.float32),
        lax.psum_scatter(
            totals[6].astype(jnp.bfloat16), "dp", scatter_dimension=0, tiled=True
        ).astype(jnp.float32),
        lax.psum_scatter(
            totals[7].astype(jnp.bfloat16), "dp", scatter_dimension=0, tiled=True
        ).astype(jnp.float32),
    )
    count = group_counts[0].astype(jnp.float32)
    correct_one = 1.0 - BETA_ONE**STEP
    correct_two = 1.0 - BETA_TWO**STEP
    updates = []
    fresh = []
    for master, moment, total in zip(owned, moments, totals):
        gradient = total / count
        first = BETA_ONE * moment[0, 0] + (1.0 - BETA_ONE) * gradient
        second = BETA_TWO * moment[0, 1] + (1.0 - BETA_TWO) * gradient * gradient
        updates.append(
            LEARN_RATE
            * (
                first / correct_one / (jnp.sqrt(second / correct_two) + ADAM_EPS)
                + DECAY_RATE * master
            )
        )
        fresh.append(jnp.stack([first, second])[None])
    summed = (
        lax.psum_scatter(
            updates[0].astype(jnp.bfloat16), "group", scatter_dimension=0, tiled=True
        ).astype(jnp.float32),
        lax.psum_scatter(
            updates[1].astype(jnp.bfloat16), "group", scatter_dimension=0, tiled=True
        ).astype(jnp.float32),
        lax.psum_scatter(
            updates[2].astype(jnp.bfloat16), "group", scatter_dimension=0, tiled=True
        ).astype(jnp.float32),
        lax.psum_scatter(
            updates[3].astype(jnp.bfloat16), "group", scatter_dimension=0, tiled=True
        ).astype(jnp.float32),
        lax.psum_scatter(
            updates[4].astype(jnp.bfloat16), "group", scatter_dimension=0, tiled=True
        ).astype(jnp.float32),
        lax.psum_scatter(
            updates[5].astype(jnp.bfloat16), "group", scatter_dimension=0, tiled=True
        ).astype(jnp.float32),
        lax.psum_scatter(
            updates[6].astype(jnp.bfloat16), "group", scatter_dimension=0, tiled=True
        ).astype(jnp.float32),
        lax.psum_scatter(
            updates[7].astype(jnp.bfloat16), "group", scatter_dimension=0, tiled=True
        ).astype(jnp.float32),
    )
    group_size = lax.axis_size("group")
    outer = []
    for state, total in zip(states, summed):
        delta = total / group_size
        momentum = OUTER_MOMENT * state[1] + delta
        weight = state[0] - OUTER_RATE * (delta + OUTER_MOMENT * momentum)
        outer.append(jnp.stack([weight, delta, momentum]))
    stacked = [jnp.stack(items, 0)[None] for items in collected]
    return (
        stacked[0],
        stacked[1],
        stacked[2],
        stacked[3],
        stacked[4],
        stacked[5],
        fresh[0],
        fresh[1],
        fresh[2],
        fresh[3],
        fresh[4],
        fresh[5],
        fresh[6],
        fresh[7],
        outer[0],
        outer[1],
        outer[2],
        outer[3],
        outer[4],
        outer[5],
        outer[6],
        outer[7],
    )


def solution(mesh):
    in_specs = (
        P("group", "dp", None, "mp"),
        P("group", "dp", None, "mp"),
        P("group", "dp", None, "mp"),
        P("group", "dp", None, "mp"),
        P("group", "dp", None, "mp"),
        P("group", "dp", None, "mp"),
        P("group"),
        P(None, ("dp", "group"), None, "mp"),
        P(None, ("mp", "dp", "group"), None),
        P(None, ("dp", "group"), "mp"),
        P(None, ("mp", "dp", "group"), None),
        P(None, ("dp", "group"), None, "mp"),
        P(None, ("mp", "dp", "group"), None),
        P(None, ("dp", "group"), "mp"),
        P(None, ("mp", "dp", "group"), None),
        P("group", None, "dp", None, "mp"),
        P("group", None, ("mp", "dp"), None),
        P("group", None, "dp", "mp"),
        P("group", None, ("mp", "dp"), None),
        P("group", None, "dp", None, "mp"),
        P("group", None, ("mp", "dp"), None),
        P("group", None, "dp", "mp"),
        P("group", None, ("mp", "dp"), None),
    )
    out_specs = (
        P("group", "dp", None, "mp"),
        P("group", "dp", None, "mp"),
        P("group", "dp", None, "mp"),
        P("group", "dp", None, "mp"),
        P("group", "dp", None, "mp"),
        P("group", "dp", None, "mp"),
        P("group", None, "dp", None, "mp"),
        P("group", None, ("mp", "dp"), None),
        P("group", None, "dp", "mp"),
        P("group", None, ("mp", "dp"), None),
        P("group", None, "dp", None, "mp"),
        P("group", None, ("mp", "dp"), None),
        P("group", None, "dp", "mp"),
        P("group", None, ("mp", "dp"), None),
        P(None, ("dp", "group"), None, "mp"),
        P(None, ("mp", "dp", "group"), None),
        P(None, ("dp", "group"), "mp"),
        P(None, ("mp", "dp", "group"), None),
        P(None, ("dp", "group"), None, "mp"),
        P(None, ("mp", "dp", "group"), None),
        P(None, ("dp", "group"), "mp"),
        P(None, ("mp", "dp", "group"), None),
    )
    return jax.shard_map(body, mesh=mesh, in_specs=in_specs, out_specs=out_specs, check_vma=False)
```

profile of v0, /device:TPU:0, one launch (start us, length us, event | category | flops | bytes accessed | tf_op | source)
XLA Modules:
  0.0 2464.5 jit_solution(7932400304551217499)
XLA Ops:
  14.4 20.8 all-reduce.3
  89.3 41.1 %all-gather.55.cloned.1.call-done = bf16[1178,1536]{1,0:T(8,128)(2,1)} async-done(((bf16[1178,384]{1,0:T(8,128)(2,1)}), bf16[1178,1536]{1,0:T(8,128)(2,1)}) %all-gather.55.cloned.1.call-update) | async-done | bytes 3618832 | tf_op jit(solution)/shard_map/all_gather | solution.py:27
  130.3 49.5 %all-gather.31.cloned.1.call-done = bf16[1536,3,384]{2,0,1:T(8,128)(2,1)} async-done(((bf16[768,3,384]{2,0,1:T(8,128)(2,1)}), bf16[1536,3,384]{2,0,1:T(8,128)(2,1)}) %all-gather.31.cloned.1.call-update) | async-done | bytes 3538960 | tf_op jit(solution)/shard_map/all_gather | solution.py:428
  183.4 47.8 %all-gather.27.cloned.1.call-done = bf16[1536,3,384]{0,2,1:T(8,128)(2,1)} async-done(((bf16[768,3,384]{0,2,1:T(8,128)(2,1)}), bf16[1536,3,384]{0,2,1:T(8,128)(2,1)}) %all-gather.27.cloned.1.call-update) | async-done | bytes 3538960 | tf_op jit(solution)/shard_map/all_gather | solution.py:424
  252.1 34.0 %while.45 = (s32[]{:T(128)}, bf16[6,1178,64]{1,2,0:T(8,128)(2,1)}, f32[6,1178]{1,0:T(8,128)S(1)}, bf16[6,1178,64]{2,1,0:T(8,128)(2,1)}, bf16[6,1178,64]{2,1,0:T(...) while((s32[]{:T(128)}, bf16[6,1178,64]{1,2,0:T(8,128)(2,1)}, ...), condition=%wide.region_21.22_spmd, body=%wide.region_18.21_spmd.sunk | while | flops 363647424 | bytes 17779336 | solution.py:144
  302.9 50.6 %all-gather.23.cloned.1.call-done = bf16[1178,1536]{1,0:T(8,128)(2,1)} async-done(((bf16[1178,384]{1,0:T(8,128)(2,1)}), bf16[1178,1536]{1,0:T(8,128)(2,1)}) %all-gather.23.cloned.1.call-update) | async-done | bytes 3618832 | tf_op jit(solution)/shard_map/all_gather | solution.py:27
  378.3 34.0 %while.44 = (s32[]{:T(128)}, bf16[6,1178,64]{1,2,0:T(8,128)(2,1)}, f32[6,1178]{1,0:T(8,128)S(1)}, bf16[6,1178,64]{2,1,0:T(8,128)(2,1)}, bf16[6,1178,64]{2,1,0:T(...) while((s32[]{:T(128)}, bf16[6,1178,64]{1,2,0:T(8,128)(2,1)}, ...), condition=%wide.region_7.8_spmd, body=%wide.region_4.7_spmd.sunk | while | flops 363647424 | bytes 17779336 | solution.py:144
  436.6 69.6 %reduce-scatter.77.cloned.1.call-done = bf16[384,1178]{1,0:T(8,128)(2,1)} async-done(((bf16[1536,1178]{1,0:T(8,128)(2,1)}), bf16[384,1178]{1,0:T(8,128)(2,1)}) %reduce-scatter.77.cloned.1.call-update) | async-done | bytes 904720
  508.4 73.7 %reduce-scatter.73.cloned.1.call-done = bf16[384,1178]{1,0:T(8,128)(2,1)} async-done(((bf16[1536,1178]{1,0:T(8,128)(2,1)}), bf16[384,1178]{1,0:T(8,128)(2,1)}) %reduce-scatter.73.cloned.1.call-update) | async-done | bytes 904720
  588.3 18.9 all-reduce.2
  618.2 64.0 %all-gather.63.cloned.1.call-done = bf16[1178,1536]{1,0:T(8,128)(2,1)} async-done(((bf16[1178,384]{1,0:T(8,128)(2,1)}), bf16[1178,1536]{1,0:T(8,128)(2,1)}) %all-gather.63.cloned.1.call-update) | async-done | bytes 3618832 | tf_op jit(solution)/shard_map/all_gather | solution.py:31
  682.1 62.7 %all-gather.53.cloned.1.call-done = bf16[1536,1536]{1,0:T(8,128)(2,1)} async-done(((bf16[768,1536]{1,0:T(8,128)(2,1)}), bf16[1536,1536]{1,0:T(8,128)(2,1)}) %all-gather.53.cloned.1.call-update) | async-done | bytes 4718608 | tf_op jit(solution)/shard_map/all_gather | solution.py:431
  750.0 58.9 %all-gather.49.cloned.1.call-done = bf16[1536,1536]{1,0:T(8,128)(2,1)} async-done(((bf16[768,1536]{1,0:T(8,128)(2,1)}), bf16[1536,1536]{1,0:T(8,128)(2,1)}) %all-gather.49.cloned.1.call-update) | async-done | bytes 4718608 | tf_op jit(solution)/shard_map/all_gather | solution.py:427
  824.2 48.8 %all-gather.41.cloned.1.call-done = bf16[1536,1536]{1,0:T(8,128)(2,1)} async-done(((bf16[768,1536]{1,0:T(8,128)(2,1)}), bf16[1536,1536]{1,0:T(8,128)(2,1)}) %all-gather.41.cloned.1.call-update) | async-done | bytes 4718608 | tf_op jit(solution)/shard_map/all_gather | solution.py:426
  873.0 73.7 %all-gather.57.cloned.1.call-done = bf16[1178,1536]{1,0:T(8,128)(2,1)} async-done(((bf16[1178,384]{1,0:T(8,128)(2,1)}), bf16[1178,1536]{1,0:T(8,128)(2,1)}) %all-gather.57.cloned.1.call-update) | async-done | bytes 3618832 | tf_op jit(solution)/shard_map/all_gather | solution.py:27
  956.7 52.8 %all-gather.45.cloned.1.call-done = bf16[1536,1536]{1,0:T(8,128)(2,1)} async-done(((bf16[768,1536]{1,0:T(8,128)(2,1)}), bf16[1536,1536]{1,0:T(8,128)(2,1)}) %all-gather.45.cloned.1.call-update) | async-done | bytes 4718608 | tf_op jit(solution)/shard_map/all_gather | solution.py:430
  1058.5 24.8 %all-gather.59.cloned.1.call-done = bf16[1178,1536]{1,0:T(8,128)(2,1)} async-done(((bf16[1178,384]{1,0:T(8,128)(2,1)}), bf16[1178,1536]{1,0:T(8,128)(2,1)}) %all-gather.59.cloned.1.call-update) | async-done | bytes 3618832 | tf_op jit(solution)/shard_map/all_gather | solution.py:31
  1098.5 57.2 %all-gather.37.cloned.1.call-done = bf16[1178,1536]{1,0:T(8,128)(2,1)} async-done(((bf16[1178,384]{1,0:T(8,128)(2,1)}), bf16[1178,1536]{1,0:T(8,128)(2,1)}) %all-gather.37.cloned.1.call-update) | async-done | bytes 3618832 | tf_op jit(solution)/shard_map/all_gather | solution.py:27
  1232.1 73.6 %reduce-scatter.79.cloned.1.call-done = bf16[384,1178]{1,0:T(8,128)(2,1)} async-done(((bf16[1536,1178]{1,0:T(8,128)(2,1)}), bf16[384,1178]{1,0:T(8,128)(2,1)}) %reduce-scatter.79.cloned.1.call-update) | async-done | bytes 904720
  1307.9 73.7 %reduce-scatter.81.cloned.1.call-done = bf16[384,1178]{1,0:T(8,128)(2,1)} async-done(((bf16[1536,1178]{1,0:T(8,128)(2,1)}), bf16[384,1178]{1,0:T(8,128)(2,1)}) %reduce-scatter.81.cloned.1.call-update) | async-done | bytes 904720
  1383.9 73.5 %reduce-scatter.75.cloned.1.call-done = bf16[384,1178]{1,0:T(8,128)(2,1)} async-done(((bf16[1536,1178]{1,0:T(8,128)(2,1)}), bf16[384,1178]{1,0:T(8,128)(2,1)}) %reduce-scatter.75.cloned.1.call-update) | async-done | bytes 904720
  1470.1 19.3 all-reduce.1
  1573.5 67.7 %all-gather.65.cloned.1.call-done = bf16[1178,1536]{1,0:T(8,128)(2,1)} async-done(((bf16[1178,384]{1,0:T(8,128)(2,1)}), bf16[1178,1536]{1,0:T(8,128)(2,1)}) %all-gather.65.cloned.1.call-update) | async-done | bytes 3618832 | tf_op jit(solution)/shard_map/all_gather | solution.py:31
  1650.7 52.0 %reduce-scatter.49.cloned.1.call-done = bf16[768,1536]{1,0:T(8,128)(2,1)} async-done(((bf16[1536,1536]{1,0:T(8,128)(2,1)}), bf16[768,1536]{1,0:T(8,128)(2,1)}) %reduce-scatter.49.cloned.1.call-update) | async-done | bytes 2359312 | tf_op jit(solution)/shard_map/reduce_scatter | solution.py:463
  1711.7 54.0 %reduce-scatter.51.cloned.1.call-done = bf16[768,1536]{1,0:T(8,128)(2,1)} async-done(((bf16[1536,1536]{1,0:T(8,128)(2,1)}), bf16[768,1536]{1,0:T(8,128)(2,1)}) %reduce-scatter.51.cloned.1.call-update) | async-done | bytes 2359312 | tf_op jit(solution)/shard_map/reduce_scatter | solution.py:466
  1774.7 53.8 %reduce-scatter.57.cloned.1.call-done = bf16[768,1536]{1,0:T(8,128)(2,1)} async-done(((bf16[1536,1536]{1,0:T(8,128)(2,1)}), bf16[768,1536]{1,0:T(8,128)(2,1)}) %reduce-scatter.57.cloned.1.call-update) | async-done | bytes 2359312 | tf_op jit(solution)/shard_map/reduce_scatter | solution.py:475
  1837.5 54.1 %reduce-scatter.59.cloned.1.call-done = bf16[768,1536]{1,0:T(8,128)(2,1)} async-done(((bf16[1536,1536]{1,0:T(8,128)(2,1)}), bf16[768,1536]{1,0:T(8,128)(2,1)}) %reduce-scatter.59.cloned.1.call-update) | async-done | bytes 2359312 | tf_op jit(solution)/shard_map/reduce_scatter | solution.py:478
  1910.5 70.9 %while.47 = (s32[]{:T(128)}, bf16[6,3,1178,64]{2,3,1,0:T(8,128)(2,1)}, bf16[6,1178,64]{2,1,0:T(8,128)(2,1)}, bf16[6,1178,64]{2,1,0:T(8,128)(2,1)}, f32[6,1178]{1...) while((s32[]{:T(128)}, ...), condition=%wide.region_48.49_spmd, body=%wide.region_46.48_spmd.sunk | while | flops 900952064 | bytes 45685536 | solution.py:283
  1992.1 70.9 %while.46 = (s32[]{:T(128)}, bf16[6,3,1178,64]{2,3,1,0:T(8,128)(2,1)}, bf16[6,1178,64]{2,1,0:T(8,128)(2,1)}, bf16[6,1178,64]{2,1,0:T(8,128)(2,1)}, f32[6,1178]{1...) while((s32[]{:T(128)}, ...), condition=%wide.region_35.36_spmd, body=%wide.region_33.35_spmd.sunk | while | flops 900952064 | bytes 45685536 | solution.py:283
  2207.1 28.5 %reduce-scatter.53.cloned.1.call-done = bf16[768,3,384]{2,0,1:T(8,128)(2,1)} async-done(((bf16[1536,3,384]{2,0,1:T(8,128)(2,1)}), bf16[768,3,384]{2,0,1:T(8,128)(2,1)}) %reduce-scatter.53.cloned.1.call-update) | async-done | bytes 1769488 | tf_op jit(solution)/shard_map/reduce_scatter | solution.py:469
  2251.4 59.1 %reduce-scatter.87.cloned.1.call-done = bf16[384,1178]{1,0:T(8,128)(2,1)} async-done(((bf16[1536,1178]{1,0:T(8,128)(2,1)}), bf16[384,1178]{1,0:T(8,128)(2,1)}) %reduce-scatter.87.cloned.1.call-update) | async-done | bytes 904720
  2315.1 70.7 %reduce-scatter.83.cloned.1.call-done = bf16[384,1178]{1,0:T(8,128)(2,1)} async-done(((bf16[1536,1178]{1,0:T(8,128)(2,1)}), bf16[384,1178]{1,0:T(8,128)(2,1)}) %reduce-scatter.83.cloned.1.call-update) | async-done | bytes 904720
  (956 shorter events, 950.5 us)
Async XLA Ops:
  60.4 226.9 %all-gather.35.cloned.1.call-start = ((), (), s32[]{:S(2)}) async-start(), calls=%async_computation.30 | async-start | bytes 1769472 | tf_op jit(solution)/shard_map/all_gather | solution.py:429
  78.6 274.8 %all-gather.23.cloned.1.call-start = ((), (), s32[]{:S(2)}) async-start(), calls=%async_computation.24 | async-start | bytes 4546560 | tf_op jit(solution)/shard_map/all_gather | solution.py:27
  82.5 352.3 %all-gather.51.cloned.1.call-start = ((), (), s32[]{:S(2)}) async-start(), calls=%async_computation.38 | async-start | bytes 2949120 | tf_op jit(solution)/shard_map/all_gather | solution.py:418
  84.7 350.7 %all-gather.47.cloned.1.call-start = ((), (), s32[]{:S(2)}) async-start(), calls=%async_computation.36 | async-start | bytes 2949120 | tf_op jit(solution)/shard_map/all_gather | solution.py:406
  87.0 349.0 %all-gather.39.cloned.1.call-start = ((), (), s32[]{:S(2)}) async-start(), calls=%async_computation.32 | async-start | bytes 2949120 | tf_op jit(solution)/shard_map/all_gather | solution.py:403
  89.2 416.9 %reduce-scatter.77.cloned.1.call-start = ((), (), s32[]{:S(2)}) async-start(), calls=%async_computation.62 | async-start | bytes 4915200
  429.4 252.8 %all-gather.63.cloned.1.call-start = ((), (), s32[]{:S(2)}) async-start(), calls=%async_computation.44 | async-start | bytes 4546560 | tf_op jit(solution)/shard_map/all_gather | solution.py:31
  434.8 310.1 %all-gather.53.cloned.1.call-start = ((), (), s32[]{:S(2)}) async-start(), calls=%async_computation.39 | async-start | bytes 7077888 | tf_op jit(solution)/shard_map/all_gather | solution.py:431
  435.3 373.6 %all-gather.49.cloned.1.call-start = ((), (), s32[]{:S(2)}) async-start(), calls=%async_computation.37 | async-start | bytes 7077888 | tf_op jit(solution)/shard_map/all_gather | solution.py:427
  435.9 437.1 %all-gather.41.cloned.1.call-start = ((), (), s32[]{:S(2)}) async-start(), calls=%async_computation.33 | async-start | bytes 7077888 | tf_op jit(solution)/shard_map/all_gather | solution.py:426
  436.5 510.2 %all-gather.57.cloned.1.call-start = ((), (), s32[]{:S(2)}) async-start(), calls=%async_computation.41 | async-start | bytes 4546560 | tf_op jit(solution)/shard_map/all_gather | solution.py:27
  612.8 396.7 %all-gather.45.cloned.1.call-start = ((), (), s32[]{:S(2)}) async-start(), calls=%async_computation.35 | async-start | bytes 7077888 | tf_op jit(solution)/shard_map/all_gather | solution.py:430
  613.4 469.9 %all-gather.59.cloned.1.call-start = ((), (), s32[]{:S(2)}) async-start(), calls=%async_computation.42 | async-start | bytes 4546560 | tf_op jit(solution)/shard_map/all_gather | solution.py:31
  618.1 537.5 %all-gather.37.cloned.1.call-start = ((), (), s32[]{:S(2)}) async-start(), calls=%async_computation.31 | async-start | bytes 4546560 | tf_op jit(solution)/shard_map/all_gather | solution.py:27
  824.1 405.8 %reduce-scatter.85.cloned.1.call-start = ((), (), s32[]{:S(2)}) async-start(), calls=%async_computation.66 | async-start | bytes 4915200
  1039.2 266.6 %reduce-scatter.79.cloned.1.call-start = ((), (), s32[]{:S(2)}) async-start(), calls=%async_computation.63 | async-start | bytes 4915200
  1058.5 323.2 %reduce-scatter.81.cloned.1.call-start = ((), (), s32[]{:S(2)}) async-start(), calls=%async_computation.64 | async-start | bytes 4915200
  1191.4 266.0 %reduce-scatter.75.cloned.1.call-start = ((), (), s32[]{:S(2)}) async-start(), calls=%async_computation.61 | async-start | bytes 4915200
  1211.2 357.7 %all-gather.61.cloned.1.call-start = ((), (), s32[]{:S(2)}) async-start(), calls=%async_computation.43 | async-start | bytes 4546560 | tf_op jit(solution)/shard_map/all_gather | solution.py:31
  1521.9 243.7 %reduce-scatter.51.cloned.1.call-start = ((), (), s32[]{:S(2)}) async-start(), calls=%async_computation.49 | async-start | bytes 7077888 | tf_op jit(solution)/shard_map/reduce_scatter | solution.py:466
  1537.4 291.1 %reduce-scatter.57.cloned.1.call-start = ((), (), s32[]{:S(2)}) async-start(), calls=%async_computation.52 | async-start | bytes 7077888 | tf_op jit(solution)/shard_map/reduce_scatter | solution.py:475
  1544.9 346.6 %reduce-scatter.59.cloned.1.call-start = ((), (), s32[]{:S(2)}) async-start(), calls=%async_computation.53 | async-start | bytes 7077888 | tf_op jit(solution)/shard_map/reduce_scatter | solution.py:478
  1552.9 527.1 %reduce-scatter.47.cloned.1.call-start = ((), (), s32[]{:S(2)}) async-start(), calls=%async_computation.47 | async-start | bytes 1769472 | tf_op jit(solution)/shard_map/reduce_scatter | solution.py:460
  1646.3 438.5 %reduce-scatter.55.cloned.1.call-start = ((), (), s32[]{:S(2)}) async-start(), calls=%async_computation.51 | async-start | bytes 1769472 | tf_op jit(solution)/shard_map/reduce_scatter | solution.py:472
  1650.7 520.7 %reduce-scatter.63.cloned.1.call-start = ((), (), s32[]{:S(2)}) async-start(), calls=%async_computation.55 | async-start | bytes 2949120 | tf_op jit(solution)/shard_map/reduce_scatter | solution.py:506
  1711.6 463.4 %reduce-scatter.65.cloned.1.call-start = ((), (), s32[]{:S(2)}) async-start(), calls=%async_computation.56 | async-start | bytes 2949120 | tf_op jit(solution)/shard_map/reduce_scatter | solution.py:509
  1774.5 404.8 %reduce-scatter.69.cloned.1.call-start = ((), (), s32[]{:S(2)}) async-start(), calls=%async_computation.58 | async-start | bytes 2949120 | tf_op jit(solution)/shard_map/reduce_scatter | solution.py:518
  1837.4 346.3 %reduce-scatter.71.cloned.1.call-start = ((), (), s32[]{:S(2)}) async-start(), calls=%async_computation.59 | async-start | bytes 2949120 | tf_op jit(solution)/shard_map/reduce_scatter | solution.py:521
  1900.5 289.9 %reduce-scatter.45.cloned.1.call-start = ((), (), s32[]{:S(2)}) async-start(), calls=%async_computation.46 | async-start | bytes 5308416 | tf_op jit(solution)/shard_map/reduce_scatter | solution.py:457
  2115.0 270.8 %reduce-scatter.83.cloned.1.call-start = ((), (), s32[]{:S(2)}) async-start(), calls=%async_computation.65 | async-start | bytes 4915200
  2145.4 283.4 %reduce-scatter.89.cloned.1.call-start = ((), (), s32[]{:S(2)}) async-start(), calls=%async_computation.68 | async-start | bytes 2211840
  2199.2 250.8 %reduce-scatter.91.cloned.1.call-start = ((), (), s32[]{:S(2)}) async-start(), calls=%async_computation.69 | async-start | bytes 2211840
  (198 other events, 8801.9 us)
Sparse Core Ops, SparseCore 0:
  58.8 71.5 all-gather.54
  131.7 48.0 all-gather.30
  181.8 49.3 all-gather.26
  281.9 71.5 all-gather.22
  433.4 72.6 reduce-scatter.76
  509.0 73.0 reduce-scatter.72
  610.6 71.5 all-gather.62
  683.5 61.2 all-gather.52
  746.3 62.6 all-gather.48
  810.3 62.6 all-gather.40
  875.2 71.5 all-gather.56
  948.2 61.3 all-gather.44
  1011.7 71.5 all-gather.58
  1085.4 70.1 all-gather.36
  1158.5 71.3 reduce-scatter.84
  1232.6 73.0 reduce-scatter.78
  1308.6 73.0 reduce-scatter.80
  1384.4 72.9 reduce-scatter.74
  1498.8 69.9 all-gather.60
  1571.0 70.1 all-gather.64
  1644.1 58.6 reduce-scatter.48
  1705.6 59.9 reduce-scatter.50
  1768.5 59.9 reduce-scatter.56
  1831.5 59.9 reduce-scatter.58
  1943.9 33.0 reduce-scatter.62
  1980.1 33.0 reduce-scatter.64
  2016.1 33.0 reduce-scatter.68
  2052.5 33.0 reduce-scatter.70
  2087.7 47.6 reduce-scatter.44
  2187.9 47.6 reduce-scatter.52
  2237.8 72.6 reduce-scatter.86
  2312.8 72.9 reduce-scatter.82
  (14 shorter events, 331.1 us)
where the time goes:
time: 2480 us; the launch traced here: 2460 us
  waiting for transfers between devices  1510 us (61%)
  matrix products  394 us (16%)
  other arithmetic  259 us (10%)
  local copies, waits for them, and re-layouts  188 us (8%)
  blocking collectives  93.2 us (4%)
    unnamed x56, waiting for transfers between devices  534 us
    all_gather x4, waiting for transfers between devices, spread_rows(): return lax.all_gather(rows, 'mp', axis=1, tiled=True)  223 us
    all_gather x4, waiting for transfers between devices, spread_grad(): return lax.all_gather(rows, 'mp', axis=1, tiled=True)  172 us
    unnamed x392, local copies, waits for them, and re-layouts  105 us
    psum x4, blocking collectives, feature_sums(): return lax.psum((first, second), 'mp')  77.1 us
    all_gather x1, waiting for transfers between devices, body(): lax.all_gather(masters[7], 'dp', axis=0, tiled=True)  62.7 us
    all_gather x1, waiting for transfers between devices, body(): lax.all_gather(masters[3], 'dp', axis=0, tiled=True)  58.9 us
    reduce_scatter x1, waiting for transfers between devices, body(): lax.psum_scatter(totals[7].astype(jnp.bfloat16), 'dp', scatter_dimension=...  54.1 us
  transfers between devices with their start and end apart: 46, of which 29 were waited for; matrix products, arithmetic and copies ran while one was open for 32% of the time, Pallas kernels for 0%

commit v1 on v0

v1 whole, which is shorter than its diff:
```python
import jax
import jax.numpy as jnp
from jax import lax
from jax.experimental import pallas as pl
from jax.experimental.pallas import tpu as pltpu
from jax.sharding import PartitionSpec as P

BF = jnp.bfloat16
F32 = jnp.float32
EPS_NORM = 1e-06
STEP = 3
BETA_ONE = 0.9
BETA_TWO = 0.95
ADAM_EPS = 1e-08
LEARN_RATE = 0.02
DECAY_RATE = 0.1
OUTER_RATE = 0.7
OUTER_MOMENT = 0.9
BLOCK = 256
VMEM_BYTES = 60 * 1024 * 1024
NT = (((1,), (1,)), ((), ()))
NN = (((1,), (0,)), ((), ()))
TN = (((0,), (0,)), ((), ()))


def mm(a, b, dims=NN):
    return lax.dot_general(a, b, dims, preferred_element_type=F32)


def call(kernel, grid, in_specs, out_specs, out_shape, flops, nbytes, scratch=(), prefetch=1):
    return pl.pallas_call(
        kernel,
        grid_spec=pltpu.PrefetchScalarGridSpec(
            num_scalar_prefetch=prefetch,
            grid=grid,
            in_specs=in_specs,
            out_specs=out_specs,
            scratch_shapes=list(scratch),
        ),
        out_shape=out_shape,
        compiler_params=pltpu.CompilerParams(
            vmem_limit_bytes=VMEM_BYTES, dimension_semantics=("arbitrary",) * len(grid)
        ),
        cost_estimate=pl.CostEstimate(flops=int(flops), bytes_accessed=int(nbytes), transcendentals=0),
    )


def rows_spec(width):
    return pl.BlockSpec((BLOCK, width), lambda i, *_: (i, 0))


def whole(shape):
    return pl.BlockSpec(shape, lambda *_: (0,) * len(shape), pipeline_mode=pl.Buffered(1))


def struct(shape, dtype):
    return jax.ShapeDtypeStruct(shape, dtype)


def ln_qkv(ids, xm, xo, mod, wi, wt, image_len, image_row, text_row):
    rows, half = xm.shape
    width, local = 2 * half, half // 2
    cols = 3 * local
    image_blocks = image_len // BLOCK

    def kernel(ids_ref, xm_ref, xo_ref, mod_ref, wi_ref, wt_ref, h_ref, qkv_ref, n_ref, inv_ref):
        i = pl.program_id(0)
        base = jnp.where(i < image_blocks, image_row, text_row)
        shift = mod_ref[pl.ds(base, 1), :]
        scale = 1.0 + mod_ref[pl.ds(base + 1, 1), :]
        first = ids_ref[1] == 0
        here = pl.ds(pl.multiple_of(ids_ref[0] * half, 128), half)
        there = pl.ds(pl.multiple_of((1 - ids_ref[0]) * half, 128), half)

        def chunk(r, carry):
            at = pl.ds(pl.multiple_of(r * 32, 32), 32)
            a = xm_ref[at, :].astype(F32)
            b = xo_ref[at, :].astype(F32)
            mean = (jnp.sum(a, 1, keepdims=True) + jnp.sum(b, 1, keepdims=True)) / width
            a, b = a - mean, b - mean
            var = (jnp.sum(a * a, 1, keepdims=True) + jnp.sum(b * b, 1, keepdims=True)) / width
            inv = lax.rsqrt(var + EPS_NORM)
            a, b = a * inv, b * inv
            n_ref[at, :] = jnp.where(first, a[:, :local], a[:, local:])
            inv_ref[at, :] = jnp.broadcast_to(inv, (32, 128))
            h_ref[at, here] = (a * scale[:, :half] + shift[:, :half]).astype(BF)
            h_ref[at, there] = (b * scale[:, half:] + shift[:, half:]).astype(BF)
            return carry

        lax.fori_loop(0, BLOCK // 32, chunk, 0, unroll=BLOCK // 32)

        def project(w_ref):
            for j in range(3):
                qkv_ref[j] = mm(h_ref[...], w_ref[j]).astype(BF)

        @pl.when(i < image_blocks)
        def _():
            project(wi_ref)

        @pl.when(i >= image_blocks)
        def _():
            project(wt_ref)

    return call(
        kernel,
        (pl.cdiv(rows, BLOCK),),
        [rows_spec(half), rows_spec(half), whole(mod.shape), whole(wi.shape), whole(wt.shape)],
        [
            rows_spec(width),
            pl.BlockSpec((3, BLOCK, local), lambda i, *_: (0, i, 0)),
            rows_spec(local),
            rows_spec(128),
        ],
        [
            struct((rows, width), BF),
            struct((3, rows, local), BF),
            struct((rows, local), F32),
            struct((rows, 128), F32),
        ],
        2 * rows * width * cols,
        rows * width * 6 + 4 * width * cols,
    )(ids, xm, xo, mod, wi, wt)


def pair_mask(array, head, dim):
    lane = lax.broadcasted_iota(jnp.int32, array.shape, 1)
    return jnp.where(lane // dim == head, array, jnp.zeros_like(array))


def q_chunks(rows, image_len):
    return [(s, BLOCK) for s in range(0, image_len, BLOCK)] + [(image_len, rows - image_len)]


def attend(qkv, length, image_len, dim=64):
    _, rows, local = qkv.shape
    pairs = local // 128
    lanes = pl.cdiv(rows, BLOCK) * BLOCK
    tail = length // 8 * 8
    scale = dim**-0.5

    def kernel(qkv_ref, out_ref, lse_ref, s_ref):
        for start, size in q_chunks(rows, image_len):
            total = None
            for head in range(128 // dim):
                q = pair_mask(qkv_ref[0, start : start + size, :], head, dim) * jnp.asarray(scale, BF)
                s_ref[:, :size] = mm(qkv_ref[1], q, NT)
                if tail < rows:
                    last = s_ref[tail:, :size]
                    row = lax.broadcasted_iota(jnp.int32, last.shape, 0) + tail
                    s_ref[tail:, :size] = jnp.where(row < length, last, -1e30)
                s = s_ref[:, :size]
                top = jnp.max(s, 0, keepdims=True)
                e = jnp.exp(s - top)
                norm = jnp.sum(e, 0, keepdims=True)
                lse_ref[0, head : head + 1, start : start + size] = top + jnp.log(norm)
                p = (e * (1.0 / norm)).astype(BF)
                mix = mm(p, pair_mask(qkv_ref[2], head, dim), TN)
                total = mix if total is None else total + mix
            out_ref[start : start + size, :] = total.astype(BF)

    return pl.pallas_call(
        kernel,
        grid=(pairs,),
        in_specs=[pl.BlockSpec((3, rows, 128), lambda j: (0, 0, j))],
        out_specs=[
            pl.BlockSpec((rows, 128), lambda j: (0, j)),
            pl.BlockSpec((1, 8, lanes), lambda j: (j, 0, 0)),
        ],
        out_shape=[struct((rows, local), BF), struct((pairs, 8, lanes), F32)],
        scratch_shapes=[pltpu.VMEM((rows, BLOCK), F32)],
        compiler_params=pltpu.CompilerParams(vmem_limit_bytes=VMEM_BYTES),
        cost_estimate=pl.CostEstimate(
            flops=16 * rows * rows * local, bytes_accessed=rows * local * 8, transcendentals=0
        ),
    )(qkv)


def attend_back(qkv, grad, lse, length, image_len, dim=64):
    _, rows, local = qkv.shape
    pairs = local // 128
    lanes = lse.shape[2]
    tail = length // 8 * 8
    scale = dim**-0.5

    def kernel(qkv_ref, grad_ref, lse_ref, out_ref, s_ref, gk_ref, gv_ref):
        gk_ref[...] = jnp.zeros_like(gk_ref)
        gv_ref[...] = jnp.zeros_like(gv_ref)
        for start, size in q_chunks(rows, image_len):
            total = None
            for head in range(128 // dim):
                q = pair_mask(qkv_ref[0, start : start + size, :], head, dim) * jnp.asarray(scale, BF)
                gm = pair_mask(grad_ref[start : start + size, :], head, dim)
                s_ref[:, :size] = mm(qkv_ref[1], q, NT)
                if tail < rows:
                    last = s_ref[tail:, :size]
                    row = lax.broadcasted_iota(jnp.int32, last.shape, 0) + tail
                    s_ref[tail:, :size] = jnp.where(row < length, last, -1e30)
                p = jnp.exp(s_ref[:, :size] - lse_ref[0, head : head + 1, start : start + size])
                gv_ref[...] += mm(p.astype(BF), gm)
                gp = mm(qkv_ref[2], gm, NT)
                delta = jnp.sum(p * gp, 0, keepdims=True)
                gs = (p * (gp - delta)).astype(BF)
                gk_ref[...] += mm(gs, q)
                gq = mm(gs, pair_mask(qkv_ref[1], head, dim), TN)
                total = gq if total is None else total + gq
            out_ref[0, start : start + size, :] = (total * scale).astype(BF)
        out_ref[1] = gk_ref[...].astype(BF)
        out_ref[2] = gv_ref[...].astype(BF)

    return pl.pallas_call(
        kernel,
        grid=(pairs,),
        in_specs=[
            pl.BlockSpec((3, rows, 128), lambda j: (0, 0, j)),
            pl.BlockSpec((rows, 128), lambda j: (0, j)),
            pl.BlockSpec((1, 8, lanes), lambda j: (j, 0, 0)),
        ],
        out_specs=pl.BlockSpec((3, rows, 128), lambda j: (0, 0, j)),
        out_shape=struct((3, rows, local), BF),
        scratch_shapes=[
            pltpu.VMEM((rows, BLOCK), F32),
            pltpu.VMEM((rows, 128), F32),
            pltpu.VMEM((rows, 128), F32),
        ],
        compiler_params=pltpu.CompilerParams(vmem_limit_bytes=VMEM_BYTES),
        cost_estimate=pl.CostEstimate(
            flops=40 * rows * rows * local, bytes_accessed=rows * local * 14, transcendentals=0
        ),
    )(qkv, grad, lse)


def out_project(ids, mixed, wi, wt, image_len):
    rows, local = mixed.shape
    width = wi.shape[1]
    half = width // 2
    image_blocks = image_len // BLOCK

    def kernel(ids_ref, a_ref, wi_ref, wt_ref, keep_ref, send_ref):
        i = pl.program_id(0)
        here = pl.ds(pl.multiple_of(ids_ref[0] * half, 128), half)
        there = pl.ds(pl.multiple_of((1 - ids_ref[0]) * half, 128), half)

        def project(w_ref):
            keep_ref[...] = mm(a_ref[...], w_ref[:, here]).astype(BF)
            send_ref[...] = mm(a_ref[...], w_ref[:, there]).astype(BF)

        @pl.when(i < image_blocks)
        def _():
            project(wi_ref)

        @pl.when(i >= image_blocks)
        def _():
            project(wt_ref)

    return call(
        kernel,
        (pl.cdiv(rows, BLOCK),),
        [rows_spec(local), whole(wi.shape), whole(wt.shape)],
        [rows_spec(half), rows_spec(half)],
        [struct((rows, half), BF), struct((rows, half), BF)],
        2 * rows * width * local,
        rows * width * 3 + 4 * width * local,
    )(ids, mixed, wi, wt)


def input_partial(ids, gqkv, wi, wt, image_len):
    _, rows, local = gqkv.shape
    width = wi.shape[1]
    half = width // 2
    image_blocks = image_len // BLOCK

    def kernel(ids_ref, a_ref, wi_ref, wt_ref, keep_ref, send_ref):
        i = pl.program_id(0)
        here = pl.ds(pl.multiple_of(ids_ref[0] * half, 128), half)
        there = pl.ds(pl.multiple_of((1 - ids_ref[0]) * half, 128), half)

        def project(w_ref):
            for out_ref, lo in ((keep_ref, here), (send_ref, there)):
                total = None
                for j in range(3):
                    part = mm(a_ref[j], w_ref[j, lo, :], NT)
                    total = part if total is None else total + part
                out_ref[...] = total.astype(BF)

        @pl.when(i < image_blocks)
        def _():
            project(wi_ref)

        @pl.when(i >= image_blocks)
        def _():
            project(wt_ref)

    return call(
        kernel,
        (pl.cdiv(rows, BLOCK),),
        [pl.BlockSpec((3, BLOCK, local), lambda i, *_: (0, i, 0)), whole(wi.shape), whole(wt.shape)],
        [rows_spec(half), rows_spec(half)],
        [struct((rows, half), BF), struct((rows, half), BF)],
        2 * rows * width * local * 3,
        rows * width * 5 + 12 * width * local,
    )(ids, gqkv, wi, wt)


def after_norm(xa, xb, aa, ab, gate, half, width):
    a = xa.astype(F32) + gate[:, :half] * aa.astype(F32)
    b = xb.astype(F32) + gate[:, half:] * ab.astype(F32)
    mean = (jnp.sum(a, 1, keepdims=True) + jnp.sum(b, 1, keepdims=True)) / width
    ca, cb = a - mean, b - mean
    var = (jnp.sum(ca * ca, 1, keepdims=True) + jnp.sum(cb * cb, 1, keepdims=True)) / width
    inv = lax.rsqrt(var + EPS_NORM)
    return a, ca * inv, cb * inv, inv


def mid_prepare(ids, live, xm, xo, am, ao, cm, co, mod, image_len, image_row, text_row):
    rows, half = xm.shape
    width, local = 2 * half, half // 2
    image_blocks = image_len // BLOCK
    step = 32

    def kernel(ids_ref, live_ref, xm_ref, xo_ref, am_ref, ao_ref, cm_ref, co_ref, mod_ref, h_ref, g_ref, own_ref):
        i = pl.program_id(0)
        base = jnp.where(i < image_blocks, image_row, text_row)
        gate_a = mod_ref[pl.ds(base + 2, 1), :]
        shift = mod_ref[pl.ds(base + 3, 1), :]
        scale = 1.0 + mod_ref[pl.ds(base + 4, 1), :]
        gate_m = mod_ref[pl.ds(base + 5, 1), :] * live_ref[0]
        first = ids_ref[1] == 0
        here = pl.ds(pl.multiple_of(ids_ref[0] * half, 128), half)
        there = pl.ds(pl.multiple_of((1 - ids_ref[0]) * half, 128), half)

        def chunk(r, carry):
            at = pl.ds(pl.multiple_of(r * step, step), step)
            a, na, nb, _ = after_norm(xm_ref[at, :], xo_ref[at, :], am_ref[at, :], ao_ref[at, :], gate_a, half, width)
            own_ref[at, :] = jnp.where(first, a[:, :local], a[:, local:])
            h_ref[at, here] = (na * scale[:, :half] + shift[:, :half]).astype(BF)
            h_ref[at, there] = (nb * scale[:, half:] + shift[:, half:]).astype(BF)
            g_ref[at, here] = (cm_ref[at, :].astype(F32) * gate_m[:, :half]).astype(BF)
            g_ref[at, there] = (co_ref[at, :].astype(F32) * gate_m[:, half:]).astype(BF)
            return carry

        lax.fori_loop(0, BLOCK // step, chunk, 0, unroll=BLOCK // step)

    return call(
        kernel,
        (pl.cdiv(rows, BLOCK),),
        [rows_spec(half)] * 6 + [whole(mod.shape)],
        [rows_spec(width), rows_spec(width), rows_spec(local)],
        [struct((rows, width), BF), struct((rows, width), BF), struct((rows, local), F32)],
        rows * width * 20,
        rows * width * 11,
        prefetch=2,
    )(ids, live, xm, xo, am, ao, cm, co, mod)


def gelu_pair(v):
    k, c3 = 0.7978845608028654, 0.044715
    v2 = v * v
    t = jnp.tanh(k * v * (1.0 + c3 * v2))
    up = 0.5 * (1.0 + t)
    return v * up, up + 0.5 * v * (1.0 - t * t) * (k * (1.0 + 3.0 * c3 * v2))


def mlp(ids, h, g, w1i, w1t, w2i, w2t, image_len, tile=256):
    rows, width = h.shape
    half = width // 2
    hidden = w1i.shape[1]
    steps = hidden // tile
    piece = 512

    def kernel(
        ids_ref, h_ref, g_ref, w1i_ref, w1t_ref, w2i_ref, w2t_ref,
        act_ref, gin_ref, bk_ref, bs_ref, gk_ref, gs_ref, b_acc, g_acc,
    ):
        i = pl.program_id(0)
        here = pl.ds(pl.multiple_of(ids_ref[0] * half, 128), half)
        there = pl.ds(pl.multiple_of((1 - ids_ref[0]) * half, 128), half)

        def work(at, w1_ref, w2_ref):
            inner = mm(h_ref[at, :], w1_ref[...])
            ag = mm(g_ref[at, :], w2_ref[...], NT)
            act, slope = gelu_pair(inner)
            act = act.astype(BF)
            gin = (ag * slope).astype(BF)
            act_ref[at, :] = act
            gin_ref[at, :] = gin
            parts = ((b_acc, mm(act, w2_ref[...])), (g_acc, mm(gin, w1_ref[...], NT)))

            @pl.when(i == 0)
            def _():
                for ref, value in parts:
                    ref[at, :] = value

            @pl.when(i > 0)
            def _():
                for ref, value in parts:
                    ref[at, :] += value

        def image_piece(r, carry):
            work(pl.ds(pl.multiple_of(r * piece, piece), piece), w1i_ref, w2i_ref)
            return carry

        lax.fori_loop(0, image_len // piece, image_piece, 0)
        work(slice(image_len, rows), w1t_ref, w2t_ref)

        @pl.when(i == steps - 1)
        def _():
            bk_ref[...] = b_acc[:, here].astype(BF)
            bs_ref[...] = b_acc[:, there].astype(BF)
            gk_ref[...] = g_acc[:, here].astype(BF)
            gs_ref[...] = g_acc[:, there].astype(BF)

    w1_spec = pl.BlockSpec((width, tile), lambda i, *_: (0, i))
    w2_spec = pl.BlockSpec((tile, width), lambda i, *_: (i, 0))
    out_tile = pl.BlockSpec((rows, tile), lambda i, *_: (0, i))
    return call(
        kernel,
        (steps,),
        [whole((rows, width)), whole((rows, width)), w1_spec, w1_spec, w2_spec, w2_spec],
        [out_tile, out_tile] + [whole((rows, half))] * 4,
        [struct((rows, hidden), BF)] * 2 + [struct((rows, half), BF)] * 4,
        8 * rows * width * hidden,
        rows * width * 12 + 8 * width * hidden,
        scratch=[pltpu.VMEM((rows, width), F32), pltpu.VMEM((rows, width), F32)],
    )(ids, h, g, w1i, w1t, w2i, w2t)


def back_prepare(ids, live, xm, xo, am, ao, cm, co, gm, go, mod, wi, wt, image_len, image_row, text_row):
    rows, half = xm.shape
    width, local = 2 * half, half // 2
    image_blocks = image_len // BLOCK
    step = 32

    def kernel(
        ids_ref, live_ref, xm_ref, xo_ref, am_ref, ao_ref, cm_ref, co_ref, gm_ref, go_ref, mod_ref, wi_ref, wt_ref,
        ga_ref, gmix_ref, own_ref, sums_ref,
    ):
        i = pl.program_id(0)
        base = jnp.where(i < image_blocks, image_row, text_row)
        gate_a = mod_ref[pl.ds(base + 2, 1), :]
        scale = 1.0 + mod_ref[pl.ds(base + 4, 1), :]
        first = ids_ref[1] == 0
        live_now = live_ref[0]
        here = pl.ds(pl.multiple_of(ids_ref[0] * half, 128), half)
        there = pl.ds(pl.multiple_of((1 - ids_ref[0]) * half, 128), half)

        @pl.when((i == 0) | (i == image_blocks))
        def _():
            sums_ref[...] = jnp.zeros_like(sums_ref)

        def own(v):
            return jnp.where(first, v[:, :local], v[:, local:])

        def chunk(r, carry):
            at = pl.ds(pl.multiple_of(r * step, step), step)
            _, na, nb, inv = after_norm(xm_ref[at, :], xo_ref[at, :], am_ref[at, :], ao_ref[at, :], gate_a, half, width)
            ga = gm_ref[at, :].astype(F32)
            gb = go_ref[at, :].astype(F32)
            qa, qb = ga * scale[:, :half], gb * scale[:, half:]
            mean = (jnp.sum(qa, 1, keepdims=True) + jnp.sum(qb, 1, keepdims=True)) / width
            cross = (jnp.sum(qa * na, 1, keepdims=True) + jnp.sum(qb * nb, 1, keepdims=True)) / width
            fa = cm_ref[at, :].astype(F32) * live_now + inv * (qa - mean - na * cross)
            fb = co_ref[at, :].astype(F32) * live_now + inv * (qb - mean - nb * cross)
            ga_ref[at, here] = (gate_a[:, :half] * fa).astype(BF)
            ga_ref[at, there] = (gate_a[:, half:] * fb).astype(BF)
            fo, go_own = own(fa), own(ga)
            own_ref[at, :] = fo
            row = i * BLOCK + r * step + lax.broadcasted_iota(jnp.int32, (step, local), 0)
            inside = row < rows
            for k, value in enumerate((go_own, go_own * own(na), fo * own(am_ref[at, :].astype(F32)))):
                value = jnp.where(inside, value, 0.0)
                sums_ref[0, k * 8 : (k + 1) * 8, :] += jnp.sum(value.reshape(step // 8, 8, local), 0)
            return carry

        lax.fori_loop(0, BLOCK // step, chunk, 0, unroll=BLOCK // step)

        def project(w_ref):
            gmix_ref[...] = mm(ga_ref[...], w_ref[...], NT).astype(BF)

        @pl.when(i < image_blocks)
        def _():
            project(wi_ref)

        @pl.when(i >= image_blocks)
        def _():
            project(wt_ref)

    return call(
        kernel,
        (pl.cdiv(rows, BLOCK),),
        [rows_spec(half)] * 8 + [whole(mod.shape), whole(wi.shape), whole(wt.shape)],
        [
            rows_spec(width),
            rows_spec(local),
            rows_spec(local),
            pl.BlockSpec((1, 24, local), lambda i, *_: (jnp.where(i < image_blocks, 0, 1), 0, 0)),
        ],
        [
            struct((rows, width), BF),
            struct((rows, local), BF),
            struct((rows, local), F32),
            struct((2, 24, local), F32),
        ],
        2 * rows * width * local,
        rows * width * 12,
        prefetch=2,
    )(ids, live, xm, xo, am, ao, cm, co, gm, go, mod, wi, wt)


def adam(ids, inv_count, moment, grad):
    _, lead, _, piece, cols = moment.shape
    correct_one = 1.0 - BETA_ONE**STEP
    correct_two = 1.0 - BETA_TWO**STEP

    def kernel(ids_ref, inv_ref, m_ref, g_ref, fresh_ref, keep_ref, send_ref):
        t = pl.program_id(1)
        g = g_ref[0, 0].astype(F32) * inv_ref[0]
        first = BETA_ONE * m_ref[0, 0, 0] + (1.0 - BETA_ONE) * g
        second = BETA_TWO * m_ref[1, 0, 0] + (1.0 - BETA_TWO) * g * g
        fresh_ref[0, 0, 0] = first
        fresh_ref[1, 0, 0] = second
        update = ((first / correct_one) / (jnp.sqrt(second / correct_two) + ADAM_EPS)).astype(BF)

        @pl.when(t < 2)
        def _():
            send_ref[0, 0] = update

        @pl.when(t >= 2)
        def _():
            keep_ref[0, 0] = update

    def block(t, ids_ref):
        return (t % 2) * 2 + jnp.where(t < 2, 1 - ids_ref[0], ids_ref[0])

    pairs = pl.BlockSpec((2, 1, 1, piece, cols), lambda l, t, ids_ref, _: (0, l, block(t, ids_ref), 0, 0))
    side = struct((2, lead, piece, cols), BF)
    return call(
        kernel,
        (lead, 4),
        [
            pairs,
            pl.BlockSpec((1, 1, piece, cols), lambda l, t, ids_ref, _: (l, block(t, ids_ref), 0, 0)),
        ],
        [
            pairs,
            pl.BlockSpec((1, 1, piece, cols), lambda l, t, *_: (jnp.maximum(t - 2, 0), l, 0, 0)),
            pl.BlockSpec((1, 1, piece, cols), lambda l, t, *_: (jnp.minimum(t, 1), l, 0, 0)),
        ],
        [struct(moment.shape, F32), side, side],
        lead * piece * cols * 80,
        lead * piece * cols * 80,
        prefetch=2,
    )(ids, inv_count, moment, grad)


def outer_step(ids, state, keep, got, far, groups):
    _, lead, piece, cols = state.shape

    def kernel(ids_ref, s_ref, k_ref, g_ref, f_ref, out_ref):
        near = (k_ref[0, 0].astype(F32) + g_ref[0, 0].astype(F32)).astype(BF).astype(F32)
        total = near + f_ref[0].astype(F32)
        master = s_ref[0, 0]
        delta = LEARN_RATE * (total * (1.0 / groups) + DECAY_RATE * master)
        momentum = OUTER_MOMENT * s_ref[1, 0] + delta
        out_ref[0, 0] = master - OUTER_RATE * (delta + OUTER_MOMENT * momentum)
        out_ref[1, 0] = delta
        out_ref[2, 0] = momentum

    side = pl.BlockSpec((1, 1, piece, cols), lambda l, ids_ref: (ids_ref[2], l, 0, 0))
    return call(
        kernel,
        (lead,),
        [
            pl.BlockSpec((2, 1, piece, cols), lambda l, *_: (0, l, 0, 0)),
            side,
            side,
            pl.BlockSpec((1, piece, cols), lambda l, *_: (l, 0, 0)),
        ],
        pl.BlockSpec((3, 1, piece, cols), lambda l, *_: (0, l, 0, 0)),
        struct((3, lead, piece, cols), F32),
        lead * piece * cols * 10,
        lead * piece * cols * 26,
    )(ids, state, keep, got, far)


def solution(mesh):
    n_group, n_dp, n_mp = mesh.shape["group"], mesh.shape["dp"], mesh.shape["mp"]
    core_perm = [(g, g ^ 1) for g in range(n_group)]
    x_perm = [(g, g ^ 2) for g in range(n_group)]
    z_perm = [(m, m ^ 1) for m in range(n_mp)]
    y_perm = [(d, d ^ 1) for d in range(n_dp)]
    turn_perm = [
        (g * n_mp + m, ((g // 2) * 2 + m // 2) * n_mp + (g % 2) * 2 + m % 2)
        for g in range(n_group)
        for m in range(n_mp)
    ]

    def core_swap(a):
        return lax.ppermute(a, "group", core_perm)

    def x_swap(a):
        return lax.ppermute(a, "group", x_perm)

    def z_swap(a):
        return lax.ppermute(a, "mp", z_perm)

    def y_swap(a):
        return lax.ppermute(a, "dp", y_perm)

    def turn(a):
        return lax.ppermute(a, ("group", "mp"), turn_perm)

    def after(value, *others):
        return lax.optimization_barrier((value,) + others)[0]

    def by(flag, a, b, axis):
        return jnp.where(flag == 0, jnp.concatenate([a, b], axis), jnp.concatenate([b, a], axis))

    def body(
        image_tokens, text_tokens, image_modulation, text_modulation, image_cotan, text_cotan,
        group_counts, *tensors,
    ):
        states, moments = tensors[:8], tensors[8:]
        g, d, m = lax.axis_index("group"), lax.axis_index("dp"), lax.axis_index("mp")
        c, xc, zl = g % 2, g // 2, m % 2
        ids = jnp.stack([c, zl, xc]).astype(jnp.int32)

        slots = image_tokens.shape[1]
        image_len, text_len = image_tokens.shape[2], text_tokens.shape[2]
        text_rows = -(-text_len // 32) * 32
        local = image_tokens.shape[3]
        width = local * n_mp
        rows_all = image_len + text_rows
        length = image_len + text_len

        def join(image, text):
            return jnp.concatenate([image, jnp.pad(text, ((0, text_rows - text_len), (0, 0)))], 0)

        mod_rows = jnp.concatenate(
            [
                image_modulation[0].reshape(-1, local),
                text_modulation[0].reshape(-1, local),
                jnp.broadcast_to(group_counts[0].astype(F32), (1, local)),
            ],
            0,
        )
        mod_rows = jnp.pad(mod_rows, ((0, -mod_rows.shape[0] % 8), (0, 0)))

        def lead_form(a):
            return a.transpose(0, 2, 1, 3) if a.ndim == 4 else a[:, None]

        def weight_pair(index):
            piece = lead_form(states[index][:1])[0].astype(BF)
            return by(c, piece, core_swap(piece), 1)

        x_own, c_own, pairs = [None] * slots, [None] * slots, [None] * 8
        jobs = [("m", 0), ("x", 0), ("w", 0), ("w", 4)]
        jobs += [("x", s) for s in range(1, slots)]
        jobs += [("w", 1), ("w", 5), ("w", 2), ("w", 6), ("c", 0), ("w", 3), ("w", 7)]
        jobs += [("c", s) for s in range(1, slots)]
        done = []
        for kind, i in jobs:
            if kind == "m":
                value = mod_rows
            elif kind == "w":
                value = weight_pair(i)
            elif kind == "x":
                value = join(image_tokens[0, i], text_tokens[0, i])
            else:
                value = join(image_cotan[0, i], text_cotan[0, i])
            if len(done) >= 2:
                value = after(value, done[-2])
            value = turn(value)
            done.append(value)
            if kind == "m":
                mod_own = value
            elif kind == "w":
                pairs[i] = value
            elif kind == "x":
                x_own[i] = value
            else:
                c_own[i] = value
        count = mod_own[slots * 12, 0]

        def gather_rows(own):
            pair = by(zl, own, z_swap(own), 1)
            return pair, core_swap(pair)

        mod_full = jnp.concatenate(gather_rows(mod_own), 1)

        def gather_weight(pair, stream):
            px = x_swap(pair)
            if n_dp == 2:
                py = y_swap(pair)
                pd = x_swap(py) if stream == 0 else y_swap(px)
                return by(d, by(xc, pair, px, 1), by(xc, py, pd, 1), 1)
            return lax.all_gather(by(xc, pair, px, 1), "dp", axis=1, tiled=True)

        full = [gather_weight(pairs[i], i // 4) for i in range(8)]
        full = [w if w.shape[0] > 1 else w[0] for w in full]

        def reduce_half(keep, send):
            return (keep.astype(F32) + core_swap(send).astype(F32)).astype(BF)

        def reduce_full(keep, send):
            mine = reduce_half(keep, send)
            mine = (mine.astype(F32) + z_swap(mine).astype(F32)).astype(BF)
            return mine, core_swap(mine)

        def reduce_own(keep, send):
            mine = reduce_half(keep, send)
            away = lax.dynamic_slice_in_dim(mine, (1 - zl) * local, local, 1)
            here = lax.dynamic_slice_in_dim(mine, zl * local, local, 1)
            return (here.astype(F32) + z_swap(away).astype(F32)).astype(BF).astype(F32)

        def column_sums(a):
            return jnp.stack([jnp.sum(a[:image_len], 0), jnp.sum(a[image_len:], 0)])

        def per_row(index, s):
            return jnp.concatenate(
                [
                    jnp.broadcast_to(mod_own[s * 6 + index], (image_len, local)),
                    jnp.broadcast_to(mod_own[(slots + s) * 6 + index], (text_rows, local)),
                ],
                0,
            )

        results, grads_x, modgrads, saved = [], [], [], []
        xs = [gather_rows(a) for a in x_own]
        cs = [gather_rows(a) for a in c_own]
        for s in range(slots):
            places = (image_len, s * 6, (slots + s) * 6)
            live = (s * n_dp + d < count).astype(F32)
            live_ref = live.reshape(1)
            h1, qkv, n1o, inv1 = ln_qkv(ids, *xs[s], mod_full, full[0], full[4], *places)
            mixed, lse = attend(qkv, length, image_len)
            att = reduce_full(*out_project(ids, mixed, full[1], full[5], image_len))
            h2, gbranch, after_own = mid_prepare(ids, live_ref, *xs[s], *att, *cs[s], mod_full, *places)
            act, ginner, bk, bs, gk, gs = mlp(ids, h2, gbranch, full[2], full[6], full[3], full[7], image_len)
            gh2 = reduce_full(gk, gs)
            gatt, gmixed, gafter_own, sums = back_prepare(
                ids, live_ref, *xs[s], *att, *cs[s], *gh2, mod_full, full[1], full[5], *places
            )
            gqkv = attend_back(qkv, gmixed, lse, length, image_len)
            branch = reduce_own(bk, bs)
            gh1 = reduce_own(*input_partial(ids, gqkv, full[0], full[4], image_len))
            q = gh1 * (1.0 + per_row(1, s))
            total = jnp.stack([jnp.sum(q, 1), jnp.sum(q * n1o, 1)])
            total = total + z_swap(total)
            total = (total + core_swap(total)) / width
            gx = gafter_own + inv1[:, :1] * (q - total[0][:, None] - n1o * total[1][:, None])
            res = after_own + per_row(5, s) * branch
            results.append(turn(res.astype(BF)))
            grads_x.append(turn(gx.astype(BF)))
            sums = jnp.sum(sums.reshape(2, 3, 8, local), 2)
            modgrads.append(
                jnp.stack(
                    [
                        column_sums(gh1), column_sums(gh1 * n1o), sums[:, 2], sums[:, 0], sums[:, 1],
                        column_sums(c_own[s].astype(F32) * live * branch),
                    ]
                )
            )
            saved.append(((h1, gqkv), (mixed, gatt), (h2, ginner), (act, gbranch)))
        mod_back = turn(jnp.stack(modgrads).reshape(slots * 12, local)).reshape(slots, 6, 2, local)

        fresh, outer = [None] * 8, [None] * 8
        inv_count = (1.0 / group_counts[0].astype(F32)).reshape(1)
        for k in (3, 2, 1, 0):
            for stream in range(2):
                idx = k + 4 * stream
                lo, hi = (0, image_len) if stream == 0 else (image_len, rows_all)

                def weight_grad(start, size):
                    total = 0.0
                    for s in range(slots):
                        left, right = saved[s][k]
                        left = lax.dynamic_slice_in_dim(left[lo:hi], start, size, 1)
                        if k == 0:
                            part = jnp.einsum("td,ctf->cdf", left, right[:, lo:hi], preferred_element_type=F32)
                        else:
                            part = mm(left, right[lo:hi], TN)[None]
                        total = total + part
                    return total

                rows = saved[0][k][0].shape[1]
                if n_dp == 2:
                    part = rows // 2
                    got = y_swap(weight_grad((1 - d) * part, part).astype(BF))
                    shard = (weight_grad(d * part, part) + got.astype(F32)).astype(BF)
                else:
                    shard = lax.psum_scatter(
                        weight_grad(0, rows).astype(BF), "dp", scatter_dimension=1, tiled=True
                    )
                grad = turn(shard)
                moment = lead_form(moments[idx][0])
                lead, rows, cols = moment.shape[1:]
                piece = rows // n_group
                new, keep, send = adam(
                    ids, inv_count, moment.reshape(2, lead, n_group, piece, cols),
                    grad.reshape(lead, n_group, piece, cols),
                )
                got = core_swap(send)
                pick = lambda a: lax.dynamic_index_in_dim(a, 1 - xc, 0, False)
                far = x_swap((pick(keep).astype(F32) + pick(got).astype(F32)).astype(BF))
                out = outer_step(ids, lead_form(states[idx]), keep, got, far, n_group)
                new = new.reshape(2, lead, rows, cols)
                if moments[idx].ndim == 5:
                    fresh[idx] = new.transpose(0, 2, 1, 3)[None]
                    outer[idx] = out.transpose(0, 2, 1, 3)
                else:
                    fresh[idx] = new[:, 0][None]
                    outer[idx] = out[:, 0]

        res = jnp.stack(results)
        gx = jnp.stack(grads_x)
        return (
            res[None, :, :image_len],
            res[None, :, image_len:length],
            gx[None, :, :image_len],
            gx[None, :, image_len:length],
            mod_back[None, :, :, 0],
            mod_back[None, :, :, 1],
            *fresh,
            *outer,
        )

    tokens = P("group", "dp", None, "mp")
    weight_specs = (
        P(None, ("dp", "group"), None, "mp"),
        P(None, ("mp", "dp", "group"), None),
        P(None, ("dp", "group"), "mp"),
        P(None, ("mp", "dp", "group"), None),
    ) * 2
    moment_specs = (
        P("group", None, "dp", None, "mp"),
        P("group", None, ("mp", "dp"), None),
        P("group", None, "dp", "mp"),
        P("group", None, ("mp", "dp"), None),
    ) * 2
    return jax.shard_map(
        body,
        mesh=mesh,
        in_specs=(tokens,) * 6 + (P("group"),) + weight_specs + moment_specs,
        out_specs=(tokens,) * 6 + moment_specs + weight_specs,
        check_vma=False,
    )
```

time: 2480 us -> 1450 us (0.58)
  waiting for transfers between devices: 1510 us -> 336 us
  Pallas kernels: 0 us -> 445 us
  starting transfers between devices: 3.9 us -> 351 us
  matrix products: 394 us -> 92.9 us
  other arithmetic: 259 us -> 116 us
  local copies, waits for them, and re-layouts: 188 us -> 79.8 us
  blocking collectives: 93.2 us -> 0 us
    all_gather x22 -> x0, waiting for transfers between devices: 731 us -> none  [the longest x4 223 us: spread_rows(): return lax.all_gather(rows, 'mp', axis=1, tiled=True)]
    unnamed x56 -> x0, waiting for transfers between devices: 534 us -> none
    pallas_call x0 -> x32, Pallas kernels: none -> 445 us  [the longest x2 94.2 us: mlp(): call(kernel, (steps,), [whole((rows, width)), whole((rows, width)), w1_sp...]
    ppermute x0 -> x116, starting transfers between devices: none -> 351 us  [the longest x26 158 us: turn(): return lax.ppermute(a, ('group', 'mp'), turn_perm)]
    ppermute x0 -> x116, waiting for transfers between devices: none -> 336 us  [the longest x20 171 us: y_swap(): return lax.ppermute(a, 'dp', y_perm)]
    dot_general x132 -> x32, matrix products: 394 us -> 92.9 us  [the longest x24 66.6 us: mm(): return lax.dot_general(a, b, dims, preferred_element_type=F32)]
    reduce_scatter x14 -> x0, waiting for transfers between devices: 242 us -> none  [the longest x1 54.1 us: body(): lax.psum_scatter(totals[7].astype(jnp.bfloat16), 'dp', scatter_dimension=...]
    unnamed x392 -> x222, local copies, waits for them, and re-layouts: 105 us -> 19.1 us
  transfers between devices with their start and end apart: 46 -> 116, of which waited for: 29 -> 28; matrix products, arithmetic and copies ran while one was open for 32% -> 19% of each run, Pallas kernels for 0% -> 31%
where the time goes in v1:
time: 1450 us; the launch traced here: 1430 us
  Pallas kernels  445 us (31%)
  starting transfers between devices  351 us (24%)
  waiting for transfers between devices  336 us (23%)
  other arithmetic  116 us (8%)
  matrix products  92.9 us (6%)
  local copies, waits for them, and re-layouts  79.8 us (6%)
    ppermute x20, waiting for transfers between devices, y_swap(): return lax.ppermute(a, 'dp', y_perm)  171 us
    ppermute x26, starting transfers between devices, turn(): return lax.ppermute(a, ('group', 'mp'), turn_perm)  158 us
    ppermute x35, starting transfers between devices, core_swap(): return lax.ppermute(a, 'group', core_perm)  128 us
    ppermute x15, waiting for transfers between devices, z_swap(): return lax.ppermute(a, 'mp', z_perm)  102 us
    pallas_call x2, Pallas kernels, mlp(): call(kernel, (steps,), [whole((rows, width)), whole((rows, width)), w1_sp...  94.2 us
    pallas_call x8, Pallas kernels, adam(): call(kernel, (lead, 4), [pairs, pl.BlockSpec((1, 1, piece, cols), lambda...  80.5 us
    dot_general x24, matrix products, mm(): return lax.dot_general(a, b, dims, preferred_element_type=F32)  66.6 us
    pallas_call x2, Pallas kernels, attend_back(): pl.pallas_call(kernel, grid=(pairs,), in_specs=[pl.BlockSpec((3, rows, 12...  65.9 us
  transfers between devices with their start and end apart: 116, of which 28 were waited for; matrix products, arithmetic and copies ran while one was open for 19% of the time, Pallas kernels for 31%

profile of v1, /device:TPU:0, one launch (start us, length us, event | category | flops | bytes accessed | tf_op | source)
XLA Modules:
  0.0 1425.5 jit_solution(3423463768614005313)
XLA Ops:
  82.0 37.1 %collective-permute-start.3 = (bf16[1184,768]{1,0:T(8,128)(2,1)S(1)}, bf16[1184,768]{1,0:T(8,128)(2,1)S(1)}, u32[]{:S(2)}, u32[]{:S(2)}) collective-permute-start(bf16[1184,768]{1,0:T(8,128)(2,1)S(1)} %maximum_select_fusion.14.xm_ref), channel_id=1, source_target_pairs={{0,8},{8,0},{16,24},{24,16},{1,9},{9,1},{17,25},{25,17},{2,10},{10... | collective-permute-start | bytes 5455880 | tf_op jit(solution)/shard_map/ppermute | solution.py:598
  124.5 23.4 %collective-permute-done.24 = bf16[1,96,1536]{2,1,0:T(8,128)(2,1)S(1)} collective-permute-done((bf16[1,96,1536]{2,1,0:T(8,128)(2,1)S(1)}, bf16[1,96,1536]{2,1,0:T(8,128)(2,1)S(1)}, u32[]{:S(2)}, u32[]{:S(2)}) %collective-permute-start.24) | collective-permute-done | bytes 294944 | tf_op jit(solution)/shard_map/ppermute | solution.py:601
  163.3 23.1 %collective-permute-done.56 = bf16[1184,384]{1,0:T(8,128)(2,1)S(1)} collective-permute-done((bf16[1184,384]{1,0:T(8,128)(2,1)S(1)}, bf16[1184,384]{1,0:T(8,128)(2,1)S(1)}, u32[]{:S(2)}, u32[]{:S(2)}) %collective-permute-start.56) | collective-permute-done | bytes 909344 | tf_op jit(solution)/shard_map/ppermute | solution.py:604
  212.3 15.2 %shard_map.390 = (bf16[1184,1536]{1,0:T(8,128)(2,1)}, bf16[3,1184,384]{2,1,0:T(8,128)(2,1)}, f32[1184,384]{1,0:T(8,128)}, f32[1184,128]{1,0:T(8,128)}) custom-call(s32[3]{0:T(128)} %pad_add_fusion.ids_ref, bf16[1184,768]{1,0:T(8,128)(2,1)} %copy-done.2, bf16[1184,768]{1,0:T(8,128)(2,1)} %copy-done.14, f32[32,1536]{1,0:T(8,128)} %pad_maximum_fusion.2.mod_ref, ...), custom_call_target="tpu_custom_call" | custom-call | flops 4190109696 | bytes 17989632 | tf_op jit(solution)/shard_map/pallas_call | solution.py:104
  240.5 22.1 %shard_map.391 = (bf16[1184,384]{1,0:T(8,128)(2,1)}, f32[3,8,1280]{2,1,0:T(8,128)}) custom-call(bf16[3,1184,384]{2,1,0:T(8,128)(2,1)} %get-tuple-element.105.qkv_ref), custom_call_target="tpu_custom_call" | custom-call | flops 8613003264 | bytes 3637248 | tf_op jit(solution)/shard_map/pallas_call | solution.py:161
  279.0 13.0 collective-permute-start.27
  312.2 15.2 %shard_map.395 = (bf16[1184,1536]{1,0:T(8,128)(2,1)}, bf16[3,1184,384]{2,1,0:T(8,128)(2,1)}, f32[1184,384]{1,0:T(8,128)}, f32[1184,128]{1,0:T(8,128)}) custom-call(s32[3]{0:T(128)} %pad_add_fusion.ids_ref, bf16[1184,768]{1,0:T(8,128)(2,1)} %copy-done.3, bf16[1184,768]{1,0:T(8,128)(2,1)} %copy-done.13, f32[32,1536]{1,0:T(8,128)} %pad_maximum_fusion.2.mod_ref, ...), custom_call_target="tpu_custom_call" | custom-call | flops 4190109696 | bytes 17989632 | tf_op jit(solution)/shard_map/pallas_call | solution.py:104
  327.4 22.1 %shard_map.396 = (bf16[1184,384]{1,0:T(8,128)(2,1)}, f32[3,8,1280]{2,1,0:T(8,128)}) custom-call(bf16[3,1184,384]{2,1,0:T(8,128)(2,1)} %get-tuple-element.122.qkv_ref), custom_call_target="tpu_custom_call" | custom-call | flops 8613003264 | bytes 3637248 | tf_op jit(solution)/shard_map/pallas_call | solution.py:161
  377.1 16.6 %collective-permute-done.42 = bf16[1,384,1536]{2,1,0:T(8,128)(2,1)S(1)} collective-permute-done((bf16[1,384,1536]{2,1,0:T(8,128)(2,1)}, bf16[1,384,1536]{2,1,0:T(8,128)(2,1)S(1)}, u32[]{:S(2)}, u32[]{:S(2)}) %collective-permute-start.42) | collective-permute-done | bytes 1179680 | tf_op jit(solution)/shard_map/ppermute | solution.py:607
  410.6 16.0 %collective-permute-done.50 = bf16[1,384,1536]{2,1,0:T(8,128)(2,1)S(1)} collective-permute-done((bf16[1,384,1536]{2,1,0:T(8,128)(2,1)}, bf16[1,384,1536]{2,1,0:T(8,128)(2,1)S(1)}, u32[]{:S(2)}, u32[]{:S(2)}) %collective-permute-start.50) | collective-permute-done | bytes 1179680 | tf_op jit(solution)/shard_map/ppermute | solution.py:601
  432.9 15.5 %collective-permute-done.47 = bf16[1,384,1536]{2,1,0:T(8,128)(2,1)S(1)} collective-permute-done((bf16[1,384,1536]{2,1,0:T(8,128)(2,1)S(1)}, bf16[1,384,1536]{2,1,0:T(8,128)(2,1)S(1)}, u32[]{:S(2)}, u32[]{:S(2)}) %collective-permute-start.47) | collective-permute-done | bytes 1179680 | tf_op jit(solution)/shard_map/ppermute | solution.py:601
  458.9 14.4 %collective-permute-done.52 = bf16[1,384,1536]{2,1,0:T(8,128)(2,1)S(1)} collective-permute-done((bf16[1,384,1536]{2,1,0:T(8,128)(2,1)S(1)}, bf16[1,384,1536]{2,1,0:T(8,128)(2,1)S(1)}, u32[]{:S(2)}, u32[]{:S(2)}) %collective-permute-start.52) | collective-permute-done | bytes 1179680 | tf_op jit(solution)/shard_map/ppermute | solution.py:607
  513.0 47.2 %shard_map.394 = (bf16[1184,1536]{1,0:T(8,128)(2,1)}, bf16[1184,1536]{1,0:T(8,128)(2,1)}, bf16[1184,768]{1,0:T(8,128)(2,1)}, bf16[1184,768]{1,0:T(8,128)(2,1)}, ...) custom-call(s32[3]{0:T(128)} %pad_add_fusion.ids_ref, bf16[1184,1536]{1,0:T(8,128)(2,1)} %get-tuple-element.115.h_ref, ...), custom_call_target="tpu_custom_call" | custom-call | flops 22347251712 | bytes 40697856 | tf_op jit(solution)/shard_map/pallas_call | solution.py:415
  581.8 47.0 %shard_map.399 = (bf16[1184,1536]{1,0:T(8,128)(2,1)}, bf16[1184,1536]{1,0:T(8,128)(2,1)}, bf16[1184,768]{1,0:T(8,128)(2,1)}, bf16[1184,768]{1,0:T(8,128)(2,1)}, ...) custom-call(s32[3]{0:T(128)} %pad_add_fusion.ids_ref, bf16[1184,1536]{1,0:T(8,128)(2,1)} %get-tuple-element.128.h_ref, ...), custom_call_target="tpu_custom_call" | custom-call | flops 22347251712 | bytes 40697856 | tf_op jit(solution)/shard_map/pallas_call | solution.py:415
  675.0 16.9 %collective-permute-done.54 = bf16[1184,384]{1,0:T(8,128)(2,1)S(1)} collective-permute-done((bf16[1184,384]{1,0:T(8,128)(2,1)S(1)}, bf16[1184,384]{1,0:T(8,128)(2,1)S(1)}, u32[]{:S(2)}, u32[]{:S(2)}) %collective-permute-start.54) | collective-permute-done | bytes 909344 | tf_op jit(solution)/shard_map/ppermute | solution.py:604
  705.0 27.9 %collective-permute-done.68 = bf16[1184,768]{1,0:T(8,128)(2,1)S(1)} collective-permute-done((bf16[1184,768]{1,0:T(8,128)(2,1)S(1)}, bf16[1184,768]{1,0:T(8,128)(2,1)S(1)}, u32[]{:S(2)}, u32[]{:S(2)}) %collective-permute-start.68) | collective-permute-done | bytes 1818656 | tf_op jit(solution)/shard_map/ppermute | solution.py:604
  777.2 25.2 %collective-permute-done.96 = bf16[1,768,1536]{2,1,0:T(8,128)(2,1)} collective-permute-done((bf16[1,768,1536]{2,1,0:T(8,128)(2,1)}, bf16[1,768,1536]{2,1,0:T(8,128)(2,1)}, u32[]{:S(2)}, u32[]{:S(2)}) %collective-permute-start.96) | collective-permute-done | bytes 2359328 | tf_op jit(solution)/shard_map/ppermute | solution.py:607
  807.3 45.2 %collective-permute-done.98 = bf16[1,768,1536]{2,1,0:T(8,128)(2,1)} collective-permute-done((bf16[1,768,1536]{2,1,0:T(8,128)(2,1)}, bf16[1,768,1536]{2,1,0:T(8,128)(2,1)}, u32[]{:S(2)}, u32[]{:S(2)}) %collective-permute-start.98) | collective-permute-done | bytes 2359328 | tf_op jit(solution)/shard_map/ppermute | solution.py:607
  852.5 19.2 %collective-permute-start.89 = (bf16[1,768,1536]{2,1,0:T(8,128)(2,1)}, bf16[1,768,1536]{2,1,0:T(8,128)(2,1)}, u32[]{:S(2)}, u32[]{:S(2)}) collective-permute-start(bf16[1,768,1536]{2,1,0:T(8,128)(2,1)} %fusion.3), channel_id=1, source_target_pairs={{0,0},{1,1},{2,8},{3,9},{8,2},{9,3},{10,10},{11,11},{16,16},{17,17... | collective-permute-start | bytes 7077896 | tf_op jit(solution)/shard_map/ppermute | solution.py:610
  876.8 19.2 %collective-permute-start.91 = (bf16[1,768,1536]{2,1,0:T(8,128)(2,1)}, bf16[1,768,1536]{2,1,0:T(8,128)(2,1)}, u32[]{:S(2)}, u32[]{:S(2)}) collective-permute-start(bf16[1,768,1536]{2,1,0:T(8,128)(2,1)} %fusion.2), channel_id=1, source_target_pairs={{0,0},{1,1},{2,8},{3,9},{8,2},{9,3},{10,10},{11,11},{16,16},{17,17... | collective-permute-start | bytes 7077896 | tf_op jit(solution)/shard_map/ppermute | solution.py:610
  896.0 19.2 %collective-permute-start.97 = (bf16[1,768,1536]{2,1,0:T(8,128)(2,1)}, bf16[1,768,1536]{2,1,0:T(8,128)(2,1)}, u32[]{:S(2)}, u32[]{:S(2)}) collective-permute-start(bf16[1,768,1536]{2,1,0:T(8,128)(2,1)} %fusion.1), channel_id=1, source_target_pairs={{0,0},{1,1},{2,8},{3,9},{8,2},{9,3},{10,10},{11,11},{16,16},{17,17... | collective-permute-start | bytes 7077896 | tf_op jit(solution)/shard_map/ppermute | solution.py:610
  916.6 19.2 %collective-permute-start.99 = (bf16[1,768,1536]{2,1,0:T(8,128)(2,1)}, bf16[1,768,1536]{2,1,0:T(8,128)(2,1)}, u32[]{:S(2)}, u32[]{:S(2)}) collective-permute-start(bf16[1,768,1536]{2,1,0:T(8,128)(2,1)} %fusion), channel_id=1, source_target_pairs={{0,0},{1,1},{2,8},{3,9},{8,2},{9,3},{10,10},{11,11},{16,16},{17,17... | collective-permute-start | bytes 7077896 | tf_op jit(solution)/shard_map/ppermute | solution.py:610
  937.7 15.2 %shard_map.400 = (bf16[1184,1536]{1,0:T(8,128)(2,1)}, bf16[1184,384]{1,0:T(8,128)(2,1)}, f32[1184,384]{1,0:T(8,128)}, f32[2,24,384]{2,1,0:T(8,128)}) custom-call(s32[3]{0:T(128)} %pad_add_fusion.ids_ref, f32[1]{0:T(128)} %bitcast.5.live_ref, bf16[1184,768]{1,0:T(8,128)(2,1)} %copy-done.2, bf16[1184,768]{1,0:T(8,128)(2,1)} %copy-done.14, ...), custom_call_target="tpu_custom_call" | custom-call | flops 1396703232 | bytes 21823488 | tf_op jit(solution)/shard_map/pallas_call | solution.py:487
  952.9 32.9 %shard_map.401.a_ref = bf16[3,1184,384]{2,1,0:T(8,128)(2,1)} custom-call(bf16[3,1184,384]{2,1,0:T(8,128)(2,1)} %get-tuple-element.105.qkv_ref, bf16[1184,384]{1,0:T(8,128)(2,1)} %get-tuple-element.136.grad_ref, f32[3,8,1280]{2,1,0:T(8,128)} %get-tuple-element.137.lse_ref), custom_call_target="tpu_custom_call" | custom-call | flops 21532508160 | bytes 6365184 | tf_op jit(solution)/shard_map/pallas_call | solution.py:210
  1046.4 14.1 collective-permute-start.112
  1071.7 15.4 %shard_map.403 = (bf16[1184,1536]{1,0:T(8,128)(2,1)}, bf16[1184,384]{1,0:T(8,128)(2,1)}, f32[1184,384]{1,0:T(8,128)}, f32[2,24,384]{2,1,0:T(8,128)}) custom-call(s32[3]{0:T(128)} %pad_add_fusion.ids_ref, f32[1]{0:T(128)} %bitcast.43.live_ref, bf16[1184,768]{1,0:T(8,128)(2,1)} %copy-done.3, bf16[1184,768]{1,0:T(8,128)(2,1)} %copy-done.13, ...), custom_call_target="tpu_custom_call" | custom-call | flops 1396703232 | bytes 21823488 | tf_op jit(solution)/shard_map/pallas_call | solution.py:487
  1093.8 33.0 %shard_map.404.a_ref = bf16[3,1184,384]{2,1,0:T(8,128)(2,1)} custom-call(bf16[3,1184,384]{2,1,0:T(8,128)(2,1)} %get-tuple-element.122.qkv_ref, bf16[1184,384]{1,0:T(8,128)(2,1)} %get-tuple-element.145.grad_ref, f32[3,8,1280]{2,1,0:T(8,128)} %get-tuple-element.146.lse_ref), custom_call_target="tpu_custom_call" | custom-call | flops 21532508160 | bytes 6365184 | tf_op jit(solution)/shard_map/pallas_call | solution.py:210
  1247.8 30.2 %collective-permute-done.92 = bf16[3,768,384]{1,2,0:T(8,128)(2,1)} collective-permute-done((bf16[3,768,384]{1,2,0:T(8,128)(2,1)}, bf16[3,768,384]{1,2,0:T(8,128)(2,1)}, u32[]{:S(2)}, u32[]{:S(2)}) %collective-permute-start.92) | collective-permute-done | bytes 1769504 | tf_op jit(solution)/shard_map/ppermute | solution.py:607
  1281.6 14.8 %collective-permute-start.93 = (bf16[3,768,384]{1,2,0:T(8,128)(2,1)}, bf16[3,768,384]{1,2,0:T(8,128)(2,1)}, u32[]{:S(2)}, u32[]{:S(2)}) collective-permute-start(bf16[3,768,384]{1,2,0:T(8,128)(2,1)} %fusion.4), channel_id=1, source_target_pairs={{0,0},{1,1},{2,8},{3,9},{8,2},{9,3},{10,10},{11,11},{16,16},{17,17... | collective-permute-start | bytes 5308424 | tf_op jit(solution)/shard_map/ppermute | solution.py:610
  1317.9 12.7 shard_map.406
  1330.5 12.7 shard_map.410
  1343.3 16.4 %collective-permute-start.100 = (bf16[2,3,192,384]{3,2,1,0:T(8,128)(2,1)}, bf16[2,3,192,384]{3,2,1,0:T(8,128)(2,1)}, u32[]{:S(2)}, u32[]{:S(2)}) collective-permute-start(bf16[2,3,192,384]{3,2,1,0:T(8,128)(2,1)} %get-tuple-element.169), channel_id=1, source_target_pairs={{0,8},{8,0},{16,24},{24,16},{1,9},{9,1},{17,25},{25,17},{2,10},{10... | collective-permute-start | bytes 2654216 | tf_op jit(solution)/shard_map/ppermute | solution.py:598
  (670 shorter events, 702.9 us)
Async XLA Ops:
  80.3 117.0 %collective-permute-start.14 = (bf16[3,384,384]{2,1,0:T(8,128)(2,1)S(1)}, bf16[3,384,384]{2,1,0:T(8,128)(2,1)S(1)}, u32[]{:S(2)}, u32[]{:S(2)}) collective-permute-start(bf16[3,384,384]{2,1,0:T(8,128)(2,1)S(1)} %collective-permute-done.12), channel_id=1, source_target_pairs={{0,4},{4,0},{1,5},{5,1},{2,6},{6,2},{3,7},{7,3},{8,12},{12,8},{9,1... | collective-permute-start | bytes 2654216 | tf_op jit(solution)/shard_map/ppermute | solution.py:607
  82.0 129.1 %collective-permute-start.3 = (bf16[1184,768]{1,0:T(8,128)(2,1)S(1)}, bf16[1184,768]{1,0:T(8,128)(2,1)S(1)}, u32[]{:S(2)}, u32[]{:S(2)}) collective-permute-start(bf16[1184,768]{1,0:T(8,128)(2,1)S(1)} %maximum_select_fusion.14.xm_ref), channel_id=1, source_target_pairs={{0,8},{8,0},{16,24},{24,16},{1,9},{9,1},{17,25},{25,17},{2,10},{10... | collective-permute-start | bytes 5455880 | tf_op jit(solution)/shard_map/ppermute | solution.py:598
  197.2 113.4 %collective-permute-start.57 = (bf16[1184,768]{1,0:T(8,128)(2,1)S(1)}, bf16[1184,768]{1,0:T(8,128)(2,1)S(1)}, u32[]{:S(2)}, u32[]{:S(2)}) collective-permute-start(bf16[1184,768]{1,0:T(8,128)(2,1)S(1)} %maximum_select_fusion.16.xm_ref), channel_id=1, source_target_pairs={{0,8},{8,0},{16,24},{24,16},{1,9},{9,1},{17,25},{25,17},{2,10},{10... | collective-permute-start | bytes 5455880 | tf_op jit(solution)/shard_map/ppermute | solution.py:598
  205.6 104.9 %collective-permute-start.36 = (bf16[1,384,1536]{2,1,0:T(8,128)(2,1)}, bf16[1,384,1536]{2,1,0:T(8,128)(2,1)}, u32[]{:S(2)}, u32[]{:S(2)}) collective-permute-start(bf16[1,384,1536]{2,1,0:T(8,128)(2,1)} %collective-permute-done.31), channel_id=1, source_target_pairs={{0,4},{4,0},{1,5},{5,1},{2,6},{6,2},{3,7},{7,3},{8,12},{12,8},{9,1... | collective-permute-start | bytes 3538952 | tf_op jit(solution)/shard_map/ppermute | solution.py:607
  279.0 89.5 %collective-permute-start.27 = (bf16[1184,768]{1,0:T(8,128)(2,1)}, bf16[1184,768]{1,0:T(8,128)(2,1)}, u32[]{:S(2)}, u32[]{:S(2)}) collective-permute-start(bf16[1184,768]{1,0:T(8,128)(2,1)} %get-tuple-element.111), channel_id=1, source_target_pairs={{0,8},{8,0},{16,24},{24,16},{1,9},{9,1},{17,25},{25,17},{2,10},{10... | collective-permute-start | bytes 5455880 | tf_op jit(solution)/shard_map/ppermute | solution.py:598
  295.8 79.1 %collective-permute-start.41 = (bf16[1,384,1536]{2,1,0:T(8,128)(2,1)}, bf16[1,384,1536]{2,1,0:T(8,128)(2,1)}, u32[]{:S(2)}, u32[]{:S(2)}) collective-permute-start(bf16[1,384,1536]{2,1,0:T(8,128)(2,1)} %collective-permute-done.39), channel_id=1, source_target_pairs={{0,4},{4,0},{1,5},{5,1},{2,6},{6,2},{3,7},{7,3},{8,12},{12,8},{9,1... | collective-permute-start | bytes 3538952 | tf_op jit(solution)/shard_map/ppermute | solution.py:607
  300.0 76.2 %collective-permute-start.49 = (bf16[1,384,1536]{2,1,0:T(8,128)(2,1)}, bf16[1,384,1536]{2,1,0:T(8,128)(2,1)}, u32[]{:S(2)}, u32[]{:S(2)}) collective-permute-start(bf16[1,384,1536]{2,1,0:T(8,128)(2,1)} %maximum_select_fusion.27), channel_id=1, source_target_pairs={{0,0},{1,1},{2,8},{3,9},{8,2},{9,3},{10,10},{11,11},{16,16},{17,17... | collective-permute-start | bytes 3538952 | tf_op jit(solution)/shard_map/ppermute | solution.py:610
  410.6 82.7 %collective-permute-start.34 = (bf16[1184,768]{1,0:T(8,128)(2,1)S(1)}, bf16[1184,768]{1,0:T(8,128)(2,1)S(1)}, u32[]{:S(2)}, u32[]{:S(2)}) collective-permute-start(bf16[1184,768]{1,0:T(8,128)(2,1)S(1)} %maximum_select_fusion.15.cm_ref), channel_id=1, source_target_pairs={{0,8},{8,0},{16,24},{24,16},{1,9},{9,1},{17,25},{25,17},{2,10},{10... | collective-permute-start | bytes 5455880 | tf_op jit(solution)/shard_map/ppermute | solution.py:598
  448.5 117.3 %collective-permute-start.63 = (bf16[1184,768]{1,0:T(8,128)(2,1)S(1)}, bf16[1184,768]{1,0:T(8,128)(2,1)S(1)}, u32[]{:S(2)}, u32[]{:S(2)}) collective-permute-start(bf16[1184,768]{1,0:T(8,128)(2,1)S(1)} %maximum_select_fusion.17.cm_ref), channel_id=1, source_target_pairs={{0,8},{8,0},{16,24},{24,16},{1,9},{9,1},{17,25},{25,17},{2,10},{10... | collective-permute-start | bytes 5455880 | tf_op jit(solution)/shard_map/ppermute | solution.py:598
  565.1 102.3 %collective-permute-start.53 = (bf16[1184,768]{1,0:T(8,128)(2,1)}, bf16[1184,768]{1,0:T(8,128)(2,1)}, u32[]{:S(2)}, u32[]{:S(2)}) collective-permute-start(bf16[1184,768]{1,0:T(8,128)(2,1)} %get-tuple-element.121), channel_id=1, source_target_pairs={{0,8},{8,0},{16,24},{24,16},{1,9},{9,1},{17,25},{25,17},{2,10},{10... | collective-permute-start | bytes 5455880 | tf_op jit(solution)/shard_map/ppermute | solution.py:598
  565.6 106.5 %collective-permute-start.67 = (bf16[1184,768]{1,0:T(8,128)(2,1)}, bf16[1184,768]{1,0:T(8,128)(2,1)}, u32[]{:S(2)}, u32[]{:S(2)}) collective-permute-start(bf16[1184,768]{1,0:T(8,128)(2,1)} %get-tuple-element.133), channel_id=1, source_target_pairs={{0,8},{8,0},{16,24},{24,16},{1,9},{9,1},{17,25},{25,17},{2,10},{10... | collective-permute-start | bytes 5455880 | tf_op jit(solution)/shard_map/ppermute | solution.py:598
  646.9 88.3 %collective-permute-start.88 = (bf16[1,768,1536]{2,1,0:T(8,128)(2,1)}, bf16[1,768,1536]{2,1,0:T(8,128)(2,1)}, u32[]{:S(2)}, u32[]{:S(2)}) collective-permute-start(bf16[1,768,1536]{2,1,0:T(8,128)(2,1)} %fusion.6), channel_id=1, source_target_pairs={{0,4},{4,0},{1,5},{5,1},{2,6},{6,2},{3,7},{7,3},{8,12},{12,8},{9,1... | collective-permute-start | bytes 7077896 | tf_op jit(solution)/shard_map/ppermute | solution.py:607
  672.2 79.7 %collective-permute-start.90 = (bf16[1,768,1536]{2,1,0:T(8,128)(2,1)}, bf16[1,768,1536]{2,1,0:T(8,128)(2,1)}, u32[]{:S(2)}, u32[]{:S(2)}) collective-permute-start(bf16[1,768,1536]{2,1,0:T(8,128)(2,1)} %fusion.7), channel_id=1, source_target_pairs={{0,4},{4,0},{1,5},{5,1},{2,6},{6,2},{3,7},{7,3},{8,12},{12,8},{9,1... | collective-permute-start | bytes 7077896 | tf_op jit(solution)/shard_map/ppermute | solution.py:607
  697.7 104.7 %collective-permute-start.96 = (bf16[1,768,1536]{2,1,0:T(8,128)(2,1)}, bf16[1,768,1536]{2,1,0:T(8,128)(2,1)}, u32[]{:S(2)}, u32[]{:S(2)}) collective-permute-start(bf16[1,768,1536]{2,1,0:T(8,128)(2,1)} %fusion.8), channel_id=1, source_target_pairs={{0,4},{4,0},{1,5},{5,1},{2,6},{6,2},{3,7},{7,3},{8,12},{12,8},{9,1... | collective-permute-start | bytes 7077896 | tf_op jit(solution)/shard_map/ppermute | solution.py:607
  701.5 151.0 %collective-permute-start.98 = (bf16[1,768,1536]{2,1,0:T(8,128)(2,1)}, bf16[1,768,1536]{2,1,0:T(8,128)(2,1)}, u32[]{:S(2)}, u32[]{:S(2)}) collective-permute-start(bf16[1,768,1536]{2,1,0:T(8,128)(2,1)} %fusion.9), channel_id=1, source_target_pairs={{0,4},{4,0},{1,5},{5,1},{2,6},{6,2},{3,7},{7,3},{8,12},{12,8},{9,1... | collective-permute-start | bytes 7077896 | tf_op jit(solution)/shard_map/ppermute | solution.py:607
  732.9 143.9 %collective-permute-start.55 = (bf16[1184,384]{1,0:T(8,128)(2,1)}, bf16[1184,384]{1,0:T(8,128)(2,1)S(1)}, u32[]{:S(2)}, u32[]{:S(2)}) collective-permute-start(bf16[1184,384]{1,0:T(8,128)(2,1)} %get-tuple-element.293), channel_id=1, source_target_pairs={{0,0},{1,1},{2,8},{3,9},{8,2},{9,3},{10,10},{11,11},{16,16},{17,17... | collective-permute-start | bytes 2727944 | tf_op jit(solution)/shard_map/ppermute | solution.py:610
  751.9 164.7 %collective-permute-start.76 = (bf16[1184,768]{1,0:T(8,128)(2,1)S(1)}, bf16[1184,768]{1,0:T(8,128)(2,1)S(1)}, u32[]{:S(2)}, u32[]{:S(2)}) collective-permute-start(bf16[1184,768]{1,0:T(8,128)(2,1)S(1)} %add_convert_fusion.6), channel_id=1, source_target_pairs={{0,1},{1,0},{2,3},{3,2},{4,5},{5,4},{6,7},{7,6},{8,9},{9,8},{10,11... | collective-permute-start | bytes 5455880 | tf_op jit(solution)/shard_map/ppermute | solution.py:604
  767.1 169.3 %collective-permute-start.69 = (bf16[1184,768]{1,0:T(8,128)(2,1)S(1)}, bf16[1184,768]{1,0:T(8,128)(2,1)S(1)}, u32[]{:S(2)}, u32[]{:S(2)}) collective-permute-start(bf16[1184,768]{1,0:T(8,128)(2,1)S(1)} %add_convert_fusion.8.gm_ref), channel_id=1, source_target_pairs={{0,8},{8,0},{16,24},{24,16},{1,9},{9,1},{17,25},{25,17},{2,10},{10... | collective-permute-start | bytes 5455880 | tf_op jit(solution)/shard_map/ppermute | solution.py:598
  802.4 93.6 %collective-permute-start.66 = (bf16[1184,384]{1,0:T(8,128)(2,1)S(1)}, bf16[1184,384]{1,0:T(8,128)(2,1)S(1)}, u32[]{:S(2)}, u32[]{:S(2)}) collective-permute-start(bf16[1184,384]{1,0:T(8,128)(2,1)S(1)} %get-tuple-element.295), channel_id=1, source_target_pairs={{0,0},{1,1},{2,8},{3,9},{8,2},{9,3},{10,10},{11,11},{16,16},{17,17... | collective-permute-start | bytes 2727944 | tf_op jit(solution)/shard_map/ppermute | solution.py:610
  852.5 151.4 %collective-permute-start.89 = (bf16[1,768,1536]{2,1,0:T(8,128)(2,1)}, bf16[1,768,1536]{2,1,0:T(8,128)(2,1)}, u32[]{:S(2)}, u32[]{:S(2)}) collective-permute-start(bf16[1,768,1536]{2,1,0:T(8,128)(2,1)} %fusion.3), channel_id=1, source_target_pairs={{0,0},{1,1},{2,8},{3,9},{8,2},{9,3},{10,10},{11,11},{16,16},{17,17... | collective-permute-start | bytes 7077896 | tf_op jit(solution)/shard_map/ppermute | solution.py:610
  876.8 138.9 %collective-permute-start.91 = (bf16[1,768,1536]{2,1,0:T(8,128)(2,1)}, bf16[1,768,1536]{2,1,0:T(8,128)(2,1)}, u32[]{:S(2)}, u32[]{:S(2)}) collective-permute-start(bf16[1,768,1536]{2,1,0:T(8,128)(2,1)} %fusion.2), channel_id=1, source_target_pairs={{0,0},{1,1},{2,8},{3,9},{8,2},{9,3},{10,10},{11,11},{16,16},{17,17... | collective-permute-start | bytes 7077896 | tf_op jit(solution)/shard_map/ppermute | solution.py:610
  896.0 130.8 %collective-permute-start.97 = (bf16[1,768,1536]{2,1,0:T(8,128)(2,1)}, bf16[1,768,1536]{2,1,0:T(8,128)(2,1)}, u32[]{:S(2)}, u32[]{:S(2)}) collective-permute-start(bf16[1,768,1536]{2,1,0:T(8,128)(2,1)} %fusion.1), channel_id=1, source_target_pairs={{0,0},{1,1},{2,8},{3,9},{8,2},{9,3},{10,10},{11,11},{16,16},{17,17... | collective-permute-start | bytes 7077896 | tf_op jit(solution)/shard_map/ppermute | solution.py:610
  916.6 129.8 %collective-permute-start.99 = (bf16[1,768,1536]{2,1,0:T(8,128)(2,1)}, bf16[1,768,1536]{2,1,0:T(8,128)(2,1)}, u32[]{:S(2)}, u32[]{:S(2)}) collective-permute-start(bf16[1,768,1536]{2,1,0:T(8,128)(2,1)} %fusion), channel_id=1, source_target_pairs={{0,0},{1,1},{2,8},{3,9},{8,2},{9,3},{10,10},{11,11},{16,16},{17,17... | collective-permute-start | bytes 7077896 | tf_op jit(solution)/shard_map/ppermute | solution.py:610
  937.7 133.9 %collective-permute-start.77 = (bf16[1184,768]{1,0:T(8,128)(2,1)S(1)}, bf16[1184,768]{1,0:T(8,128)(2,1)}, u32[]{:S(2)}, u32[]{:S(2)}) collective-permute-start(bf16[1184,768]{1,0:T(8,128)(2,1)S(1)} %add_convert_fusion.5.gm_ref), channel_id=1, source_target_pairs={{0,8},{8,0},{16,24},{24,16},{1,9},{9,1},{17,25},{25,17},{2,10},{10... | collective-permute-start | bytes 5455880 | tf_op jit(solution)/shard_map/ppermute | solution.py:598
  1003.9 158.9 %collective-permute-start.70 = (bf16[1184,768]{1,0:T(8,128)(2,1)}, bf16[1184,768]{1,0:T(8,128)(2,1)}, u32[]{:S(2)}, u32[]{:S(2)}) collective-permute-start(bf16[1184,768]{1,0:T(8,128)(2,1)} %get-tuple-element.139), channel_id=1, source_target_pairs={{0,8},{8,0},{16,24},{24,16},{1,9},{9,1},{17,25},{25,17},{2,10},{10... | collective-permute-start | bytes 5455880 | tf_op jit(solution)/shard_map/ppermute | solution.py:598
  1015.6 144.8 %collective-permute-start.104 = (bf16[2,1,192,1536]{3,2,1,0:T(8,128)(2,1)}, bf16[2,1,192,1536]{3,2,1,0:T(8,128)(2,1)S(1)}, u32[]{:S(2)}, u32[]{:S(2)}) collective-permute-start(bf16[2,1,192,1536]{3,2,1,0:T(8,128)(2,1)} %get-tuple-element.173), channel_id=1, source_target_pairs={{0,8},{8,0},{16,24},{24,16},{1,9},{9,1},{17,25},{25,17},{2,10},{10... | collective-permute-start | bytes 3538952 | tf_op jit(solution)/shard_map/ppermute | solution.py:598
  1026.8 163.0 %collective-permute-start.106 = (bf16[2,1,192,1536]{3,2,1,0:T(8,128)(2,1)}, bf16[2,1,192,1536]{3,2,1,0:T(8,128)(2,1)}, u32[]{:S(2)}, u32[]{:S(2)}) collective-permute-start(bf16[2,1,192,1536]{3,2,1,0:T(8,128)(2,1)} %get-tuple-element.175), channel_id=1, source_target_pairs={{0,8},{8,0},{16,24},{24,16},{1,9},{9,1},{17,25},{25,17},{2,10},{10... | collective-permute-start | bytes 3538952 | tf_op jit(solution)/shard_map/ppermute | solution.py:598
  1046.4 146.3 %collective-permute-start.112 = (bf16[2,1,192,1536]{3,2,1,0:T(8,128)(2,1)}, bf16[2,1,192,1536]{3,2,1,0:T(8,128)(2,1)}, u32[]{:S(2)}, u32[]{:S(2)}) collective-permute-start(bf16[2,1,192,1536]{3,2,1,0:T(8,128)(2,1)} %get-tuple-element.181), channel_id=1, source_target_pairs={{0,8},{8,0},{16,24},{24,16},{1,9},{9,1},{17,25},{25,17},{2,10},{10... | collective-permute-start | bytes 3538952 | tf_op jit(solution)/shard_map/ppermute | solution.py:598
  1071.6 127.7 %collective-permute-start.114 = (bf16[2,1,192,1536]{3,2,1,0:T(8,128)(2,1)}, bf16[2,1,192,1536]{3,2,1,0:T(8,128)(2,1)}, u32[]{:S(2)}, u32[]{:S(2)}) collective-permute-start(bf16[2,1,192,1536]{3,2,1,0:T(8,128)(2,1)} %get-tuple-element.183), channel_id=1, source_target_pairs={{0,8},{8,0},{16,24},{24,16},{1,9},{9,1},{17,25},{25,17},{2,10},{10... | collective-permute-start | bytes 3538952 | tf_op jit(solution)/shard_map/ppermute | solution.py:598
  1202.8 75.2 %collective-permute-start.92 = (bf16[3,768,384]{1,2,0:T(8,128)(2,1)}, bf16[3,768,384]{1,2,0:T(8,128)(2,1)}, u32[]{:S(2)}, u32[]{:S(2)}) collective-permute-start(bf16[3,768,384]{1,2,0:T(8,128)(2,1)} %fusion.99), channel_id=1, source_target_pairs={{0,4},{4,0},{1,5},{5,1},{2,6},{6,2},{3,7},{7,3},{8,12},{12,8},{9,1... | collective-permute-start | bytes 5308424 | tf_op jit(solution)/shard_map/ppermute | solution.py:607
  1209.1 134.2 %collective-permute-start.105 = (bf16[1,192,1536]{2,1,0:T(8,128)(2,1)}, bf16[1,192,1536]{2,1,0:T(8,128)(2,1)}, u32[]{:S(2)}, u32[]{:S(2)}) collective-permute-start(bf16[1,192,1536]{2,1,0:T(8,128)(2,1)} %fusion.108), channel_id=1, source_target_pairs={{0,16},{8,24},{16,0},{24,8},{1,17},{9,25},{17,1},{25,9},{2,18},{10... | collective-permute-start | bytes 1769480 | tf_op jit(solution)/shard_map/ppermute | solution.py:601
  1237.8 121.8 %collective-permute-start.107 = (bf16[1,192,1536]{2,1,0:T(8,128)(2,1)}, bf16[1,192,1536]{2,1,0:T(8,128)(2,1)}, u32[]{:S(2)}, u32[]{:S(2)}) collective-permute-start(bf16[1,192,1536]{2,1,0:T(8,128)(2,1)} %fusion.109), channel_id=1, source_target_pairs={{0,16},{8,24},{16,0},{24,8},{1,17},{9,25},{17,1},{25,9},{2,18},{10... | collective-permute-start | bytes 1769480 | tf_op jit(solution)/shard_map/ppermute | solution.py:601
  (190 other events, 3745.9 us)

commit v2 on v1

--- a/solution.py
+++ b/solution.py
@@ -18,6 +18,7 @@
 OUTER_MOMENT = 0.9
 BLOCK = 256
 VMEM_BYTES = 60 * 1024 * 1024
+COST_SHARE = 4
 NT = (((1,), (1,)), ((), ()))
 NN = (((1,), (0,)), ((), ()))
 TN = (((0,), (0,)), ((), ()))
@@ -25,6 +26,12 @@
 
 def mm(a, b, dims=NN):
     return lax.dot_general(a, b, dims, preferred_element_type=F32)
+
+
+def cost(flops, nbytes):
+    return pl.CostEstimate(
+        flops=int(flops) // COST_SHARE, bytes_accessed=int(nbytes) // COST_SHARE, transcendentals=0
+    )
 
 
 def call(kernel, grid, in_specs, out_specs, out_shape, flops, nbytes, scratch=(), prefetch=1):
@@ -41,7 +48,7 @@
         compiler_params=pltpu.CompilerParams(
             vmem_limit_bytes=VMEM_BYTES, dimension_semantics=("arbitrary",) * len(grid)
         ),
-        cost_estimate=pl.CostEstimate(flops=int(flops), bytes_accessed=int(nbytes), transcendentals=0),
+        cost_estimate=cost(flops, nbytes),
     )
 
 
@@ -55,6 +62,86 @@
 
 def struct(shape, dtype):
     return jax.ShapeDtypeStruct(shape, dtype)
+
+
+def cast_states(states):
+    cols = states[0].shape[-1]
+    sizes = [s.shape[1] * s.shape[2] for s in states]
+
+    def kernel(*refs):
+        out_ref, at = refs[-1], 0
+        for ref, state in zip(refs, states):
+            for lead in range(state.shape[1]):
+                rows = state.shape[2]
+                out_ref[at : at + rows, :] = ref[0, lead].astype(BF)
+                at += rows
+
+    return call(
+        kernel,
+        (1,),
+        [pl.BlockSpec((1,) + s.shape[1:], lambda *_: (0, 0, 0, 0), pipeline_mode=pl.Buffered(1)) for s in states],
+        whole((sum(sizes), cols)),
+        struct((sum(sizes), cols), BF),
+        sum(sizes) * cols,
+        sum(sizes) * cols * 6,
+        prefetch=0,
+    )(*states)
+
+
+def pair_pieces(ids, mine, other, shapes):
+    cols = mine.shape[1]
+
+    def kernel(ids_ref, m_ref, o_ref, *out_refs):
+        def lay(first_ref, second_ref):
+            at = 0
+            for out_ref, group in zip(out_refs, shapes):
+                for k, (lead, rows) in enumerate(group):
+                    for j in range(lead):
+                        out_ref[k * lead + j, :rows, :] = first_ref[at : at + rows, :]
+                        out_ref[k * lead + j, rows:, :] = second_ref[at : at + rows, :]
+                        at += rows
+
+        @pl.when(ids_ref[0] == 0)
+        def _():
+            lay(m_ref, o_ref)
+
+        @pl.when(ids_ref[0] == 1)
+        def _():
+            lay(o_ref, m_ref)
+
+    outs = [(len(group) * group[0][0], 2 * group[0][1], cols) for group in shapes]
+    return call(
+        kernel,
+        (1,),
+        [whole(mine.shape), whole(mine.shape)],
+        [whole(s) for s in outs],
+        [struct(s, BF) for s in outs],
+        mine.size,
+        mine.size * 8,
+    )(ids, mine, other)
+
+
+def lay_quads(ids, parts):
+    lead, rows, cols = parts[0].shape
+
+    def kernel(ids_ref, *refs):
+        copies = []
+        for k in range(4):
+            at = pl.multiple_of(ids_ref[5 + k] * rows, 16)
+            copies.append(pltpu.make_async_copy(refs[k], refs[4].at[:, pl.ds(at, rows), :], refs[5].at[k]))
+            copies[-1].start()
+        for copy in copies:
+            copy.wait()
+
+    return pl.pallas_call(
+        kernel,
+        in_specs=[pl.BlockSpec(memory_space=pltpu.SMEM)] + [pl.BlockSpec(memory_space=pl.ANY)] * 4,
+        out_specs=pl.BlockSpec(memory_space=pl.ANY),
+        out_shape=struct((lead, 4 * rows, cols), BF),
+        scratch_shapes=[pltpu.SemaphoreType.DMA((4,))],
+        compiler_params=pltpu.CompilerParams(vmem_limit_bytes=1024 * 1024),
+        cost_estimate=cost(0, lead * rows * cols * 16),
+    )(ids, *parts)
 
 
 def ln_qkv(ids, xm, xo, mod, wi, wt, image_len, image_row, text_row):
@@ -169,9 +256,7 @@
         out_shape=[struct((rows, local), BF), struct((pairs, 8, lanes), F32)],
         scratch_shapes=[pltpu.VMEM((rows, BLOCK), F32)],
         compiler_params=pltpu.CompilerParams(vmem_limit_bytes=VMEM_BYTES),
-        cost_estimate=pl.CostEstimate(
-            flops=16 * rows * rows * local, bytes_accessed=rows * local * 8, transcendentals=0
-        ),
+        cost_estimate=cost(16 * rows * rows * local, rows * local * 8),
     )(qkv)
 
 
@@ -223,9 +308,7 @@
             pltpu.VMEM((rows, 128), F32),
         ],
         compiler_params=pltpu.CompilerParams(vmem_limit_bytes=VMEM_BYTES),
-        cost_estimate=pl.CostEstimate(
-            flops=40 * rows * rows * local, bytes_accessed=rows * local * 14, transcendentals=0
-        ),
+        cost_estimate=cost(40 * rows * rows * local, rows * local * 14),
     )(qkv, grad, lse)
 
 
@@ -360,7 +443,7 @@
     return v * up, up + 0.5 * v * (1.0 - t * t) * (k * (1.0 + 3.0 * c3 * v2))
 
 
-def mlp(ids, h, g, w1i, w1t, w2i, w2t, image_len, tile=256):
+def mlp(ids, h, g, w1i, w1t, w2i, w2t, image_len, tile=512):
     rows, width = h.shape
     half = width // 2
     hidden = w1i.shape[1]
@@ -506,6 +589,62 @@
     )(ids, live, xm, xo, am, ao, cm, co, gm, go, mod, wi, wt)
 
 
+def grad_specs(right, tile, height, row_block):
+    if right.ndim == 3:
+        return (
+            pl.BlockSpec((1, height, right.shape[2]), lambda j, *_: (j, row_block, 0)),
+            right.shape[0],
+            right.shape[2],
+        )
+    return pl.BlockSpec((height, tile), lambda j, *_: (row_block, j)), right.shape[1] // tile, tile
+
+
+def grad_out(right, tile, part):
+    if right.ndim == 3:
+        lead, _, cols = right.shape
+        return pl.BlockSpec((1, part, cols), lambda j, *_: (j, 0, 0)), struct((lead, part, cols), BF)
+    return (
+        pl.BlockSpec((1, part, tile), lambda j, *_: (0, 0, j)),
+        struct((1, part, right.shape[1]), BF),
+    )
+
+
+def weight_grad(ids, which, lefts, rights, height, add=None, tile=512):
+    part = lefts[0].shape[1] // 2
+    n = len(lefts)
+    right_spec, steps, _ = grad_specs(rights[0], tile, height, 0)
+    narrow = part % 128 != 0
+    left_spec = pl.BlockSpec(
+        (height, 2 * part if narrow else part),
+        lambda j, ids_ref: (0, 0 if narrow else ids_ref[which]),
+        pipeline_mode=pl.Buffered(1),
+    )
+    out_spec, out_shape = grad_out(rights[0], tile, part)
+    flat = rights[0].ndim == 2
+
+    def kernel(ids_ref, *refs):
+        total = None
+        for left_ref, right_ref in zip(refs[:n], refs[n : 2 * n]):
+            value = mm(left_ref[...], right_ref[...] if flat else right_ref[0], TN)
+            total = value if total is None else total + value
+        if narrow:
+            total = jnp.where(ids_ref[which] == 0, total[:part], total[part:])
+        if add is not None:
+            total = total + refs[2 * n][0].astype(F32)
+        refs[-1][0] = total.astype(BF)
+
+    more = [] if add is None else [add]
+    return call(
+        kernel,
+        (steps,),
+        [left_spec] * n + [right_spec] * n + [out_spec] * len(more),
+        out_spec,
+        out_shape,
+        2 * n * height * part * out_shape.shape[0] * out_shape.shape[2],
+        n * height * (part + out_shape.shape[0] * out_shape.shape[2]) * 2,
+    )(ids, *lefts, *rights, *more)
+
+
 def adam(ids, inv_count, moment, grad):
     _, lead, _, piece, cols = moment.shape
     correct_one = 1.0 - BETA_ONE**STEP
@@ -609,9 +748,6 @@
     def turn(a):
         return lax.ppermute(a, ("group", "mp"), turn_perm)
 
-    def after(value, *others):
-        return lax.optimization_barrier((value,) + others)[0]
-
     def by(flag, a, b, axis):
         return jnp.where(flag == 0, jnp.concatenate([a, b], axis), jnp.concatenate([b, a], axis))
 
@@ -622,7 +758,8 @@
         states, moments = tensors[:8], tensors[8:]
         g, d, m = lax.axis_index("group"), lax.axis_index("dp"), lax.axis_index("mp")
         c, xc, zl = g % 2, g // 2, m % 2
-        ids = jnp.stack([c, zl, xc]).astype(jnp.int32)
+        place = (d % 2) * 2 + xc
+        ids = jnp.stack([c, zl, xc, d % 2, 1 - d % 2, place, place ^ 1, place ^ 2, place ^ 3]).astype(jnp.int32)
 
         slots = image_tokens.shape[1]
         image_len, text_len = image_tokens.shape[2], text_tokens.shape[2]
@@ -632,85 +769,92 @@
         rows_all = image_len + text_rows
         length = image_len + text_len
 
-        def join(image, text):
+        last = []
+
+        def hold(value, others):
+            if not others:
+                return value
+            leaves, tree = jax.tree.flatten(value)
+            held = lax.optimization_barrier(tuple(leaves) + tuple(others))
+            return jax.tree.unflatten(tree, list(held[: len(leaves)]))
+
+        def step(fn, first, *rest, need=()):
+            out = fn(hold(first, last + jax.tree.leaves(need)), *rest)
+            last[:] = [jax.tree.leaves(out)[0]]
+            return out
+
+        def send(move, value):
+            return move(hold(value, last))
+
+        turned, over_x, over_y, over_z = (lambda value, move=move: send(move, value) for move in (turn, x_swap, y_swap, z_swap))
+
+        def sync(*need):
+            if n_dp == 2:
+                last.extend(jax.tree.leaves(need))
+
+        def join(tokens):
+            image, text = tokens
             return jnp.concatenate([image, jnp.pad(text, ((0, text_rows - text_len), (0, 0)))], 0)
 
-        mod_rows = jnp.concatenate(
-            [
-                image_modulation[0].reshape(-1, local),
-                text_modulation[0].reshape(-1, local),
-                jnp.broadcast_to(group_counts[0].astype(F32), (1, local)),
-            ],
-            0,
-        )
-        mod_rows = jnp.pad(mod_rows, ((0, -mod_rows.shape[0] % 8), (0, 0)))
+        def mod_join(parts):
+            image, text, counts = parts
+            rows = jnp.concatenate(
+                [
+                    image[0].reshape(-1, local),
+                    text[0].reshape(-1, local),
+                    jnp.broadcast_to(counts[0].astype(F32), (1, local)),
+                ],
+                0,
+            )
+            return jnp.pad(rows, ((0, -rows.shape[0] % 8), (0, 0)))
 
         def lead_form(a):
             return a.transpose(0, 2, 1, 3) if a.ndim == 4 else a[:, None]
 
-        def weight_pair(index):
-            piece = lead_form(states[index][:1])[0].astype(BF)
-            return by(c, piece, core_swap(piece), 1)
-
-        x_own, c_own, pairs = [None] * slots, [None] * slots, [None] * 8
-        jobs = [("m", 0), ("x", 0), ("w", 0), ("w", 4)]
-        jobs += [("x", s) for s in range(1, slots)]
-        jobs += [("w", 1), ("w", 5), ("w", 2), ("w", 6), ("c", 0), ("w", 3), ("w", 7)]
-        jobs += [("c", s) for s in range(1, slots)]
-        done = []
-        for kind, i in jobs:
-            if kind == "m":
-                value = mod_rows
-            elif kind == "w":
-                value = weight_pair(i)
-            elif kind == "x":
-                value = join(image_tokens[0, i], text_tokens[0, i])
-            else:
-                value = join(image_cotan[0, i], text_cotan[0, i])
-            if len(done) >= 2:
-                value = after(value, done[-2])
-            value = turn(value)
-            done.append(value)
-            if kind == "m":
-                mod_own = value
-            elif kind == "w":
-                pairs[i] = value
-            elif kind == "x":
-                x_own[i] = value
-            else:
-                c_own[i] = value
-        count = mod_own[slots * 12, 0]
-
-        def gather_rows(own):
-            pair = by(zl, own, z_swap(own), 1)
-            return pair, core_swap(pair)
-
-        mod_full = jnp.concatenate(gather_rows(mod_own), 1)
-
-        def gather_weight(pair, stream):
-            px = x_swap(pair)
-            if n_dp == 2:
-                py = y_swap(pair)
-                pd = x_swap(py) if stream == 0 else y_swap(px)
-                return by(d, by(xc, pair, px, 1), by(xc, py, pd, 1), 1)
-            return lax.all_gather(by(xc, pair, px, 1), "dp", axis=1, tiled=True)
-
-        full = [gather_weight(pairs[i], i // 4) for i in range(8)]
-        full = [w if w.shape[0] > 1 else w[0] for w in full]
-
-        def reduce_half(keep, send):
-            return (keep.astype(F32) + core_swap(send).astype(F32)).astype(BF)
-
-        def reduce_full(keep, send):
-            mine = reduce_half(keep, send)
-            mine = (mine.astype(F32) + z_swap(mine).astype(F32)).astype(BF)
-            return mine, core_swap(mine)
-
-        def reduce_own(keep, send):
-            mine = reduce_half(keep, send)
+        def gather_one(a):
+            if n_dp != 2:
+                return (lax.all_gather(by(xc, a, over_x(a), 1), "dp", axis=1, tiled=True),)
+            return a, over_x(a), over_y(a)
+
+        def corner(parts, stream):
+            if len(parts) == 1:
+                return parts
+            a, px, py = parts
+            return a, px, py, (over_x(py) if stream == 0 else over_y(px))
+
+        def assemble(parts, need=()):
+            if len(parts) > 1:
+                return step(lambda a, *rest: lay_quads(ids, (a,) + rest), *parts, need=need)
+            return parts[0]
+
+        def flat(w):
+            return w if w.shape[0] > 1 else w[0]
+
+        def z_pair(own):
+            got = over_z(own)
+            return lambda need=(): with_core(step(lambda a, b: by(zl, a, b, 1), own, got, need=need))
+
+        def with_core(pair):
+            return pair, send(core_swap, pair)
+
+        def half_sum(keep, give, need=()):
+            got = send(core_swap, give)
+            return step(lambda a, b: (a.astype(F32) + b.astype(F32)).astype(BF), keep, got, need=need)
+
+        def half_start(keep, give):
+            got = send(core_swap, give)
+            return lambda: step(lambda a, b: (a.astype(F32) + b.astype(F32)).astype(BF), keep, got)
+
+        def full_sum(mine, got, need=()):
+            return with_core(step(lambda a, b: (a.astype(F32) + b.astype(F32)).astype(BF), mine, got, need=need))
+
+        def own_part(mine):
             away = lax.dynamic_slice_in_dim(mine, (1 - zl) * local, local, 1)
             here = lax.dynamic_slice_in_dim(mine, zl * local, local, 1)
-            return (here.astype(F32) + z_swap(away).astype(F32)).astype(BF).astype(F32)
+            return here, over_z(away)
+
+        def own_sum(here, got):
+            return (here.astype(F32) + got.astype(F32)).astype(BF).astype(F32)
 
         def column_sums(a):
             return jnp.stack([jnp.sum(a[:image_len], 0), jnp.sum(a[image_len:], 0)])
@@ -724,92 +868,423 @@
                 0,
             )
 
-        results, grads_x, modgrads, saved = [], [], [], []
-        xs = [gather_rows(a) for a in x_own]
-        cs = [gather_rows(a) for a in c_own]
-        for s in range(slots):
-            places = (image_len, s * 6, (slots + s) * 6)
-            live = (s * n_dp + d < count).astype(F32)
-            live_ref = live.reshape(1)
-            h1, qkv, n1o, inv1 = ln_qkv(ids, *xs[s], mod_full, full[0], full[4], *places)
-            mixed, lse = attend(qkv, length, image_len)
-            att = reduce_full(*out_project(ids, mixed, full[1], full[5], image_len))
-            h2, gbranch, after_own = mid_prepare(ids, live_ref, *xs[s], *att, *cs[s], mod_full, *places)
-            act, ginner, bk, bs, gk, gs = mlp(ids, h2, gbranch, full[2], full[6], full[3], full[7], image_len)
-            gh2 = reduce_full(gk, gs)
-            gatt, gmixed, gafter_own, sums = back_prepare(
-                ids, live_ref, *xs[s], *att, *cs[s], *gh2, mod_full, full[1], full[5], *places
+        places = [(image_len, s * 6, (slots + s) * 6) for s in range(slots)]
+
+        def first_part(s, need=()):
+            return step(lambda a, b: ln_qkv(ids, a, b, mod_full, *wq, *places[s]), *xs[s], need=need)
+
+        def mixing(s, need=()):
+            return step(lambda a: attend(a, length, image_len), firsts[s][1], need=need)
+
+        def projection(s, need=()):
+            keep, give = step(lambda a: out_project(ids, a, *wo, image_len), lses[s][0], need=need)
+            mine = half_sum(keep, give)
+            return mine, over_z(mine)
+
+        def middle(s, need=()):
+            return step(
+                lambda a, b: mid_prepare(ids, lives[s].reshape(1), a, b, *atts[s], *cs[s], mod_full, *places[s]),
+                *xs[s],
+                need=need,
             )
-            gqkv = attend_back(qkv, gmixed, lse, length, image_len)
-            branch = reduce_own(bk, bs)
-            gh1 = reduce_own(*input_partial(ids, gqkv, full[0], full[4], image_len))
-            q = gh1 * (1.0 + per_row(1, s))
-            total = jnp.stack([jnp.sum(q, 1), jnp.sum(q * n1o, 1)])
-            total = total + z_swap(total)
-            total = (total + core_swap(total)) / width
-            gx = gafter_own + inv1[:, :1] * (q - total[0][:, None] - n1o * total[1][:, None])
-            res = after_own + per_row(5, s) * branch
-            results.append(turn(res.astype(BF)))
-            grads_x.append(turn(gx.astype(BF)))
-            sums = jnp.sum(sums.reshape(2, 3, 8, local), 2)
-            modgrads.append(
-                jnp.stack(
-                    [
-                        column_sums(gh1), column_sums(gh1 * n1o), sums[:, 2], sums[:, 0], sums[:, 1],
-                        column_sums(c_own[s].astype(F32) * live * branch),
-                    ]
+
+        def dense(s):
+            return step(lambda a, b: mlp(ids, a, b, *w1, *w2, image_len), mids[s][0], mids[s][1])
+
+        def text_of(arrays):
+            return jnp.concatenate([a[..., image_len:, :] for a in arrays], arrays[0].ndim - 2)
+
+        lead_states = [lead_form(a) for a in states]
+        mine = step(lambda a, b: cast_states((a, b)), lead_states[0], lead_states[4])
+        got = send(core_swap, mine)
+        rest_order = (1, 5, 2, 6, 7, 3)
+        rest = step(lambda *a: cast_states(a), *(lead_states[i] for i in rest_order))
+        rows_of = [a.shape[2] for a in lead_states]
+        pairs = dict(zip((0, 4), step(lambda a, b: pair_pieces(ids, a, b, [[(3, rows_of[0])]] * 2), mine, got)))
+        pairs = {i: turned(a) for i, a in pairs.items()}
+        rest_got = send(core_swap, rest)
+        mod_own = turned(mod_join((image_modulation, text_modulation, group_counts)))
+        x_own = [turned(join((image_tokens[0, 0], text_tokens[0, 0])))]
+        count = mod_own[slots * 12, 0]
+        lives = [(s * n_dp + d < count).astype(F32) for s in range(slots)]
+        pieces = step(
+            lambda a, b: pair_pieces(
+                ids, a, b, [[(1, rows_of[1])] * 2] + [[(1, rows_of[i])] for i in (2, 6, 7, 3)]
+            ),
+            rest, rest_got,
+        )
+        pieces = dict(zip((1, 2, 6, 7, 3), pieces))
+        x_in = [join((image_tokens[0, s], text_tokens[0, s])) for s in range(slots)]
+        c_in = [join((image_cotan[0, s], text_cotan[0, s])) for s in range(slots)]
+        sync(pairs[0])
+        quads = [gather_one(pairs[0])]
+        sync(pairs[4], quads[0])
+        quads.append(gather_one(pairs[4]))
+        pairs[1] = turned(pieces[1])
+        sync(quads[1], mod_own, x_own[0])
+        ready = z_pair(x_own[0])
+        mod_ready = z_pair(mod_own)
+        quads = [corner(a, s) for s, a in enumerate(quads)]
+        mod_pair = mod_ready()
+        sync(quads)
+        xs = [ready()]
+        pairs[2] = turned(pieces[2])
+        wq = [assemble(a) for a in quads]
+        mod_full = jnp.concatenate(mod_pair, 1)
+        sync(pairs[1])
+        if n_dp == 2:
+            outs = gather_one(pairs[1])
+        firsts = [first_part(0)]
+        sync(outs if n_dp == 2 else (), pairs[2])
+        if n_dp == 2:
+            outs = [corner(tuple(a[s : s + 1] for a in outs), s) for s in range(2)]
+        else:
+            outs = [gather_one(pairs[1][s : s + 1]) for s in range(2)]
+        expand = [gather_one(pairs[2])]
+        x_own += [turned(a) for a in x_in[1:]]
+        lses = [mixing(0)]
+        sync(outs, x_own, expand[0])
+        wo = [flat(assemble(a)) for a in outs]
+        pairs[6] = turned(pieces[6])
+        ready = [z_pair(x_own[s]) for s in range(1, slots)]
+        keep, give = step(lambda a: out_project(ids, a, *wo, image_len), lses[0][0])
+        half = half_start(keep, give)
+        sync(ready and x_own)
+        xs += [a() for a in ready]
+        mine = half()
+        sums = [(mine, over_z(mine))]
+        sync(pairs[6])
+        expand.append(gather_one(pairs[6]))
+        pairs[7] = turned(pieces[7])
+        atts, mids, mlps, c_own, cots = [], [], [], [], []
+        for s in range(1, slots):
+            firsts.append(first_part(s))
+            if s == 1:
+                sync(expand[1], pairs[7])
+                expand = [corner(a, e) for e, a in enumerate(expand)]
+                reduce = [None, gather_one(pairs[7])]
+                pairs[3] = turned(pieces[3])
+            lses.append(mixing(s))
+            sync(sums[s - 1], pairs[3], reduce[1], expand)
+            atts.append(full_sum(*sums[s - 1]))
+            if s == 1:
+                c_own.append(turned(c_in[0]))
+                w1 = [flat(assemble(a)) for a in expand]
+                reduce[0] = gather_one(pairs[3])
+                c_own += [turned(a) for a in c_in[1:]]
+            keep, give = step(lambda a: out_project(ids, a, *wo, image_len), lses[s][0])
+            mine = half_sum(keep, give)
+            if s == 1:
+                sync(c_own[0])
+                cots = [z_pair(c_own[0])]
+            sums.append((mine, over_z(mine)))
+        sync(reduce[0])
+        reduce = [corner(a, s) for s, a in enumerate(reduce)]
+        cs = [cots[0]()]
+        cots += [z_pair(c_own[s]) for s in range(1, slots)]
+        mids.append(middle(0))
+        sync(reduce)
+        w2 = [flat(assemble(a)) for a in reduce]
+
+        lefts_text, rights_text = {}, {}
+
+        def text_left(k):
+            def halves(a):
+                part = a.shape[1] // 2
+                return (
+                    lax.dynamic_slice_in_dim(a, d * part, part, 1),
+                    lax.dynamic_slice_in_dim(a, (1 - d) * part, part, 1),
+                )
+
+            mine, away = step(halves, lefts_text[k])
+            return mine, over_y(away)
+
+        def text_right(k):
+            return rights_text[k], over_y(rights_text[k])
+
+        def text_grad(k):
+            def product(left, left_got, right, right_got):
+                left = jnp.concatenate([left, left_got], 0)
+                right = jnp.concatenate([right, right_got], right.ndim - 2)
+                if right.ndim == 3:
+                    return jnp.einsum("td,ctf->cdf", left, right, preferred_element_type=F32).astype(BF)
+                return mm(left, right, TN).astype(BF)[None]
+
+            return turned(step(product, *text_lefts[k], *text_rights[k]))
+
+        def give_half(k, stream=0):
+            left, right, height = ((lefts, rights, image_len), (lefts_text, rights_text, slots * text_rows))[stream]
+            left, right = (a[k] if isinstance(a[k], list) else [a[k]] for a in (left, right))
+            return over_y(step(lambda a: weight_grad(ids, 4, a, right, height), left))
+
+        def keep_half(k, got, stream=0, need=()):
+            left, right, height = ((lefts, rights, image_len), (lefts_text, rights_text, slots * text_rows))[stream]
+            left, right = (a[k] if isinstance(a[k], list) else [a[k]] for a in (left, right))
+            return turned(step(lambda a: weight_grad(ids, 3, a, right, height, got), left, need=need))
+
+        def whole_grads(k):
+            def one(left, right):
+                if right.ndim == 3:
+                    return jnp.einsum("td,ctf->cdf", left, right, preferred_element_type=F32)
+                return mm(left, right, TN)[None]
+
+            image = sum(one(a[:image_len], b[..., :image_len, :]) for a, b in zip(lefts[k], rights[k]))
+            text = one(lefts_text[k], rights_text[k])
+            return [
+                turn(lax.psum_scatter(a.astype(BF), "dp", scatter_dimension=1, tiled=True)) for a in (image, text)
+            ]
+
+        two_way = n_dp == 2
+        sent, text_lefts, text_rights, grads = {}, {}, {}, {}
+        lefts, rights, backs, gqkvs, gh1_mine, branch_mine = {}, {}, [], [], [], []
+
+        def backward(s, need=()):
+            backs.append(
+                step(
+                    lambda a, b: back_prepare(
+                        ids, lives[s].reshape(1), a, b, *atts[s], *cs[s], *gh2s[s], mod_full, *wo, *places[s]
+                    ),
+                    *xs[s],
+                    need=need,
                 )
             )
-            saved.append(((h1, gqkv), (mixed, gatt), (h2, ginner), (act, gbranch)))
+
+        def unmix(s, need=()):
+            gqkvs.append(
+                step(
+                    lambda a, b: attend_back(a, b, lses[s][1], length, image_len),
+                    firsts[s][1], backs[s][1],
+                    need=need,
+                )
+            )
+
+        def to_input(s, need=()):
+            out = step(lambda a: input_partial(ids, a, *wq, image_len), gqkvs[s], need=need)
+            gh1_mine.append(own_part(half_sum(*out)))
+
+        def to_branch(s):
+            branch_mine.append(own_part(half_sum(mlps[s][2], mlps[s][3])))
+
+        results, grads_x, modgrads, gates = [], [], [], []
+
+        def row_results(s):
+            def first(here, got):
+                branch = own_sum(here, got)
+                res = (mids[s][2] + per_row(5, s) * branch).astype(BF)
+                return res, column_sums(c_own[s].astype(F32) * lives[s] * branch)
+
+            res, gate = step(first, *branch_mine[s])
+            results.append(turned(res))
+            gates.append(gate)
+
+        def row_sums(s):
+            _, _, n1o, _ = firsts[s]
+
+            def first(here, got):
+                gh1 = own_sum(here, got)
+                q = gh1 * (1.0 + per_row(1, s))
+                total = jnp.stack([jnp.sum(q, 1), jnp.sum(q * n1o, 1)])
+                sums = jnp.sum(backs[s][3].reshape(2, 3, 8, local), 2)
+                mods = jnp.stack(
+                    [column_sums(gh1), column_sums(gh1 * n1o), sums[:, 2], sums[:, 0], sums[:, 1], gates[s]]
+                )
+                return total, mods
+
+            total, mods = step(first, *gh1_mine[s])
+            modgrads.append(mods)
+            return total, over_z(total)
+
+        def row_total(total, got):
+            total = step(jnp.add, total, got)
+            return total, send(core_swap, total)
+
+        def row_grads(s, total, got):
+            _, _, n1o, inv1 = firsts[s]
+
+            def second(total, got, here, away):
+                total = (total + got) / width
+                q = own_sum(here, away) * (1.0 + per_row(1, s))
+                gx = backs[s][2] + inv1[:, :1] * (q - total[0][:, None] - n1o * total[1][:, None])
+                return gx.astype(BF)
+
+            grads_x.append(turned(step(second, total, got, *gh1_mine[s])))
+
+        fresh, outer, waiting = [None] * 8, [None] * 8, {}
+        inv_count = (1.0 / group_counts[0].astype(F32)).reshape(1)
+
+        updates = {}
+
+        def optimize(idx):
+            moment = lead_form(moments[idx][0])
+            lead, rows, cols = moment.shape[1:]
+            piece = rows // n_group
+            new, keep, give = step(
+                lambda grad: adam(ids, inv_count, moment.reshape(2, lead, n_group, piece, cols), grad),
+                grads[idx].reshape(lead, n_group, piece, cols),
+            )
+            updates[idx] = keep, send(core_swap, give)
+            new = new.reshape(2, lead, rows, cols)
+            fresh[idx] = new.transpose(0, 2, 1, 3)[None] if moments[idx].ndim == 5 else new[:, 0][None]
+
+        def finish(idx):
+            keep, got = updates[idx]
+            out = step(
+                lambda a: outer_step(ids, lead_form(states[idx]), keep, got, a, n_group), waiting[idx]
+            )
+            outer[idx] = out.transpose(0, 2, 1, 3) if moments[idx].ndim == 5 else out[:, 0]
+
+        def fill_dense():
+            lefts.update({3: [a[0] for a in mlps], 2: [a[0] for a in mids], 1: [a[0] for a in lses], 0: [a[0] for a in firsts]})
+            rights.update({3: [a[1] for a in mids], 2: [a[1] for a in mlps]})
+
+        def fill_mixing():
+            rights[1] = [a[0] for a in backs]
+            rights[0] = gqkvs
+            lefts_text[0] = step(text_of, lefts[0])
+            rights_text[0] = step(text_of, gqkvs)
+            lefts_text[1] = step(text_of, [a[0] for a in lses])
+            rights_text[1] = step(text_of, rights[1])
+
+        def fill_text(k):
+            lefts_text[k] = step(text_of, lefts[k])
+            rights_text[k] = step(text_of, rights[k])
+
+        mlps.append(dense(0))
+        sync(sums[-1], cots and c_own)
+        gh_sums = []
+
+        def gh_half(s):
+            mine = half_sum(mlps[s][4], mlps[s][5])
+            gh_sums.append((mine, over_z(mine)))
+
+        def small_sum(idx):
+            keep, got = updates[idx]
+            pick = lambda a: lax.dynamic_index_in_dim(a, 1 - xc, 0, False)
+            far = over_x(
+                step(lambda a, b: (pick(a).astype(F32) + pick(b).astype(F32)).astype(BF), keep, got)
+            )
+            waiting[idx] = far
+
+        if two_way and slots == 2:
+            gh, br = half_start(mlps[0][4], mlps[0][5]), half_start(mlps[0][2], mlps[0][3])
+            atts.append(full_sum(*sums[1]))
+            mine = gh()
+            gh_sums.append((mine, over_z(mine)))
+            cs.append(cots[1]())
+            branch_mine.append(own_part(br()))
+            mids.append(middle(1))
+            mlps.append(dense(1))
+            sync(gh_sums[0], branch_mine[0])
+            gh, br = half_start(mlps[1][4], mlps[1][5]), half_start(mlps[1][2], mlps[1][3])
+            gh2s = [full_sum(*gh_sums[0])]
+            fill_dense()
+            fill_text(3)
+            text_lefts[3] = text_left(3)
+            text_rights[3] = text_right(3)
+            mine = gh()
+            gh_sums.append((mine, over_z(mine)))
+            row_results(0)
+            branch_half = br()
+            backward(0)
+            sync(text_lefts[3], text_rights[3], results[0])
+            fill_text(2)
+            text_rights[2] = text_right(2)
+            text_lefts[2] = text_left(2)
+            grads[7] = text_grad(3)
+            sent[3] = give_half(3)
+            sync(gh_sums[1], text_rights[2])
+            gh2s.append(full_sum(*gh_sums[1]))
+            branch_mine.append(own_part(branch_half))
+            sent[2] = give_half(2)
+            unmix(0)
+            sync(text_lefts[2], grads[7], branch_mine[1])
+            grads[6] = text_grad(2)
+            row_results(1)
+            out = step(lambda a: input_partial(ids, a, *wq, image_len), gqkvs[0])
+            half = half_start(*out)
+            optimize(7)
+            gh1_mine.append(own_part(half()))
+            small_sum(7)
+            sync(sent[3])
+            grads[3] = keep_half(3, sent[3])
+            backward(1)
+            sync(gh1_mine[0], waiting[7], grads[6])
+            totals = [row_sums(0)]
+            finish(7)
+            totals[0] = row_total(*totals[0])
+            unmix(1)
+            sync(sent[2], results[1])
+            grads[2] = keep_half(2, sent[2])
+            row_grads(0, *totals[0])
+            out = step(lambda a: input_partial(ids, a, *wq, image_len), gqkvs[1])
+            half = half_start(*out)
+            optimize(6)
+            gh1_mine.append(own_part(half()))
+            small_sum(6)
+            fill_mixing()
+            text_lefts[0] = text_left(0)
+            text_rights[0] = text_right(0)
+            sent[0] = give_half(0)
+            sync(grads[3], waiting[6], gh1_mine[1])
+            optimize(3)
+            sent[5] = give_half(1, 1)
+            sent[1] = give_half(1)
+            small_sum(3)
+            totals.append(row_sums(1))
+            finish(6)
+            totals[1] = row_total(*totals[1])
+            sync(text_lefts[0], text_rights[0])
+            grads[4] = text_grad(0)
+            sync(grads[2], waiting[3])
+            optimize(2)
+            finish(3)
+            row_grads(1, *totals[1])
+            small_sum(2)
+            sync(sent[0])
+            grads[0] = keep_half(0, sent[0])
+            sync(sent[5], sent[1])
+            grads[5] = keep_half(1, sent[5], 1)
+            grads[1] = keep_half(1, sent[1])
+            finish(2)
+            sync(grads[4])
+            optimize(4)
+            sync(grads[0])
+            optimize(0)
+            small_sum(4)
+            small_sum(0)
+            optimize(5)
+            optimize(1)
+            small_sum(5)
+            small_sum(1)
+            for i in (4, 0, 5, 1):
+                finish(i)
+        else:
+            for s in range(1, slots):
+                atts.append(full_sum(*sums[s]))
+                cs.append(cots[s]())
+                mids.append(middle(s))
+                mlps.append(dense(s))
+            fill_dense()
+            for s in range(slots):
+                gh_half(s)
+            gh2s = [full_sum(*a) for a in gh_sums]
+            for s in range(slots):
+                backward(s)
+                unmix(s)
+                to_input(s)
+                to_branch(s)
+                row_results(s)
+                row_grads(s, *row_total(*row_sums(s)))
+            fill_mixing()
+            fill_text(2)
+            fill_text(3)
+            for k in (3, 2, 1, 0):
+                grads[k], grads[k + 4] = whole_grads(k)
+            for i in range(8):
+                optimize(i)
+                small_sum(i)
+                finish(i)
         mod_back = turn(jnp.stack(modgrads).reshape(slots * 12, local)).reshape(slots, 6, 2, local)
-
-        fresh, outer = [None] * 8, [None] * 8
-        inv_count = (1.0 / group_counts[0].astype(F32)).reshape(1)
-        for k in (3, 2, 1, 0):
-            for stream in range(2):
-                idx = k + 4 * stream
-                lo, hi = (0, image_len) if stream == 0 else (image_len, rows_all)
-
-                def weight_grad(start, size):
-                    total = 0.0
-                    for s in range(slots):
-                        left, right = saved[s][k]
-                        left = lax.dynamic_slice_in_dim(left[lo:hi], start, size, 1)
-                        if k == 0:
-                            part = jnp.einsum("td,ctf->cdf", left, right[:, lo:hi], preferred_element_type=F32)
-                        else:
-                            part = mm(left, right[lo:hi], TN)[None]
-                        total = total + part
-                    return total
-
-                rows = saved[0][k][0].shape[1]
-                if n_dp == 2:
-                    part = rows // 2
-                    got = y_swap(weight_grad((1 - d) * part, part).astype(BF))
-                    shard = (weight_grad(d * part, part) + got.astype(F32)).astype(BF)
-                else:
-                    shard = lax.psum_scatter(
-                        weight_grad(0, rows).astype(BF), "dp", scatter_dimension=1, tiled=True
-                    )
-                grad = turn(shard)
-                moment = lead_form(moments[idx][0])
-                lead, rows, cols = moment.shape[1:]
-                piece = rows // n_group
-                new, keep, send = adam(
-                    ids, inv_count, moment.reshape(2, lead, n_group, piece, cols),
-                    grad.reshape(lead, n_group, piece, cols),
-                )
-                got = core_swap(send)
-                pick = lambda a: lax.dynamic_index_in_dim(a, 1 - xc, 0, False)
-                far = x_swap((pick(keep).astype(F32) + pick(got).astype(F32)).astype(BF))
-                out = outer_step(ids, lead_form(states[idx]), keep, got, far, n_group)
-                new = new.reshape(2, lead, rows, cols)
-                if moments[idx].ndim == 5:
-                    fresh[idx] = new.transpose(0, 2, 1, 3)[None]
-                    outer[idx] = out.transpose(0, 2, 1, 3)
-                else:
-                    fresh[idx] = new[:, 0][None]
-                    outer[idx] = out[:, 0]
 
         res = jnp.stack(results)
         gx = jnp.stack(grads_x)

time: 1450 us -> 1260 us (0.87)
  waiting for transfers between devices: 336 us -> 183 us
  Pallas kernels: 445 us -> 549 us
  matrix products: 92.9 us -> 13.9 us
  other arithmetic: 116 us -> 74.9 us
    ppermute x20 -> x22, waiting for transfers between devices: 171 us -> 32.8 us  [y_swap(): return lax.ppermute(a, 'dp', y_perm)]
    pallas_call x0 -> x22, Pallas kernels: none -> 117 us  [the longest x10 83.1 us: weight_grad(): call(kernel, (steps,), [left_spec] * n + [right_spec] * n + [out_spec] *...]
    dot_general x24 -> x2, matrix products: 66.6 us -> 9.56 us  [mm(): return lax.dot_general(a, b, dims, preferred_element_type=F32)]
    select_n x35 -> x5, other arithmetic: 57.5 us -> 8.14 us  [by(): jnp.where(flag == 0, jnp.concatenate([a, b], axis), jnp.concatenate([b, a...]
    ppermute x35 -> x29, starting transfers between devices: 128 us -> 87.8 us  [core_swap(): return lax.ppermute(a, 'group', core_perm)]
    ppermute x26 -> x25, starting transfers between devices: 158 us -> 197 us  [turn(): return lax.ppermute(a, ('group', 'mp'), turn_perm)]
    dot_general x8 -> x1, matrix products: 26.3 us -> 4.31 us  [product(): jnp.einsum('td,ctf->cdf', left, right, preferred_element_type=F32)]
    ppermute x20 -> x19, waiting for transfers between devices: 61.4 us -> 40.5 us  [x_swap(): return lax.ppermute(a, 'group', x_perm)]
  transfers between devices with their start and end apart: 116 -> 110, of which waited for: 28 -> 23; matrix products, arithmetic and copies ran while one was open for 19% -> 9% of each run, Pallas kernels for 31% -> 39%
where the time goes in v2:
time: 1260 us; the launch traced here: 1240 us
  Pallas kernels  549 us (44%)
  starting transfers between devices  343 us (27%)
  waiting for transfers between devices  183 us (15%)
  other arithmetic  74.9 us (6%)
  local copies, waits for them, and re-layouts  67.3 us (5%)
  matrix products  13.9 us (1%)
    ppermute x25, starting transfers between devices, turn(): return lax.ppermute(a, ('group', 'mp'), turn_perm)  197 us
    ppermute x15, waiting for transfers between devices, z_swap(): return lax.ppermute(a, 'mp', z_perm)  108 us
    ppermute x29, starting transfers between devices, core_swap(): return lax.ppermute(a, 'group', core_perm)  87.8 us
    pallas_call x10, Pallas kernels, weight_grad(): call(kernel, (steps,), [left_spec] * n + [right_spec] * n + [out_spec] *...  83.1 us
    pallas_call x2, Pallas kernels, mlp(): call(kernel, (steps,), [whole((rows, width)), whole((rows, width)), w1_sp...  81.1 us
    pallas_call x8, Pallas kernels, adam(): call(kernel, (lead, 4), [pairs, pl.BlockSpec((1, 1, piece, cols), lambda...  80.6 us
    pallas_call x2, Pallas kernels, attend_back(): pl.pallas_call(kernel, grid=(pairs,), in_specs=[pl.BlockSpec((3, rows, 12...  66.1 us
    pallas_call x2, Pallas kernels, attend(): pl.pallas_call(kernel, grid=(pairs,), in_specs=[pl.BlockSpec((3, rows, 12...  44.4 us
  transfers between devices with their start and end apart: 110, of which 23 were waited for; matrix products, arithmetic and copies ran while one was open for 9% of the time, Pallas kernels for 39%

profile of v2, /device:TPU:0, one launch (start us, length us, event | category | flops | bytes accessed | tf_op | source)
XLA Modules:
  0.0 1237.0 jit_solution(5698477584155427967)
XLA Ops:
  44.3 12.9 %collective-permute-done.8.refs_1_ = bf16[3,384,384]{2,1,0:T(8,128)(2,1)} collective-permute-done((bf16[3,384,384]{2,1,0:T(8,128)(2,1)S(1)}, bf16[3,384,384]{2,1,0:T(8,128)(2,1)}, u32[]{:S(2)}, u32[]{:S(2)}) %collective-permute-start.8) | collective-permute-done | bytes 884768 | tf_op jit(solution)/shard_map/ppermute | solution.py:740
  62.2 19.6 %collective-permute-done.10 = f32[32,384]{1,0:T(8,128)S(1)} collective-permute-done((f32[32,384]{1,0:T(8,128)S(1)}, f32[32,384]{1,0:T(8,128)S(1)}, u32[]{:S(2)}, u32[]{:S(2)}) %collective-permute-start.10) | collective-permute-done | bytes 49184 | tf_op jit(solution)/shard_map/ppermute | solution.py:743
  84.5 15.4 %collective-permute-start.15 = (bf16[1184,768]{1,0:T(8,128)(2,1)S(1)}, bf16[1184,768]{1,0:T(8,128)(2,1)}, u32[]{:S(2)}, u32[]{:S(2)}) collective-permute-start(bf16[1184,768]{1,0:T(8,128)(2,1)S(1)} %maximum_select_fusion.xm_ref), channel_id=1, source_target_pairs={{0,8},{8,0},{16,24},{24,16},{1,9},{9,1},{17,25},{25,17},{2,10},{10... | collective-permute-start | bytes 5455880 | tf_op jit(solution)/shard_map/ppermute | solution.py:737
  119.3 15.2 %shard_map.396 = (bf16[1184,1536]{1,0:T(8,128)(2,1)}, bf16[3,1184,384]{2,1,0:T(8,128)(2,1)}, f32[1184,384]{1,0:T(8,128)}, f32[1184,128]{1,0:T(8,128)}) custom-call(s32[9]{0:T(128)} %stack.162.ids_ref, bf16[1184,768]{1,0:T(8,128)(2,1)} %copy-done.19, bf16[1184,768]{1,0:T(8,128)(2,1)} %collective-permute-done.15.xo_ref, ...), custom_call_target="tpu_custom_call" | custom-call | flops 1047527424 | bytes 4497408 | tf_op jit(solution)/shard_map/pallas_call | solution.py:191
  150.3 22.2 %shard_map.397 = (bf16[1184,384]{1,0:T(8,128)(2,1)}, f32[3,8,1280]{2,1,0:T(8,128)}) custom-call(bf16[3,1184,384]{2,1,0:T(8,128)(2,1)} %get-tuple-element.459.qkv_ref), custom_call_target="tpu_custom_call" | custom-call | flops 2153250816 | bytes 909312 | tf_op jit(solution)/shard_map/pallas_call | solution.py:248
  210.9 22.7 %collective-permute-done.25 = bf16[1184,384]{1,0:T(8,128)(2,1)S(1)} collective-permute-done((bf16[1184,384]{1,0:T(8,128)(2,1)}, bf16[1184,384]{1,0:T(8,128)(2,1)S(1)}, u32[]{:S(2)}, u32[]{:S(2)}) %collective-permute-start.25) | collective-permute-done | bytes 909344 | tf_op jit(solution)/shard_map/ppermute | solution.py:743
  241.3 15.2 %shard_map.401 = (bf16[1184,1536]{1,0:T(8,128)(2,1)}, bf16[3,1184,384]{2,1,0:T(8,128)(2,1)}, f32[1184,384]{1,0:T(8,128)}, f32[1184,128]{1,0:T(8,128)}) custom-call(s32[9]{0:T(128)} %stack.162.ids_ref, bf16[1184,768]{1,0:T(8,128)(2,1)} %copy-done.18, bf16[1184,768]{1,0:T(8,128)(2,1)} %collective-permute-done.28.xo_ref, ...), custom_call_target="tpu_custom_call" | custom-call | flops 1047527424 | bytes 4497408 | tf_op jit(solution)/shard_map/pallas_call | solution.py:191
  271.7 20.8 %collective-permute-done.32 = bf16[1184,768]{1,0:T(8,128)(2,1)} collective-permute-done((bf16[1184,768]{1,0:T(8,128)(2,1)}, bf16[1184,768]{1,0:T(8,128)(2,1)}, u32[]{:S(2)}, u32[]{:S(2)}) %collective-permute-start.32) | collective-permute-done | bytes 1818656 | tf_op jit(solution)/shard_map/ppermute | solution.py:743
  302.9 22.2 %shard_map.402 = (bf16[1184,384]{1,0:T(8,128)(2,1)}, f32[3,8,1280]{2,1,0:T(8,128)}) custom-call(bf16[3,1184,384]{2,1,0:T(8,128)(2,1)} %get-tuple-element.495.qkv_ref), custom_call_target="tpu_custom_call" | custom-call | flops 2153250816 | bytes 909312 | tf_op jit(solution)/shard_map/pallas_call | solution.py:248
  352.9 20.3 %collective-permute-start.43 = (bf16[1184,768]{1,0:T(8,128)(2,1)S(1)}, bf16[1184,768]{1,0:T(8,128)(2,1)S(1)}, u32[]{:S(2)}, u32[]{:S(2)}) collective-permute-start(bf16[1184,768]{1,0:T(8,128)(2,1)S(1)} %copy-done.23), channel_id=1, source_target_pairs={{0,8},{8,0},{16,24},{24,16},{1,9},{9,1},{17,25},{25,17},{2,10},{10... | collective-permute-start | bytes 5455880 | tf_op jit(solution)/shard_map/ppermute | solution.py:737
  425.9 40.3 %shard_map.409 = (bf16[1184,1536]{1,0:T(8,128)(2,1)}, bf16[1184,1536]{1,0:T(8,128)(2,1)}, bf16[1184,768]{1,0:T(8,128)(2,1)}, bf16[1184,768]{1,0:T(8,128)(2,1)}, ...) custom-call(s32[9]{0:T(128)} %stack.162.ids_ref, bf16[1184,1536]{1,0:T(8,128)(2,1)} %get-tuple-element.499.h_ref.refs_0_, ...), custom_call_target="tpu_custom_call" | custom-call | flops 5586812928 | bytes 10174464 | tf_op jit(solution)/shard_map/pallas_call | solution.py:498
  474.3 14.8 %collective-permute-done.50 = bf16[1184,384]{1,0:T(8,128)(2,1)S(1)} collective-permute-done((bf16[1184,384]{1,0:T(8,128)(2,1)}, bf16[1184,384]{1,0:T(8,128)(2,1)S(1)}, u32[]{:S(2)}, u32[]{:S(2)}) %collective-permute-start.50) | collective-permute-done | bytes 909344 | tf_op jit(solution)/shard_map/ppermute | solution.py:743
  498.1 11.8 shard_map.410
  509.9 40.8 %shard_map.411 = (bf16[1184,1536]{1,0:T(8,128)(2,1)}, bf16[1184,1536]{1,0:T(8,128)(2,1)}, bf16[1184,768]{1,0:T(8,128)(2,1)}, bf16[1184,768]{1,0:T(8,128)(2,1)}, ...) custom-call(s32[9]{0:T(128)} %stack.162.ids_ref, bf16[1184,1536]{1,0:T(8,128)(2,1)} %get-tuple-element.500.h_ref.refs_1_, ...), custom_call_target="tpu_custom_call" | custom-call | flops 5586812928 | bytes 10174464 | tf_op jit(solution)/shard_map/pallas_call | solution.py:498
  581.5 15.4 %shard_map.412 = (bf16[1184,1536]{1,0:T(8,128)(2,1)}, bf16[1184,384]{1,0:T(8,128)(2,1)}, f32[1184,384]{1,0:T(8,128)}, f32[2,24,384]{2,1,0:T(8,128)}) custom-call(s32[9]{0:T(128)} %stack.162.ids_ref, f32[1]{0:T(128)} %bitcast.19.live_ref, bf16[1184,768]{1,0:T(8,128)(2,1)} %copy-done.19, bf16[1184,768]{1,0:T(8,128)(2,1)} %collective-permute-done.15.xo_ref, ...), custom_call_target="tpu_custom_call" | custom-call | flops 349175808 | bytes 5455872 | tf_op jit(solution)/shard_map/pallas_call | solution.py:570
  610.4 19.2 %collective-permute-start.65 = (bf16[1,768,1536]{2,1,0:T(8,128)(2,1)}, bf16[1,768,1536]{2,1,0:T(8,128)(2,1)}, u32[]{:S(2)}, u32[]{:S(2)}) collective-permute-start(bf16[1,768,1536]{2,1,0:T(8,128)(2,1)} %fusion), channel_id=1, source_target_pairs={{0,0},{1,1},{2,8},{3,9},{8,2},{9,3},{10,10},{11,11},{16,16},{17,17... | collective-permute-start | bytes 7077896 | tf_op jit(solution)/shard_map/ppermute | solution.py:749
  656.4 33.2 %shard_map.415.a_ref.refs_2_ = bf16[3,1184,384]{2,1,0:T(8,128)(2,1)} custom-call(bf16[3,1184,384]{2,1,0:T(8,128)(2,1)} %get-tuple-element.459.qkv_ref, bf16[1184,384]{1,0:T(8,128)(2,1)} %get-tuple-element.460.grad_ref, f32[3,8,1280]{2,1,0:T(8,128)} %get-tuple-element.461.lse_ref), custom_call_target="tpu_custom_call" | custom-call | flops 5383127040 | bytes 1591296 | tf_op jit(solution)/shard_map/pallas_call | solution.py:295
  699.0 11.9 shard_map.416
  711.8 19.2 %collective-permute-start.74 = (bf16[1,768,1536]{2,1,0:T(8,128)(2,1)}, bf16[1,768,1536]{2,1,0:T(8,128)(2,1)}, u32[]{:S(2)}, u32[]{:S(2)}) collective-permute-start(bf16[1,768,1536]{2,1,0:T(8,128)(2,1)} %fusion.1), channel_id=1, source_target_pairs={{0,0},{1,1},{2,8},{3,9},{8,2},{9,3},{10,10},{11,11},{16,16},{17,17... | collective-permute-start | bytes 7077896 | tf_op jit(solution)/shard_map/ppermute | solution.py:749
  748.3 16.6 %collective-permute-done.71.refs_4_ = bf16[1,768,1536]{2,1,0:T(8,128)(2,1)} collective-permute-done((bf16[1,768,1536]{2,1,0:T(8,128)(2,1)}, bf16[1,768,1536]{2,1,0:T(8,128)(2,1)}, u32[]{:S(2)}, u32[]{:S(2)}) %collective-permute-start.71) | collective-permute-done | bytes 2359328 | tf_op jit(solution)/shard_map/ppermute | solution.py:746
  784.6 15.2 %shard_map.419 = (bf16[1184,1536]{1,0:T(8,128)(2,1)}, bf16[1184,384]{1,0:T(8,128)(2,1)}, f32[1184,384]{1,0:T(8,128)}, f32[2,24,384]{2,1,0:T(8,128)}) custom-call(s32[9]{0:T(128)} %stack.162.ids_ref, f32[1]{0:T(128)} %bitcast.34.live_ref, bf16[1184,768]{1,0:T(8,128)(2,1)} %copy-done.18, bf16[1184,768]{1,0:T(8,128)(2,1)} %collective-permute-done.28.xo_ref, ...), custom_call_target="tpu_custom_call" | custom-call | flops 349175808 | bytes 5455872 | tf_op jit(solution)/shard_map/pallas_call | solution.py:570
  808.3 32.9 %shard_map.421.a_ref.refs_3_ = bf16[3,1184,384]{2,1,0:T(8,128)(2,1)} custom-call(bf16[3,1184,384]{2,1,0:T(8,128)(2,1)} %get-tuple-element.495.qkv_ref, bf16[1184,384]{1,0:T(8,128)(2,1)} %get-tuple-element.496.grad_ref, f32[3,8,1280]{2,1,0:T(8,128)} %get-tuple-element.497.lse_ref), custom_call_target="tpu_custom_call" | custom-call | flops 5383127040 | bytes 1591296 | tf_op jit(solution)/shard_map/pallas_call | solution.py:295
  855.2 12.3 shard_map.423
  879.3 19.3 %collective-permute-start.81 = (bf16[1,768,1536]{2,1,0:T(8,128)(2,1)}, bf16[1,768,1536]{2,1,0:T(8,128)(2,1)}, u32[]{:S(2)}, u32[]{:S(2)}) collective-permute-start(bf16[1,768,1536]{2,1,0:T(8,128)(2,1)} %shard_map.418), channel_id=1, source_target_pairs={{0,0},{1,1},{2,8},{3,9},{8,2},{9,3},{10,10},{11,11},{16,16},{17,17... | collective-permute-start | bytes 7077896 | tf_op jit(solution)/shard_map/ppermute | solution.py:749
  924.4 14.9 %collective-permute-done.80 = bf16[1184,384]{1,0:T(8,128)(2,1)S(1)} collective-permute-done((bf16[1184,384]{1,0:T(8,128)(2,1)S(1)}, bf16[1184,384]{1,0:T(8,128)(2,1)S(1)}, u32[]{:S(2)}, u32[]{:S(2)}) %collective-permute-start.80) | collective-permute-done | bytes 909344 | tf_op jit(solution)/shard_map/ppermute | solution.py:743
  952.2 19.1 %collective-permute-start.87 = (bf16[1,768,1536]{2,1,0:T(8,128)(2,1)}, bf16[1,768,1536]{2,1,0:T(8,128)(2,1)}, u32[]{:S(2)}, u32[]{:S(2)}) collective-permute-start(bf16[1,768,1536]{2,1,0:T(8,128)(2,1)} %shard_map.422), channel_id=1, source_target_pairs={{0,0},{1,1},{2,8},{3,9},{8,2},{9,3},{10,10},{11,11},{16,16},{17,17... | collective-permute-start | bytes 7077896 | tf_op jit(solution)/shard_map/ppermute | solution.py:749
  996.2 12.3 collective-permute-done.85
  1014.1 14.8 %collective-permute-start.96 = (bf16[3,768,384]{1,2,0:T(8,128)(2,1)}, bf16[3,768,384]{1,2,0:T(8,128)(2,1)}, u32[]{:S(2)}, u32[]{:S(2)}) collective-permute-start(bf16[3,768,384]{1,2,0:T(8,128)(2,1)} %convert_bitcast_fusion), channel_id=1, source_target_pairs={{0,0},{1,1},{2,8},{3,9},{8,2},{9,3},{10,10},{11,11},{16,16},{17,17... | collective-permute-start | bytes 5308424 | tf_op jit(solution)/shard_map/ppermute | solution.py:749
  1060.1 14.9 %collective-permute-start.95 = (bf16[3,768,384]{2,1,0:T(8,128)(2,1)}, bf16[3,768,384]{2,1,0:T(8,128)(2,1)}, u32[]{:S(2)}, u32[]{:S(2)}) collective-permute-start(bf16[3,768,384]{2,1,0:T(8,128)(2,1)} %shard_map.432), channel_id=1, source_target_pairs={{0,0},{1,1},{2,8},{3,9},{8,2},{9,3},{10,10},{11,11},{16,16},{17,17... | collective-permute-start | bytes 5308424 | tf_op jit(solution)/shard_map/ppermute | solution.py:749
  1113.9 12.7 %shard_map.436 = (f32[2,3,4,192,384]{4,3,2,1,0:T(8,128)}, bf16[2,3,192,384]{3,2,1,0:T(8,128)(2,1)}, bf16[2,3,192,384]{3,2,1,0:T(8,128)(2,1)}) custom-call(s32[9]{0:T(128)} %stack.162.ids_ref, f32[1]{0:T(128)} %bitcast.41.inv_ref, f32[2,3,4,192,384]{4,3,2,1,0:T(8,128)} %bitcast.184, bf16[3,4,192,384]{3,2,1,0:T(8,128)(2,1)} %bitcast.183), custom_call_target="tpu_custom_call" | custom-call | flops 4423680 | bytes 4423680 | tf_op jit(solution)/shard_map/pallas_call | solution.py:675
  1127.0 12.6 %shard_map.437 = (f32[2,3,4,192,384]{4,3,2,1,0:T(8,128)}, bf16[2,3,192,384]{3,2,1,0:T(8,128)(2,1)}, bf16[2,3,192,384]{3,2,1,0:T(8,128)(2,1)}) custom-call(s32[9]{0:T(128)} %stack.162.ids_ref, f32[1]{0:T(128)} %bitcast.41.inv_ref, f32[2,3,4,192,384]{4,3,2,1,0:T(8,128)} %bitcast.185, bf16[3,4,192,384]{3,2,1,0:T(8,128)(2,1)} %bitcast.75.g_ref), custom_call_target="tpu_custom_call" | custom-call | flops 4423680 | bytes 4423680 | tf_op jit(solution)/shard_map/pallas_call | solution.py:675
  1167.8 26.8 %collective-permute-start.106 = (bf16[2,1,48,1536]{3,2,1,0:T(8,128)(2,1)}, bf16[2,1,48,1536]{3,2,1,0:T(8,128)(2,1)S(1)}, u32[]{:S(2)}, u32[]{:S(2)}) collective-permute-start(bf16[2,1,48,1536]{3,2,1,0:T(8,128)(2,1)} %get-tuple-element.598), channel_id=1, source_target_pairs={{0,8},{8,0},{16,24},{24,16},{1,9},{9,1},{17,25},{25,17},{2,10},{10... | collective-permute-start | bytes 884744 | tf_op jit(solution)/shard_map/ppermute | solution.py:737
  (611 shorter events, 614.5 us)
Async XLA Ops:
  134.5 38.0 %collective-permute-start.23 = (bf16[1,384,1536]{2,1,0:T(8,128)(2,1)S(1)}, bf16[1,384,1536]{2,1,0:T(8,128)(2,1)S(1)}, u32[]{:S(2)}, u32[]{:S(2)}) collective-permute-start(bf16[1,384,1536]{2,1,0:T(8,128)(2,1)S(1)} %collective-permute-done.19.refs_0_), channel_id=1, source_target_pairs={{0,16},{8,24},{16,0},{24,8},{1,17},{9,25},{17,1},{25,9},{2,18},{10... | collective-permute-start | bytes 3538952 | tf_op jit(solution)/shard_map/ppermute | solution.py:740
  187.3 48.4 %collective-permute-start.26 = (bf16[1184,768]{1,0:T(8,128)(2,1)}, bf16[1184,768]{1,0:T(8,128)(2,1)S(1)}, u32[]{:S(2)}, u32[]{:S(2)}) collective-permute-start(bf16[1184,768]{1,0:T(8,128)(2,1)} %get-tuple-element.358), channel_id=1, source_target_pairs={{0,8},{8,0},{16,24},{24,16},{1,9},{9,1},{17,25},{25,17},{2,10},{10... | collective-permute-start | bytes 5455880 | tf_op jit(solution)/shard_map/ppermute | solution.py:737
  237.4 55.0 %collective-permute-start.32 = (bf16[1184,768]{1,0:T(8,128)(2,1)}, bf16[1184,768]{1,0:T(8,128)(2,1)}, u32[]{:S(2)}, u32[]{:S(2)}) collective-permute-start(bf16[1184,768]{1,0:T(8,128)(2,1)} %add_convert_fusion.11), channel_id=1, source_target_pairs={{0,1},{1,0},{2,3},{3,2},{4,5},{5,4},{6,7},{7,6},{8,9},{9,8},{10,11... | collective-permute-start | bytes 5455880 | tf_op jit(solution)/shard_map/ppermute | solution.py:743
  267.6 57.5 %collective-permute-start.34 = (bf16[1,384,1536]{2,1,0:T(8,128)(2,1)S(1)}, bf16[1,384,1536]{2,1,0:T(8,128)(2,1)}, u32[]{:S(2)}, u32[]{:S(2)}) collective-permute-start(bf16[1,384,1536]{2,1,0:T(8,128)(2,1)S(1)} %collective-permute-done.31.refs_0_), channel_id=1, source_target_pairs={{0,16},{8,24},{16,0},{24,8},{1,17},{9,25},{17,1},{25,9},{2,18},{10... | collective-permute-start | bytes 3538952 | tf_op jit(solution)/shard_map/ppermute | solution.py:740
  268.9 56.2 %collective-permute-start.35 = (bf16[1,384,1536]{2,1,0:T(8,128)(2,1)S(1)}, bf16[1,384,1536]{2,1,0:T(8,128)(2,1)}, u32[]{:S(2)}, u32[]{:S(2)}) collective-permute-start(bf16[1,384,1536]{2,1,0:T(8,128)(2,1)S(1)} %collective-permute-done.31.refs_0_), channel_id=1, source_target_pairs={{0,4},{4,0},{1,5},{5,1},{2,6},{6,2},{3,7},{7,3},{8,12},{12,8},{9,1... | collective-permute-start | bytes 3538952 | tf_op jit(solution)/shard_map/ppermute | solution.py:746
  270.1 55.0 %collective-permute-start.37 = (bf16[1,384,1536]{2,1,0:T(8,128)(2,1)}, bf16[1,384,1536]{2,1,0:T(8,128)(2,1)}, u32[]{:S(2)}, u32[]{:S(2)}) collective-permute-start(bf16[1,384,1536]{2,1,0:T(8,128)(2,1)} %collective-permute-done.29.refs_1_), channel_id=1, source_target_pairs={{0,4},{4,0},{1,5},{5,1},{2,6},{6,2},{3,7},{7,3},{8,12},{12,8},{9,1... | collective-permute-start | bytes 3538952 | tf_op jit(solution)/shard_map/ppermute | solution.py:746
  270.9 54.2 %collective-permute-start.36 = (bf16[1,384,1536]{2,1,0:T(8,128)(2,1)}, bf16[1,384,1536]{2,1,0:T(8,128)(2,1)}, u32[]{:S(2)}, u32[]{:S(2)}) collective-permute-start(bf16[1,384,1536]{2,1,0:T(8,128)(2,1)} %collective-permute-done.24.refs_2_), channel_id=1, source_target_pairs={{0,16},{8,24},{16,0},{24,8},{1,17},{9,25},{17,1},{25,9},{2,18},{10... | collective-permute-start | bytes 3538952 | tf_op jit(solution)/shard_map/ppermute | solution.py:740
  352.9 37.3 %collective-permute-start.43 = (bf16[1184,768]{1,0:T(8,128)(2,1)S(1)}, bf16[1184,768]{1,0:T(8,128)(2,1)S(1)}, u32[]{:S(2)}, u32[]{:S(2)}) collective-permute-start(bf16[1184,768]{1,0:T(8,128)(2,1)S(1)} %copy-done.23), channel_id=1, source_target_pairs={{0,8},{8,0},{16,24},{24,16},{1,9},{9,1},{17,25},{25,17},{2,10},{10... | collective-permute-start | bytes 5455880 | tf_op jit(solution)/shard_map/ppermute | solution.py:737
  386.9 79.3 %collective-permute-start.48 = (bf16[1184,768]{1,0:T(8,128)(2,1)}, bf16[1184,768]{1,0:T(8,128)(2,1)}, u32[]{:S(2)}, u32[]{:S(2)}) collective-permute-start(bf16[1184,768]{1,0:T(8,128)(2,1)} %add_convert_fusion.9), channel_id=1, source_target_pairs={{0,1},{1,0},{2,3},{3,2},{4,5},{5,4},{6,7},{7,6},{8,9},{9,8},{10,11... | collective-permute-start | bytes 5455880 | tf_op jit(solution)/shard_map/ppermute | solution.py:743
  391.4 74.9 %collective-permute-start.47 = (bf16[1184,384]{1,0:T(8,128)(2,1)}, bf16[1184,384]{1,0:T(8,128)(2,1)}, u32[]{:S(2)}, u32[]{:S(2)}) collective-permute-start(bf16[1184,384]{1,0:T(8,128)(2,1)} %fusion.60), channel_id=1, source_target_pairs={{0,0},{1,1},{2,8},{3,9},{8,2},{9,3},{10,10},{11,11},{16,16},{17,17... | collective-permute-start | bytes 2727944 | tf_op jit(solution)/shard_map/ppermute | solution.py:749
  491.3 61.8 %collective-permute-start.54 = (bf16[1184,768]{1,0:T(8,128)(2,1)}, bf16[1184,768]{1,0:T(8,128)(2,1)}, u32[]{:S(2)}, u32[]{:S(2)}) collective-permute-start(bf16[1184,768]{1,0:T(8,128)(2,1)} %add_convert_fusion.7), channel_id=1, source_target_pairs={{0,1},{1,0},{2,3},{3,2},{4,5},{5,4},{6,7},{7,6},{8,9},{9,8},{10,11... | collective-permute-start | bytes 5455880 | tf_op jit(solution)/shard_map/ppermute | solution.py:743
  496.9 56.1 %collective-permute-start.55 = (bf16[1184,384]{1,0:T(8,128)(2,1)}, bf16[1184,384]{1,0:T(8,128)(2,1)S(1)}, u32[]{:S(2)}, u32[]{:S(2)}) collective-permute-start(bf16[1184,384]{1,0:T(8,128)(2,1)} %get-tuple-element.422), channel_id=1, source_target_pairs={{0,1},{1,0},{2,3},{3,2},{4,5},{5,4},{6,7},{7,6},{8,9},{9,8},{10,11... | collective-permute-start | bytes 2727944 | tf_op jit(solution)/shard_map/ppermute | solution.py:743
  579.3 61.3 %collective-permute-start.62 = (bf16[1184,768]{1,0:T(8,128)(2,1)S(1)}, bf16[1184,768]{1,0:T(8,128)(2,1)}, u32[]{:S(2)}, u32[]{:S(2)}) collective-permute-start(bf16[1184,768]{1,0:T(8,128)(2,1)S(1)} %add_convert_fusion.4), channel_id=1, source_target_pairs={{0,1},{1,0},{2,3},{3,2},{4,5},{5,4},{6,7},{7,6},{8,9},{9,8},{10,11... | collective-permute-start | bytes 5455880 | tf_op jit(solution)/shard_map/ppermute | solution.py:743
  610.4 79.3 %collective-permute-start.65 = (bf16[1,768,1536]{2,1,0:T(8,128)(2,1)}, bf16[1,768,1536]{2,1,0:T(8,128)(2,1)}, u32[]{:S(2)}, u32[]{:S(2)}) collective-permute-start(bf16[1,768,1536]{2,1,0:T(8,128)(2,1)} %fusion), channel_id=1, source_target_pairs={{0,0},{1,1},{2,8},{3,9},{8,2},{9,3},{10,10},{11,11},{16,16},{17,17... | collective-permute-start | bytes 7077896 | tf_op jit(solution)/shard_map/ppermute | solution.py:749
  643.9 45.8 %collective-permute-start.66 = (bf16[1184,384]{1,0:T(8,128)(2,1)}, bf16[1184,384]{1,0:T(8,128)(2,1)S(1)}, u32[]{:S(2)}, u32[]{:S(2)}) collective-permute-start(bf16[1184,384]{1,0:T(8,128)(2,1)} %get-tuple-element.464), channel_id=1, source_target_pairs={{0,1},{1,0},{2,3},{3,2},{4,5},{5,4},{6,7},{7,6},{8,9},{9,8},{10,11... | collective-permute-start | bytes 2727944 | tf_op jit(solution)/shard_map/ppermute | solution.py:743
  645.6 44.0 %collective-permute-start.64 = (bf16[320,768]{1,0:T(8,128)(2,1)S(1)}, bf16[320,768]{1,0:T(8,128)(2,1)S(1)}, u32[]{:S(2)}, u32[]{:S(2)}) collective-permute-start(bf16[320,768]{1,0:T(8,128)(2,1)S(1)} %copy-done.82), channel_id=1, source_target_pairs={{0,4},{4,0},{1,5},{5,1},{2,6},{6,2},{3,7},{7,3},{8,12},{12,8},{9,1... | collective-permute-start | bytes 1474568 | tf_op jit(solution)/shard_map/ppermute | solution.py:746
  710.9 54.0 %collective-permute-start.71 = (bf16[1,768,1536]{2,1,0:T(8,128)(2,1)}, bf16[1,768,1536]{2,1,0:T(8,128)(2,1)}, u32[]{:S(2)}, u32[]{:S(2)}) collective-permute-start(bf16[1,768,1536]{2,1,0:T(8,128)(2,1)} %shard_map.413), channel_id=1, source_target_pairs={{0,4},{4,0},{1,5},{5,1},{2,6},{6,2},{3,7},{7,3},{8,12},{12,8},{9,1... | collective-permute-start | bytes 7077896 | tf_op jit(solution)/shard_map/ppermute | solution.py:746
  711.8 88.0 %collective-permute-start.74 = (bf16[1,768,1536]{2,1,0:T(8,128)(2,1)}, bf16[1,768,1536]{2,1,0:T(8,128)(2,1)}, u32[]{:S(2)}, u32[]{:S(2)}) collective-permute-start(bf16[1,768,1536]{2,1,0:T(8,128)(2,1)} %fusion.1), channel_id=1, source_target_pairs={{0,0},{1,1},{2,8},{3,9},{8,2},{9,3},{10,10},{11,11},{16,16},{17,17... | collective-permute-start | bytes 7077896 | tf_op jit(solution)/shard_map/ppermute | solution.py:749
  744.4 55.4 %collective-permute-start.69 = (bf16[1184,384]{1,0:T(8,128)(2,1)}, bf16[1184,384]{1,0:T(8,128)(2,1)S(1)}, u32[]{:S(2)}, u32[]{:S(2)}) collective-permute-start(bf16[1184,384]{1,0:T(8,128)(2,1)} %get-tuple-element.477), channel_id=1, source_target_pairs={{0,1},{1,0},{2,3},{3,2},{4,5},{5,4},{6,7},{7,6},{8,9},{9,8},{10,11... | collective-permute-start | bytes 2727944 | tf_op jit(solution)/shard_map/ppermute | solution.py:743
  747.5 52.3 %collective-permute-start.73 = (bf16[1,192,1536]{2,1,0:T(8,128)(2,1)}, bf16[1,192,1536]{2,1,0:T(8,128)(2,1)}, u32[]{:S(2)}, u32[]{:S(2)}) collective-permute-start(bf16[1,192,1536]{2,1,0:T(8,128)(2,1)} %fusion.61), channel_id=1, source_target_pairs={{0,16},{8,24},{16,0},{24,8},{1,17},{9,25},{17,1},{25,9},{2,18},{10... | collective-permute-start | bytes 1769480 | tf_op jit(solution)/shard_map/ppermute | solution.py:740
  764.9 76.3 %collective-permute-start.76 = (bf16[1,768,1536]{2,1,0:T(8,128)(2,1)}, bf16[1,768,1536]{2,1,0:T(8,128)(2,1)}, u32[]{:S(2)}, u32[]{:S(2)}) collective-permute-start(bf16[1,768,1536]{2,1,0:T(8,128)(2,1)} %shard_map.414), channel_id=1, source_target_pairs={{0,4},{4,0},{1,5},{5,1},{2,6},{6,2},{3,7},{7,3},{8,12},{12,8},{9,1... | collective-permute-start | bytes 7077896 | tf_op jit(solution)/shard_map/ppermute | solution.py:746
  776.2 65.0 %collective-permute-start.67 = (bf16[1184,384]{1,0:T(8,128)(2,1)}, bf16[1184,384]{1,0:T(8,128)(2,1)}, u32[]{:S(2)}, u32[]{:S(2)}) collective-permute-start(bf16[1184,384]{1,0:T(8,128)(2,1)} %get-tuple-element.467), channel_id=1, source_target_pairs={{0,0},{1,1},{2,8},{3,9},{8,2},{9,3},{10,10},{11,11},{16,16},{17,17... | collective-permute-start | bytes 2727944 | tf_op jit(solution)/shard_map/ppermute | solution.py:749
  879.3 45.1 %collective-permute-start.81 = (bf16[1,768,1536]{2,1,0:T(8,128)(2,1)}, bf16[1,768,1536]{2,1,0:T(8,128)(2,1)}, u32[]{:S(2)}, u32[]{:S(2)}) collective-permute-start(bf16[1,768,1536]{2,1,0:T(8,128)(2,1)} %shard_map.418), channel_id=1, source_target_pairs={{0,0},{1,1},{2,8},{3,9},{8,2},{9,3},{10,10},{11,11},{16,16},{17,17... | collective-permute-start | bytes 7077896 | tf_op jit(solution)/shard_map/ppermute | solution.py:749
  952.2 76.6 %collective-permute-start.87 = (bf16[1,768,1536]{2,1,0:T(8,128)(2,1)}, bf16[1,768,1536]{2,1,0:T(8,128)(2,1)}, u32[]{:S(2)}, u32[]{:S(2)}) collective-permute-start(bf16[1,768,1536]{2,1,0:T(8,128)(2,1)} %shard_map.422), channel_id=1, source_target_pairs={{0,0},{1,1},{2,8},{3,9},{8,2},{9,3},{10,10},{11,11},{16,16},{17,17... | collective-permute-start | bytes 7077896 | tf_op jit(solution)/shard_map/ppermute | solution.py:749
  971.4 38.3 %collective-permute-start.88 = (bf16[3,320,384]{2,1,0:T(8,128)(2,1)}, bf16[3,320,384]{2,1,0:T(8,128)(2,1)}, u32[]{:S(2)}, u32[]{:S(2)}) collective-permute-start(bf16[3,320,384]{2,1,0:T(8,128)(2,1)} %pad_maximum_fusion.6), channel_id=1, source_target_pairs={{0,4},{4,0},{1,5},{5,1},{2,6},{6,2},{3,7},{7,3},{8,12},{12,8},{9,1... | collective-permute-start | bytes 2211848 | tf_op jit(solution)/shard_map/ppermute | solution.py:746
  989.8 39.0 %collective-permute-start.86 = (bf16[1,192,1536]{2,1,0:T(8,128)(2,1)}, bf16[1,192,1536]{2,1,0:T(8,128)(2,1)}, u32[]{:S(2)}, u32[]{:S(2)}) collective-permute-start(bf16[1,192,1536]{2,1,0:T(8,128)(2,1)} %fusion.63), channel_id=1, source_target_pairs={{0,16},{8,24},{16,0},{24,8},{1,17},{9,25},{17,1},{25,9},{2,18},{10... | collective-permute-start | bytes 1769480 | tf_op jit(solution)/shard_map/ppermute | solution.py:740
  1008.5 41.6 %collective-permute-start.94 = (bf16[3,768,384]{2,1,0:T(8,128)(2,1)}, bf16[3,768,384]{2,1,0:T(8,128)(2,1)}, u32[]{:S(2)}, u32[]{:S(2)}) collective-permute-start(bf16[3,768,384]{2,1,0:T(8,128)(2,1)} %shard_map.425), channel_id=1, source_target_pairs={{0,4},{4,0},{1,5},{5,1},{2,6},{6,2},{3,7},{7,3},{8,12},{12,8},{9,1... | collective-permute-start | bytes 5308424 | tf_op jit(solution)/shard_map/ppermute | solution.py:746
  1014.1 90.8 %collective-permute-start.96 = (bf16[3,768,384]{1,2,0:T(8,128)(2,1)}, bf16[3,768,384]{1,2,0:T(8,128)(2,1)}, u32[]{:S(2)}, u32[]{:S(2)}) collective-permute-start(bf16[3,768,384]{1,2,0:T(8,128)(2,1)} %convert_bitcast_fusion), channel_id=1, source_target_pairs={{0,0},{1,1},{2,8},{3,9},{8,2},{9,3},{10,10},{11,11},{16,16},{17,17... | collective-permute-start | bytes 5308424 | tf_op jit(solution)/shard_map/ppermute | solution.py:749
  1060.1 66.9 %collective-permute-start.95 = (bf16[3,768,384]{2,1,0:T(8,128)(2,1)}, bf16[3,768,384]{2,1,0:T(8,128)(2,1)}, u32[]{:S(2)}, u32[]{:S(2)}) collective-permute-start(bf16[3,768,384]{2,1,0:T(8,128)(2,1)} %shard_map.432), channel_id=1, source_target_pairs={{0,0},{1,1},{2,8},{3,9},{8,2},{9,3},{10,10},{11,11},{16,16},{17,17... | collective-permute-start | bytes 5308424 | tf_op jit(solution)/shard_map/ppermute | solution.py:749
  1086.4 114.8 %collective-permute-start.78 = (bf16[1184,384]{1,0:T(8,128)(2,1)}, bf16[1184,384]{1,0:T(8,128)(2,1)S(1)}, u32[]{:S(2)}, u32[]{:S(2)}) collective-permute-start(bf16[1184,384]{1,0:T(8,128)(2,1)} %fusion.30), channel_id=1, source_target_pairs={{0,0},{1,1},{2,8},{3,9},{8,2},{9,3},{10,10},{11,11},{16,16},{17,17... | collective-permute-start | bytes 2727944 | tf_op jit(solution)/shard_map/ppermute | solution.py:749
  1140.2 61.0 %collective-permute-start.91 = (bf16[1184,384]{1,0:T(8,128)(2,1)}, bf16[1184,384]{1,0:T(8,128)(2,1)S(1)}, u32[]{:S(2)}, u32[]{:S(2)}) collective-permute-start(bf16[1184,384]{1,0:T(8,128)(2,1)} %fusion.37), channel_id=1, source_target_pairs={{0,0},{1,1},{2,8},{3,9},{8,2},{9,3},{10,10},{11,11},{16,16},{17,17... | collective-permute-start | bytes 2727944 | tf_op jit(solution)/shard_map/ppermute | solution.py:749
  1150.6 45.3 %collective-permute-start.100 = (bf16[1,192,1536]{2,1,0:T(8,128)(2,1)}, bf16[1,192,1536]{2,1,0:T(8,128)(2,1)}, u32[]{:S(2)}, u32[]{:S(2)}) collective-permute-start(bf16[1,192,1536]{2,1,0:T(8,128)(2,1)} %shard_map.434), channel_id=1, source_target_pairs={{0,0},{1,1},{2,8},{3,9},{8,2},{9,3},{10,10},{11,11},{16,16},{17,17... | collective-permute-start | bytes 1769480 | tf_op jit(solution)/shard_map/ppermute | solution.py:749
  (176 other events, 2676.3 us)

commit v3 on v2

--- a/solution.py
+++ b/solution.py
@@ -18,7 +18,7 @@
 OUTER_MOMENT = 0.9
 BLOCK = 256
 VMEM_BYTES = 60 * 1024 * 1024
-COST_SHARE = 4
+COST_SHARE = 1000
 NT = (((1,), (1,)), ((), ()))
 NN = (((1,), (0,)), ((), ()))
 TN = (((0,), (0,)), ((), ()))
@@ -610,13 +610,13 @@
 
 
 def weight_grad(ids, which, lefts, rights, height, add=None, tile=512):
-    part = lefts[0].shape[1] // 2
+    part = lefts[0].shape[1] // (1 if which is None else 2)
     n = len(lefts)
     right_spec, steps, _ = grad_specs(rights[0], tile, height, 0)
-    narrow = part % 128 != 0
+    narrow = which is not None and part % 128 != 0
     left_spec = pl.BlockSpec(
         (height, 2 * part if narrow else part),
-        lambda j, ids_ref: (0, 0 if narrow else ids_ref[which]),
+        lambda j, ids_ref: (0, 0 if narrow or which is None else ids_ref[which]),
         pipeline_mode=pl.Buffered(1),
     )
     out_spec, out_shape = grad_out(rights[0], tile, part)
@@ -645,76 +645,75 @@
     )(ids, *lefts, *rights, *more)
 
 
-def adam(ids, inv_count, moment, grad):
+def adam(ids, inv_count, moment, near, far):
     _, lead, _, piece, cols = moment.shape
     correct_one = 1.0 - BETA_ONE**STEP
     correct_two = 1.0 - BETA_TWO**STEP
 
-    def kernel(ids_ref, inv_ref, m_ref, g_ref, fresh_ref, keep_ref, send_ref):
-        t = pl.program_id(1)
-        g = g_ref[0, 0].astype(F32) * inv_ref[0]
-        first = BETA_ONE * m_ref[0, 0, 0] + (1.0 - BETA_ONE) * g
-        second = BETA_TWO * m_ref[1, 0, 0] + (1.0 - BETA_TWO) * g * g
-        fresh_ref[0, 0, 0] = first
-        fresh_ref[1, 0, 0] = second
-        update = ((first / correct_one) / (jnp.sqrt(second / correct_two) + ADAM_EPS)).astype(BF)
-
-        @pl.when(t < 2)
-        def _():
-            send_ref[0, 0] = update
-
-        @pl.when(t >= 2)
-        def _():
-            keep_ref[0, 0] = update
+    def kernel(ids_ref, inv_ref, m_ref, near_ref, far_ref, fresh_ref, keep_ref, send_ref):
+        t = pl.program_id(0)
+        for l in range(lead):
+            g = jnp.where(ids_ref[9] == 1, near_ref[l, 0], far_ref[l, 0]).astype(F32) * inv_ref[0]
+            first = BETA_ONE * m_ref[0, l, 0] + (1.0 - BETA_ONE) * g
+            second = BETA_TWO * m_ref[1, l, 0] + (1.0 - BETA_TWO) * g * g
+            fresh_ref[0, l, 0] = first
+            fresh_ref[1, l, 0] = second
+            update = (first * (1.0 / correct_one) / (jnp.sqrt(second * (1.0 / correct_two)) + ADAM_EPS)).astype(BF)
+
+            @pl.when(t < 2)
+            def _(l=l, update=update):
+                send_ref[0, l] = update
+
+            @pl.when(t >= 2)
+            def _(l=l, update=update):
+                keep_ref[0, l] = update
 
     def block(t, ids_ref):
         return (t % 2) * 2 + jnp.where(t < 2, 1 - ids_ref[0], ids_ref[0])
 
-    pairs = pl.BlockSpec((2, 1, 1, piece, cols), lambda l, t, ids_ref, _: (0, l, block(t, ids_ref), 0, 0))
+    pairs = pl.BlockSpec((2, lead, 1, piece, cols), lambda t, ids_ref, _: (0, 0, block(t, ids_ref), 0, 0))
+    grad = pl.BlockSpec((lead, 1, piece, cols), lambda t, ids_ref, _: (0, block(t, ids_ref), 0, 0))
     side = struct((2, lead, piece, cols), BF)
     return call(
         kernel,
-        (lead, 4),
+        (4,),
+        [pairs, grad, grad],
         [
             pairs,
-            pl.BlockSpec((1, 1, piece, cols), lambda l, t, ids_ref, _: (l, block(t, ids_ref), 0, 0)),
-        ],
-        [
-            pairs,
-            pl.BlockSpec((1, 1, piece, cols), lambda l, t, *_: (jnp.maximum(t - 2, 0), l, 0, 0)),
-            pl.BlockSpec((1, 1, piece, cols), lambda l, t, *_: (jnp.minimum(t, 1), l, 0, 0)),
+            pl.BlockSpec((1, lead, piece, cols), lambda t, *_: (jnp.maximum(t - 2, 0), 0, 0, 0)),
+            pl.BlockSpec((1, lead, piece, cols), lambda t, *_: (jnp.minimum(t, 1), 0, 0, 0)),
         ],
         [struct(moment.shape, F32), side, side],
         lead * piece * cols * 80,
         lead * piece * cols * 80,
         prefetch=2,
-    )(ids, inv_count, moment, grad)
+    )(ids, inv_count, moment, near, far)
 
 
 def outer_step(ids, state, keep, got, far, groups):
     _, lead, piece, cols = state.shape
 
     def kernel(ids_ref, s_ref, k_ref, g_ref, f_ref, out_ref):
-        near = (k_ref[0, 0].astype(F32) + g_ref[0, 0].astype(F32)).astype(BF).astype(F32)
-        total = near + f_ref[0].astype(F32)
-        master = s_ref[0, 0]
+        near = (k_ref[0].astype(F32) + g_ref[0].astype(F32)).astype(BF).astype(F32)
+        total = near + f_ref[...].astype(F32)
+        master = s_ref[0]
         delta = LEARN_RATE * (total * (1.0 / groups) + DECAY_RATE * master)
-        momentum = OUTER_MOMENT * s_ref[1, 0] + delta
-        out_ref[0, 0] = master - OUTER_RATE * (delta + OUTER_MOMENT * momentum)
-        out_ref[1, 0] = delta
-        out_ref[2, 0] = momentum
-
-    side = pl.BlockSpec((1, 1, piece, cols), lambda l, ids_ref: (ids_ref[2], l, 0, 0))
+        momentum = OUTER_MOMENT * s_ref[1] + delta
+        out_ref[0] = master - OUTER_RATE * (delta + OUTER_MOMENT * momentum)
+        out_ref[1] = delta
+        out_ref[2] = momentum
+
+    side = pl.BlockSpec((1, lead, piece, cols), lambda i, ids_ref: (ids_ref[2], 0, 0, 0))
     return call(
         kernel,
-        (lead,),
+        (1,),
         [
-            pl.BlockSpec((2, 1, piece, cols), lambda l, *_: (0, l, 0, 0)),
+            pl.BlockSpec((2, lead, piece, cols), lambda i, *_: (0, 0, 0, 0)),
             side,
             side,
-            pl.BlockSpec((1, piece, cols), lambda l, *_: (l, 0, 0)),
+            pl.BlockSpec((lead, piece, cols), lambda i, *_: (0, 0, 0)),
         ],
-        pl.BlockSpec((3, 1, piece, cols), lambda l, *_: (0, l, 0, 0)),
+        pl.BlockSpec((3, lead, piece, cols), lambda i, *_: (0, 0, 0, 0)),
         struct((3, lead, piece, cols), F32),
         lead * piece * cols * 10,
         lead * piece * cols * 26,
@@ -733,6 +732,8 @@
         for m in range(n_mp)
     ]
 
+    trade_perm = [(i, j if i != j else (i // n_mp ^ 2) * n_mp + i % n_mp) for i, j in turn_perm]
+
     def core_swap(a):
         return lax.ppermute(a, "group", core_perm)
 
@@ -747,6 +748,9 @@
 
     def turn(a):
         return lax.ppermute(a, ("group", "mp"), turn_perm)
+
+    def trade(a):
+        return lax.ppermute(a, ("group", "mp"), trade_perm)
 
     def by(flag, a, b, axis):
         return jnp.where(flag == 0, jnp.concatenate([a, b], axis), jnp.concatenate([b, a], axis))
@@ -759,7 +763,7 @@
         g, d, m = lax.axis_index("group"), lax.axis_index("dp"), lax.axis_index("mp")
         c, xc, zl = g % 2, g // 2, m % 2
         place = (d % 2) * 2 + xc
-        ids = jnp.stack([c, zl, xc, d % 2, 1 - d % 2, place, place ^ 1, place ^ 2, place ^ 3]).astype(jnp.int32)
+        ids = jnp.stack([c, zl, xc, d % 2, 1 - d % 2, place, place ^ 1, place ^ 2, place ^ 3, c == m // 2]).astype(jnp.int32)
 
         slots = image_tokens.shape[1]
         image_len, text_len = image_tokens.shape[2], text_tokens.shape[2]
@@ -787,6 +791,11 @@
             return move(hold(value, last))
 
         turned, over_x, over_y, over_z = (lambda value, move=move: send(move, value) for move in (turn, x_swap, y_swap, z_swap))
+        stays = c == m // 2
+
+        def owned(value):
+            return value, send(trade, value)
+
 
         def sync(*need):
             if n_dp == 2:
@@ -900,13 +909,13 @@
         rest_order = (1, 5, 2, 6, 7, 3)
         rest = step(lambda *a: cast_states(a), *(lead_states[i] for i in rest_order))
         rows_of = [a.shape[2] for a in lead_states]
+        def pair_start(own):
+            got = over_z(own)
+            return lambda: step(lambda a, b: by(zl, a, b, 1), own, got), got
+
         pairs = dict(zip((0, 4), step(lambda a, b: pair_pieces(ids, a, b, [[(3, rows_of[0])]] * 2), mine, got)))
         pairs = {i: turned(a) for i, a in pairs.items()}
         rest_got = send(core_swap, rest)
-        mod_own = turned(mod_join((image_modulation, text_modulation, group_counts)))
-        x_own = [turned(join((image_tokens[0, 0], text_tokens[0, 0])))]
-        count = mod_own[slots * 12, 0]
-        lives = [(s * n_dp + d < count).astype(F32) for s in range(slots)]
         pieces = step(
             lambda a, b: pair_pieces(
                 ids, a, b, [[(1, rows_of[1])] * 2] + [[(1, rows_of[i])] for i in (2, 6, 7, 3)]
@@ -918,72 +927,75 @@
         c_in = [join((image_cotan[0, s], text_cotan[0, s])) for s in range(slots)]
         sync(pairs[0])
         quads = [gather_one(pairs[0])]
+        x_own = [turned(x_in[0])]
         sync(pairs[4], quads[0])
         quads.append(gather_one(pairs[4]))
+        mod_own = turned(mod_join((image_modulation, text_modulation, group_counts)))
+        count = mod_own[slots * 12, 0]
+        lives = [(s * n_dp + d < count).astype(F32) for s in range(slots)]
+        sync(quads[1], x_own[0], mod_own)
+        x_pair, x_got = pair_start(x_own[0])
+        quads = [corner(a, s) for s, a in enumerate(quads)]
+        mod_pair, mod_got = pair_start(mod_own)
         pairs[1] = turned(pieces[1])
-        sync(quads[1], mod_own, x_own[0])
-        ready = z_pair(x_own[0])
-        mod_ready = z_pair(mod_own)
-        quads = [corner(a, s) for s, a in enumerate(quads)]
-        mod_pair = mod_ready()
-        sync(quads)
-        xs = [ready()]
+        sync(quads, x_got, mod_got)
+        xs = [with_core(x_pair())]
+        mod_pair = with_core(mod_pair())
+        sync(pairs[1])
+        outs = gather_one(pairs[1]) if n_dp == 2 else None
         pairs[2] = turned(pieces[2])
         wq = [assemble(a) for a in quads]
         mod_full = jnp.concatenate(mod_pair, 1)
-        sync(pairs[1])
-        if n_dp == 2:
-            outs = gather_one(pairs[1])
         firsts = [first_part(0)]
         sync(outs if n_dp == 2 else (), pairs[2])
         if n_dp == 2:
             outs = [corner(tuple(a[s : s + 1] for a in outs), s) for s in range(2)]
         else:
             outs = [gather_one(pairs[1][s : s + 1]) for s in range(2)]
+        pairs[6] = turned(pieces[6])
+        sync(outs)
         expand = [gather_one(pairs[2])]
         x_own += [turned(a) for a in x_in[1:]]
+        wo = [flat(assemble(a)) for a in outs]
         lses = [mixing(0)]
-        sync(outs, x_own, expand[0])
-        wo = [flat(assemble(a)) for a in outs]
-        pairs[6] = turned(pieces[6])
-        ready = [z_pair(x_own[s]) for s in range(1, slots)]
         keep, give = step(lambda a: out_project(ids, a, *wo, image_len), lses[0][0])
+        sync(expand[0], pairs[6], x_own)
         half = half_start(keep, give)
-        sync(ready and x_own)
-        xs += [a() for a in ready]
-        mine = half()
-        sums = [(mine, over_z(mine))]
-        sync(pairs[6])
         expand.append(gather_one(pairs[6]))
         pairs[7] = turned(pieces[7])
-        atts, mids, mlps, c_own, cots = [], [], [], [], []
+        more_x = [pair_start(x_own[s]) for s in range(1, slots)]
+        mine = half()
+        sync(expand[1], pairs[7], [a[1] for a in more_x])
+        expand = [corner(a, e) for e, a in enumerate(expand)]
+        pairs[3] = turned(pieces[3])
+        xs += [with_core(a[0]()) for a in more_x]
+        sums = [(mine, over_z(mine))]
+        atts, mids, mlps, c_own = [], [], [], []
         for s in range(1, slots):
             firsts.append(first_part(s))
             if s == 1:
-                sync(expand[1], pairs[7])
-                expand = [corner(a, e) for e, a in enumerate(expand)]
+                sync(expand, pairs[3])
                 reduce = [None, gather_one(pairs[7])]
-                pairs[3] = turned(pieces[3])
-            lses.append(mixing(s))
-            sync(sums[s - 1], pairs[3], reduce[1], expand)
-            atts.append(full_sum(*sums[s - 1]))
-            if s == 1:
                 c_own.append(turned(c_in[0]))
                 w1 = [flat(assemble(a)) for a in expand]
+            lses.append(mixing(s))
+            if s == 1:
+                sync(reduce[1], c_own[0], sums[0])
                 reduce[0] = gather_one(pairs[3])
+                cots = [pair_start(c_own[0])]
                 c_own += [turned(a) for a in c_in[1:]]
             keep, give = step(lambda a: out_project(ids, a, *wo, image_len), lses[s][0])
-            mine = half_sum(keep, give)
+            half = half_start(keep, give)
+            atts.append(full_sum(*sums[s - 1]))
+            mine = half()
             if s == 1:
-                sync(c_own[0])
-                cots = [z_pair(c_own[0])]
+                sync(reduce[0], cots[0][1])
+                reduce = [corner(a, e) for e, a in enumerate(reduce)]
+                cs = [with_core(cots[0][0]())]
             sums.append((mine, over_z(mine)))
-        sync(reduce[0])
-        reduce = [corner(a, s) for s, a in enumerate(reduce)]
-        cs = [cots[0]()]
-        cots += [z_pair(c_own[s]) for s in range(1, slots)]
         mids.append(middle(0))
-        sync(reduce)
+        sync(reduce, c_own)
+        cots += [pair_start(c_own[s]) for s in range(1, slots)]
         w2 = [flat(assemble(a)) for a in reduce]
 
         lefts_text, rights_text = {}, {}
@@ -1004,23 +1016,20 @@
 
         def text_grad(k):
             def product(left, left_got, right, right_got):
-                left = jnp.concatenate([left, left_got], 0)
-                right = jnp.concatenate([right, right_got], right.ndim - 2)
-                if right.ndim == 3:
-                    return jnp.einsum("td,ctf->cdf", left, right, preferred_element_type=F32).astype(BF)
-                return mm(left, right, TN).astype(BF)[None]
-
-            return turned(step(product, *text_lefts[k], *text_rights[k]))
-
-        def give_half(k, stream=0):
-            left, right, height = ((lefts, rights, image_len), (lefts_text, rights_text, slots * text_rows))[stream]
-            left, right = (a[k] if isinstance(a[k], list) else [a[k]] for a in (left, right))
-            return over_y(step(lambda a: weight_grad(ids, 4, a, right, height), left))
+                return weight_grad(ids, None, [left, left_got], [right, right_got], slots * text_rows)
+
+            return owned(step(product, *text_lefts[k], *text_rights[k]))
+
+        def give_later(k, right=None, stream=0):
+            left, rights_now, height = ((lefts, rights, image_len), (lefts_text, rights_text, slots * text_rows))[stream]
+            right = rights_now[k] if right is None else right
+            left, right = (a if isinstance(a, list) else [a] for a in (left[k], right))
+            return step(lambda a: weight_grad(ids, 4, a, right, height), left)
 
         def keep_half(k, got, stream=0, need=()):
             left, right, height = ((lefts, rights, image_len), (lefts_text, rights_text, slots * text_rows))[stream]
             left, right = (a[k] if isinstance(a[k], list) else [a[k]] for a in (left, right))
-            return turned(step(lambda a: weight_grad(ids, 3, a, right, height, got), left, need=need))
+            return owned(step(lambda a: weight_grad(ids, 3, a, right, height, got), left, need=need))
 
         def whole_grads(k):
             def one(left, right):
@@ -1031,7 +1040,7 @@
             image = sum(one(a[:image_len], b[..., :image_len, :]) for a, b in zip(lefts[k], rights[k]))
             text = one(lefts_text[k], rights_text[k])
             return [
-                turn(lax.psum_scatter(a.astype(BF), "dp", scatter_dimension=1, tiled=True)) for a in (image, text)
+                owned(lax.psum_scatter(a.astype(BF), "dp", scatter_dimension=1, tiled=True)) for a in (image, text)
             ]
 
         two_way = n_dp == 2
@@ -1074,8 +1083,8 @@
                 return res, column_sums(c_own[s].astype(F32) * lives[s] * branch)
 
             res, gate = step(first, *branch_mine[s])
-            results.append(turned(res))
             gates.append(gate)
+            return res
 
         def row_sums(s):
             _, _, n1o, _ = firsts[s]
@@ -1107,7 +1116,7 @@
                 gx = backs[s][2] + inv1[:, :1] * (q - total[0][:, None] - n1o * total[1][:, None])
                 return gx.astype(BF)
 
-            grads_x.append(turned(step(second, total, got, *gh1_mine[s])))
+            grads_x.append(owned(step(second, total, got, *gh1_mine[s])))
 
         fresh, outer, waiting = [None] * 8, [None] * 8, {}
         inv_count = (1.0 / group_counts[0].astype(F32)).reshape(1)
@@ -1119,12 +1128,15 @@
             lead, rows, cols = moment.shape[1:]
             piece = rows // n_group
             new, keep, give = step(
-                lambda grad: adam(ids, inv_count, moment.reshape(2, lead, n_group, piece, cols), grad),
-                grads[idx].reshape(lead, n_group, piece, cols),
+                lambda near, far: adam(ids, inv_count, moment.reshape(2, lead, n_group, piece, cols), near, far),
+                *(a.reshape(lead, n_group, piece, cols) for a in grads[idx]),
             )
-            updates[idx] = keep, send(core_swap, give)
+            updates[idx] = keep, give
             new = new.reshape(2, lead, rows, cols)
             fresh[idx] = new.transpose(0, 2, 1, 3)[None] if moments[idx].ndim == 5 else new[:, 0][None]
+
+        def send_update(idx):
+            updates[idx] = updates[idx][0], send(core_swap, updates[idx][1])
 
         def finish(idx):
             keep, got = updates[idx]
@@ -1140,7 +1152,6 @@
         def fill_mixing():
             rights[1] = [a[0] for a in backs]
             rights[0] = gqkvs
-            lefts_text[0] = step(text_of, lefts[0])
             rights_text[0] = step(text_of, gqkvs)
             lefts_text[1] = step(text_of, [a[0] for a in lses])
             rights_text[1] = step(text_of, rights[1])
@@ -1150,7 +1161,7 @@
             rights_text[k] = step(text_of, rights[k])
 
         mlps.append(dense(0))
-        sync(sums[-1], cots and c_own)
+        sync(sums[-1], [a[1] for a in cots])
         gh_sums = []
 
         def gh_half(s):
@@ -1166,16 +1177,17 @@
             waiting[idx] = far
 
         if two_way and slots == 2:
-            gh, br = half_start(mlps[0][4], mlps[0][5]), half_start(mlps[0][2], mlps[0][3])
+            gh = half_start(mlps[0][4], mlps[0][5])
             atts.append(full_sum(*sums[1]))
+            cs.append(with_core(cots[1][0]()))
             mine = gh()
             gh_sums.append((mine, over_z(mine)))
-            cs.append(cots[1]())
-            branch_mine.append(own_part(br()))
             mids.append(middle(1))
+            lefts_text[0] = step(text_of, [a[0] for a in firsts])
+            text_lefts[0] = text_left(0)
             mlps.append(dense(1))
-            sync(gh_sums[0], branch_mine[0])
-            gh, br = half_start(mlps[1][4], mlps[1][5]), half_start(mlps[1][2], mlps[1][3])
+            sync(gh_sums[0], text_lefts[0])
+            gh = half_start(mlps[1][4], mlps[1][5])
             gh2s = [full_sum(*gh_sums[0])]
             fill_dense()
             fill_text(3)
@@ -1183,85 +1195,96 @@
             text_rights[3] = text_right(3)
             mine = gh()
             gh_sums.append((mine, over_z(mine)))
-            row_results(0)
-            branch_half = br()
             backward(0)
-            sync(text_lefts[3], text_rights[3], results[0])
+            sent_three = give_later(3)
+            sent_two = give_later(2)
             fill_text(2)
+            sync(text_lefts[3], text_rights[3], gh_sums[1])
+            gh2s.append(full_sum(*gh_sums[1]))
+            br = [half_start(mlps[s][2], mlps[s][3]) for s in range(2)]
+            grads[7] = text_grad(3)
             text_rights[2] = text_right(2)
             text_lefts[2] = text_left(2)
-            grads[7] = text_grad(3)
-            sent[3] = give_half(3)
-            sync(gh_sums[1], text_rights[2])
-            gh2s.append(full_sum(*gh_sums[1]))
-            branch_mine.append(own_part(branch_half))
-            sent[2] = give_half(2)
+            br = [a() for a in br]
+            branch_mine.append(own_part(br[0]))
             unmix(0)
-            sync(text_lefts[2], grads[7], branch_mine[1])
+            sync(grads[7], text_rights[2], text_lefts[2], branch_mine[0])
+            sent[3] = over_y(sent_three)
             grads[6] = text_grad(2)
-            row_results(1)
+            branch_mine.append(own_part(br[1]))
+            res = [row_results(0)]
+            backward(1)
             out = step(lambda a: input_partial(ids, a, *wq, image_len), gqkvs[0])
+            optimize(7)
+            sync(sent[3], grads[6], branch_mine[1])
             half = half_start(*out)
-            optimize(7)
+            send_update(7)
+            grads[3] = keep_half(3, sent[3])
             gh1_mine.append(own_part(half()))
             small_sum(7)
-            sync(sent[3])
-            grads[3] = keep_half(3, sent[3])
-            backward(1)
-            sync(gh1_mine[0], waiting[7], grads[6])
+            sent[2] = over_y(sent_two)
+            unmix(1)
+            sync(grads[3], gh1_mine[0], waiting[7], sent[2])
+            grads[2] = keep_half(2, sent[2])
+            results.append(owned(res[0]))
             totals = [row_sums(0)]
+            sent_zero = give_later(0, gqkvs)
+            out = step(lambda a: input_partial(ids, a, *wq, image_len), gqkvs[1])
             finish(7)
+            res.append(row_results(1))
+            fill_mixing()
+            text_rights[0] = text_right(0)
+            optimize(6)
+            sync(grads[2], totals[0], text_rights[0], results[0])
+            half = half_start(*out)
+            send_update(6)
             totals[0] = row_total(*totals[0])
-            unmix(1)
-            sync(sent[2], results[1])
-            grads[2] = keep_half(2, sent[2])
-            row_grads(0, *totals[0])
-            out = step(lambda a: input_partial(ids, a, *wq, image_len), gqkvs[1])
-            half = half_start(*out)
-            optimize(6)
+            grads[4] = text_grad(0)
+            sent[0] = over_y(sent_zero)
             gh1_mine.append(own_part(half()))
             small_sum(6)
-            fill_mixing()
-            text_lefts[0] = text_left(0)
-            text_rights[0] = text_right(0)
-            sent[0] = give_half(0)
-            sync(grads[3], waiting[6], gh1_mine[1])
+            row_grads(0, *totals[0])
             optimize(3)
-            sent[5] = give_half(1, 1)
-            sent[1] = give_half(1)
+            sent_text, sent_one = give_later(1, None, 1), give_later(1)
+            sync(grads[4], gh1_mine[1], waiting[6], sent[0])
+            send_update(3)
+            grads[0] = keep_half(0, sent[0])
+            results.append(owned(res[1]))
+            totals.append(row_sums(1))
+            sent[5], sent[1] = over_y(sent_text), over_y(sent_one)
             small_sum(3)
-            totals.append(row_sums(1))
             finish(6)
+            optimize(2)
+            optimize(4)
+            sync(totals[1], sent[5], sent[1], grads[0], waiting[3], results[1], grads_x[0])
             totals[1] = row_total(*totals[1])
-            sync(text_lefts[0], text_rights[0])
-            grads[4] = text_grad(0)
-            sync(grads[2], waiting[3])
-            optimize(2)
-            finish(3)
-            row_grads(1, *totals[1])
-            small_sum(2)
-            sync(sent[0])
-            grads[0] = keep_half(0, sent[0])
-            sync(sent[5], sent[1])
+            send_update(2)
+            send_update(4)
             grads[5] = keep_half(1, sent[5], 1)
             grads[1] = keep_half(1, sent[1])
-            finish(2)
-            sync(grads[4])
-            optimize(4)
-            sync(grads[0])
+            small_sum(2)
+            small_sum(4)
+            row_grads(1, *totals[1])
+            finish(3)
             optimize(0)
-            small_sum(4)
-            small_sum(0)
+            sync(waiting[2], waiting[4], grads[5], grads[1])
+            send_update(0)
             optimize(5)
             optimize(1)
+            small_sum(0)
+            send_update(5)
+            send_update(1)
+            finish(2)
+            finish(4)
             small_sum(5)
             small_sum(1)
-            for i in (4, 0, 5, 1):
+            for i in (0, 5, 1):
                 finish(i)
         else:
             for s in range(1, slots):
-                atts.append(full_sum(*sums[s]))
-                cs.append(cots[s]())
+                if len(atts) == s:
+                    atts.append(full_sum(*sums[s]))
+                cs.append(with_core(cots[s][0]()))
                 mids.append(middle(s))
                 mlps.append(dense(s))
             fill_dense()
@@ -1273,21 +1296,22 @@
                 unmix(s)
                 to_input(s)
                 to_branch(s)
-                row_results(s)
+                results.append(owned(row_results(s)))
                 row_grads(s, *row_total(*row_sums(s)))
             fill_mixing()
+            lefts_text[0] = step(text_of, lefts[0])
             fill_text(2)
             fill_text(3)
             for k in (3, 2, 1, 0):
                 grads[k], grads[k + 4] = whole_grads(k)
             for i in range(8):
                 optimize(i)
+                send_update(i)
                 small_sum(i)
                 finish(i)
         mod_back = turn(jnp.stack(modgrads).reshape(slots * 12, local)).reshape(slots, 6, 2, local)
 
-        res = jnp.stack(results)
-        gx = jnp.stack(grads_x)
+        res, gx = (jnp.stack([jnp.where(stays, a, b) for a, b in pairs]) for pairs in (results, grads_x))
         return (
             res[None, :, :image_len],
             res[None, :, image_len:length],

time: 1260 us -> 1110 us (0.88)
  starting transfers between devices: 343 us -> 196 us
  other arithmetic: 74.9 us -> 89.9 us
  matrix products: 13.9 us -> 0 us
    ppermute x25 -> x13, starting transfers between devices: 197 us -> 48.8 us  [turn(): return lax.ppermute(a, ('group', 'mp'), turn_perm)]
    ppermute x15, waiting for transfers between devices: 108 us -> 75.7 us  [z_swap(): return lax.ppermute(a, 'mp', z_perm)]
    pallas_call x10 -> x13, Pallas kernels: 83.1 us -> 102 us  [weight_grad(): call(kernel, (steps,), [left_spec] * n + [right_spec] * n + [out_spec] *...]
    dot_general x3 -> x0, matrix products: 13.9 us -> none  [the longest x2 9.56 us: mm(): return lax.dot_general(a, b, dims, preferred_element_type=F32)]
    ppermute x22, waiting for transfers between devices: 32.8 us -> 45.8 us  [y_swap(): return lax.ppermute(a, 'dp', y_perm)]
    unnamed x206 -> x204, local copies, waits for them, and re-layouts: 28.2 us -> 32.8 us
  transfers between devices with their start and end apart: 110 -> 110, of which waited for: 23 -> 27; matrix products, arithmetic and copies ran while one was open for 9% -> 11% of each run, Pallas kernels for 39% -> 49%
where the time goes in v3:
time: 1110 us; the launch traced here: 1090 us
  Pallas kernels  561 us (51%)
  starting transfers between devices  196 us (18%)
  waiting for transfers between devices  175 us (16%)
  other arithmetic  89.9 us (8%)
  local copies, waits for them, and re-layouts  65.7 us (6%)
    pallas_call x13, Pallas kernels, weight_grad(): call(kernel, (steps,), [left_spec] * n + [right_spec] * n + [out_spec] *...  102 us
    pallas_call x2, Pallas kernels, mlp(): call(kernel, (steps,), [whole((rows, width)), whole((rows, width)), w1_sp...  81.4 us
    ppermute x29, starting transfers between devices, core_swap(): return lax.ppermute(a, 'group', core_perm)  79.3 us
    pallas_call x8, Pallas kernels, adam(): call(kernel, (4,), [pairs, grad, grad], [pairs, pl.BlockSpec((1, lead, pi...  75.8 us
    ppermute x15, waiting for transfers between devices, z_swap(): return lax.ppermute(a, 'mp', z_perm)  75.7 us
    pallas_call x2, Pallas kernels, attend_back(): pl.pallas_call(kernel, grid=(pairs,), in_specs=[pl.BlockSpec((3, rows, 12...  65.8 us
    ppermute x13, starting transfers between devices, turn(): return lax.ppermute(a, ('group', 'mp'), turn_perm)  48.8 us
    ppermute x19, waiting for transfers between devices, x_swap(): return lax.ppermute(a, 'group', x_perm)  47.8 us
  transfers between devices with their start and end apart: 110, of which 27 were waited for; matrix products, arithmetic and copies ran while one was open for 11% of the time, Pallas kernels for 49%

profile of v3, /device:TPU:0, one launch (start us, length us, event | category | flops | bytes accessed | tf_op | source)
XLA Modules:
  0.0 1092.7 jit_solution(9333577359013212906)
XLA Ops:
  43.5 13.4 %collective-permute-done.8.refs_1_ = bf16[3,384,384]{2,1,0:T(8,128)(2,1)} collective-permute-done((bf16[3,384,384]{2,1,0:T(8,128)(2,1)S(1)}, bf16[3,384,384]{2,1,0:T(8,128)(2,1)}, u32[]{:S(2)}, u32[]{:S(2)}) %collective-permute-start.8) | collective-permute-done | bytes 884768 | tf_op jit(solution)/shard_map/ppermute | solution.py:741
  63.3 17.5 %collective-permute-done.13 = f32[32,384]{1,0:T(8,128)S(1)} collective-permute-done((f32[32,384]{1,0:T(8,128)S(1)}, f32[32,384]{1,0:T(8,128)S(1)}, u32[]{:S(2)}, u32[]{:S(2)}) %collective-permute-start.13) | collective-permute-done | bytes 49184 | tf_op jit(solution)/shard_map/ppermute | solution.py:744
  83.3 19.7 %collective-permute-start.15 = (bf16[1184,768]{1,0:T(8,128)(2,1)S(1)}, bf16[1184,768]{1,0:T(8,128)(2,1)}, u32[]{:S(2)}, u32[]{:S(2)}) collective-permute-start(bf16[1184,768]{1,0:T(8,128)(2,1)S(1)} %maximum_select_fusion.xm_ref), channel_id=1, source_target_pairs={{0,8},{8,0},{16,24},{24,16},{1,9},{9,1},{17,25},{25,17},{2,10},{10... | collective-permute-start | bytes 5455880 | tf_op jit(solution)/shard_map/ppermute | solution.py:738
  122.8 15.4 %shard_map.396 = (bf16[1184,1536]{1,0:T(8,128)(2,1)}, bf16[3,1184,384]{2,1,0:T(8,128)(2,1)}, f32[1184,384]{1,0:T(8,128)}, f32[1184,128]{1,0:T(8,128)}) custom-call(s32[10]{0:T(128)} %stack.170.ids_ref, bf16[1184,768]{1,0:T(8,128)(2,1)} %copy-done.25, bf16[1184,768]{1,0:T(8,128)(2,1)} %collective-permute-done.15.xo_ref, ...), custom_call_target="tpu_custom_call" | custom-call | flops 4190109 | bytes 17989 | tf_op jit(solution)/shard_map/pallas_call | solution.py:191
  163.7 22.2 %shard_map.399 = (bf16[1184,384]{1,0:T(8,128)(2,1)}, f32[3,8,1280]{2,1,0:T(8,128)}) custom-call(bf16[3,1184,384]{2,1,0:T(8,128)(2,1)} %get-tuple-element.456.qkv_ref), custom_call_target="tpu_custom_call" | custom-call | flops 8613003 | bytes 3637 | tf_op jit(solution)/shard_map/pallas_call | solution.py:248
  202.0 31.0 %collective-permute-done.30 = bf16[1184,384]{1,0:T(8,128)(2,1)S(1)} collective-permute-done((bf16[1184,384]{1,0:T(8,128)(2,1)}, bf16[1184,384]{1,0:T(8,128)(2,1)S(1)}, u32[]{:S(2)}, u32[]{:S(2)}) %collective-permute-start.30) | collective-permute-done | bytes 909344 | tf_op jit(solution)/shard_map/ppermute | solution.py:744
  242.6 15.4 %shard_map.401 = (bf16[1184,1536]{1,0:T(8,128)(2,1)}, bf16[3,1184,384]{2,1,0:T(8,128)(2,1)}, f32[1184,384]{1,0:T(8,128)}, f32[1184,128]{1,0:T(8,128)}) custom-call(s32[10]{0:T(128)} %stack.170.ids_ref, bf16[1184,768]{1,0:T(8,128)(2,1)} %copy-done.24, bf16[1184,768]{1,0:T(8,128)(2,1)} %collective-permute-done.31.xo_ref, ...), custom_call_target="tpu_custom_call" | custom-call | flops 4190109 | bytes 17989 | tf_op jit(solution)/shard_map/pallas_call | solution.py:191
  290.5 22.2 %shard_map.404 = (bf16[1184,384]{1,0:T(8,128)(2,1)}, f32[3,8,1280]{2,1,0:T(8,128)}) custom-call(bf16[3,1184,384]{2,1,0:T(8,128)(2,1)} %get-tuple-element.484.qkv_ref), custom_call_target="tpu_custom_call" | custom-call | flops 8613003 | bytes 3637 | tf_op jit(solution)/shard_map/pallas_call | solution.py:248
  328.0 16.9 %collective-permute-done.42 = bf16[1184,384]{1,0:T(8,128)(2,1)S(1)} collective-permute-done((bf16[1184,384]{1,0:T(8,128)(2,1)}, bf16[1184,384]{1,0:T(8,128)(2,1)S(1)}, u32[]{:S(2)}, u32[]{:S(2)}) %collective-permute-start.42) | collective-permute-done | bytes 909344 | tf_op jit(solution)/shard_map/ppermute | solution.py:744
  368.3 11.8 %shard_map.406 = (bf16[1184,1536]{1,0:T(8,128)(2,1)}, bf16[1184,1536]{1,0:T(8,128)(2,1)}, f32[1184,384]{1,0:T(8,128)}) custom-call(s32[10]{0:T(128)} %stack.170.ids_ref, f32[1]{0:T(128)} %bitcast.20.live_ref, bf16[1184,768]{1,0:T(8,128)(2,1)} %copy-done.25, bf16[1184,768]{1,0:T(8,128)(2,1)} %collective-permute-done.15.xo_ref, bf16[1184,768]{1,0:T(8,128)(2,1)} %copy-done.29, ...), custom_call_target="tpu_custom_call" | custom-call | flops 36372 | bytes 20004 | tf_op jit(solution)/shard_map/pallas_call | solution.py:426
  393.1 40.6 %shard_map.409 = (bf16[1184,1536]{1,0:T(8,128)(2,1)}, bf16[1184,1536]{1,0:T(8,128)(2,1)}, bf16[1184,768]{1,0:T(8,128)(2,1)}, bf16[1184,768]{1,0:T(8,128)(2,1)}, ...) custom-call(s32[10]{0:T(128)} %stack.170.ids_ref, bf16[1184,1536]{1,0:T(8,128)(2,1)} %get-tuple-element.491.h_ref.refs_0_, ...), custom_call_target="tpu_custom_call" | custom-call | flops 22347252 | bytes 40697 | tf_op jit(solution)/shard_map/pallas_call | solution.py:498
  447.1 11.7 %shard_map.410 = (bf16[1184,1536]{1,0:T(8,128)(2,1)}, bf16[1184,1536]{1,0:T(8,128)(2,1)}, f32[1184,384]{1,0:T(8,128)}) custom-call(s32[10]{0:T(128)} %stack.170.ids_ref, f32[1]{0:T(128)} %bitcast.35.live_ref, bf16[1184,768]{1,0:T(8,128)(2,1)} %copy-done.24, bf16[1184,768]{1,0:T(8,128)(2,1)} %collective-permute-done.31.xo_ref, ...), custom_call_target="tpu_custom_call" | custom-call | flops 36372 | bytes 20004 | tf_op jit(solution)/shard_map/pallas_call | solution.py:426
  462.6 40.8 %shard_map.411 = (bf16[1184,1536]{1,0:T(8,128)(2,1)}, bf16[1184,1536]{1,0:T(8,128)(2,1)}, bf16[1184,768]{1,0:T(8,128)(2,1)}, bf16[1184,768]{1,0:T(8,128)(2,1)}, ...) custom-call(s32[10]{0:T(128)} %stack.170.ids_ref, bf16[1184,1536]{1,0:T(8,128)(2,1)} %get-tuple-element.492.h_ref.refs_1_, ...), custom_call_target="tpu_custom_call" | custom-call | flops 22347252 | bytes 40697 | tf_op jit(solution)/shard_map/pallas_call | solution.py:498
  517.9 15.2 %shard_map.412 = (bf16[1184,1536]{1,0:T(8,128)(2,1)}, bf16[1184,384]{1,0:T(8,128)(2,1)}, f32[1184,384]{1,0:T(8,128)}, f32[2,24,384]{2,1,0:T(8,128)}) custom-call(s32[10]{0:T(128)} %stack.170.ids_ref, f32[1]{0:T(128)} %bitcast.20.live_ref, bf16[1184,768]{1,0:T(8,128)(2,1)} %copy-done.25, bf16[1184,768]{1,0:T(8,128)(2,1)} %collective-permute-done.15.xo_ref, ...), custom_call_target="tpu_custom_call" | custom-call | flops 1396703 | bytes 21823 | tf_op jit(solution)/shard_map/pallas_call | solution.py:570
  533.1 9.6 shard_map.413
  542.7 9.6 shard_map.414
  576.9 32.8 %shard_map.416.a_ref.refs_2_ = bf16[3,1184,384]{2,1,0:T(8,128)(2,1)} custom-call(bf16[3,1184,384]{2,1,0:T(8,128)(2,1)} %get-tuple-element.456.qkv_ref, bf16[1184,384]{1,0:T(8,128)(2,1)} %get-tuple-element.457.grad_ref, f32[3,8,1280]{2,1,0:T(8,128)} %get-tuple-element.458.lse_ref), custom_call_target="tpu_custom_call" | custom-call | flops 21532508 | bytes 6365 | tf_op jit(solution)/shard_map/pallas_call | solution.py:295
  618.5 12.0 %collective-permute-start.66 = (bf16[1184,768]{1,0:T(8,128)(2,1)S(1)}, bf16[1184,768]{1,0:T(8,128)(2,1)}, u32[]{:S(2)}, u32[]{:S(2)}) collective-permute-start(bf16[1184,768]{1,0:T(8,128)(2,1)S(1)} %add_convert_fusion.4.gm_ref), channel_id=1, source_target_pairs={{0,8},{8,0},{16,24},{24,16},{1,9},{9,1},{17,25},{25,17},{2,10},{10... | collective-permute-start | bytes 5455880 | tf_op jit(solution)/shard_map/ppermute | solution.py:738
  638.4 15.4 %shard_map.418 = (bf16[1184,1536]{1,0:T(8,128)(2,1)}, bf16[1184,384]{1,0:T(8,128)(2,1)}, f32[1184,384]{1,0:T(8,128)}, f32[2,24,384]{2,1,0:T(8,128)}) custom-call(s32[10]{0:T(128)} %stack.170.ids_ref, f32[1]{0:T(128)} %bitcast.35.live_ref, bf16[1184,768]{1,0:T(8,128)(2,1)} %copy-done.24, bf16[1184,768]{1,0:T(8,128)(2,1)} %collective-permute-done.31.xo_ref, ...), custom_call_target="tpu_custom_call" | custom-call | flops 1396703 | bytes 21823 | tf_op jit(solution)/shard_map/pallas_call | solution.py:570
  653.9 11.9 %shard_map.419 = (bf16[1184,768]{1,0:T(8,128)(2,1)}, bf16[1184,768]{1,0:T(8,128)(2,1)}) custom-call(s32[10]{0:T(128)} %stack.170.ids_ref, bf16[3,1184,384]{2,1,0:T(8,128)(2,1)} %shard_map.416.a_ref.refs_2_, bf16[3,1536,384]{2,1,0:T(8,128)(2,1)} %copy-done, bf16[3,1536,384]{2,1,0:T(8,128)(2,1)} %copy-done.1), custom_call_target="tpu_custom_call" | custom-call | flops 4190109 | bytes 16171 | tf_op jit(solution)/shard_map/pallas_call | solution.py:376
  665.8 11.5 %shard_map.420 = (f32[2,1,4,192,1536]{4,3,2,1,0:T(8,128)}, bf16[2,1,192,1536]{3,2,1,0:T(8,128)(2,1)}, bf16[2,1,192,1536]{3,2,1,0:T(8,128)(2,1)}) custom-call(s32[10]{0:T(128)} %stack.170.ids_ref, f32[1]{0:T(128)} %bitcast.36.inv_ref, f32[2,1,4,192,1536]{4,3,2,1,0:T(8,128)} %bitcast.175, bf16[1,4,192,1536]{3,2,1,0:T(8,128)(2,1)} %bitcast.190, ...), custom_call_target="tpu_custom_call" | custom-call | flops 23592 | bytes 23592 | tf_op jit(solution)/shard_map/pallas_call | solution.py:677
  683.4 10.5 shard_map.421
  700.3 33.0 %shard_map.422.refs_3_.a_ref = bf16[3,1184,384]{2,1,0:T(8,128)(2,1)} custom-call(bf16[3,1184,384]{2,1,0:T(8,128)(2,1)} %get-tuple-element.484.qkv_ref, bf16[1184,384]{1,0:T(8,128)(2,1)} %get-tuple-element.485.grad_ref, f32[3,8,1280]{2,1,0:T(8,128)} %get-tuple-element.486.lse_ref), custom_call_target="tpu_custom_call" | custom-call | flops 21532508 | bytes 6365 | tf_op jit(solution)/shard_map/pallas_call | solution.py:295
  735.6 15.4 %collective-permute-done.75.refs_4_ = bf16[1,768,1536]{2,1,0:T(8,128)(2,1)} collective-permute-done((bf16[1,768,1536]{2,1,0:T(8,128)(2,1)}, bf16[1,768,1536]{2,1,0:T(8,128)(2,1)}, u32[]{:S(2)}, u32[]{:S(2)}) %collective-permute-start.75) | collective-permute-done | bytes 2359328 | tf_op jit(solution)/shard_map/ppermute | solution.py:747
  751.0 10.7 shard_map.423
  775.6 11.9 %shard_map.425 = (bf16[1184,768]{1,0:T(8,128)(2,1)}, bf16[1184,768]{1,0:T(8,128)(2,1)}) custom-call(s32[10]{0:T(128)} %stack.170.ids_ref, bf16[3,1184,384]{2,1,0:T(8,128)(2,1)} %shard_map.422.refs_3_.a_ref, bf16[3,1536,384]{2,1,0:T(8,128)(2,1)} %copy-done, bf16[3,1536,384]{2,1,0:T(8,128)(2,1)} %copy-done.1), custom_call_target="tpu_custom_call" | custom-call | flops 4190109 | bytes 16171 | tf_op jit(solution)/shard_map/pallas_call | solution.py:376
  808.4 11.5 %shard_map.427 = (f32[2,1,4,192,1536]{4,3,2,1,0:T(8,128)}, bf16[2,1,192,1536]{3,2,1,0:T(8,128)(2,1)}, bf16[2,1,192,1536]{3,2,1,0:T(8,128)(2,1)}) custom-call(s32[10]{0:T(128)} %stack.170.ids_ref, f32[1]{0:T(128)} %bitcast.36.inv_ref, f32[2,1,4,192,1536]{4,3,2,1,0:T(8,128)} %bitcast.176, bf16[1,4,192,1536]{3,2,1,0:T(8,128)(2,1)} %bitcast.189, ...), custom_call_target="tpu_custom_call" | custom-call | flops 23592 | bytes 23592 | tf_op jit(solution)/shard_map/pallas_call | solution.py:677
  825.4 9.9 collective-permute-start.80
  858.7 11.5 %shard_map.429 = (f32[2,1,4,192,1536]{4,3,2,1,0:T(8,128)}, bf16[2,1,192,1536]{3,2,1,0:T(8,128)(2,1)}, bf16[2,1,192,1536]{3,2,1,0:T(8,128)(2,1)}) custom-call(s32[10]{0:T(128)} %stack.170.ids_ref, f32[1]{0:T(128)} %bitcast.36.inv_ref, f32[2,1,4,192,1536]{4,3,2,1,0:T(8,128)} %bitcast.177, bf16[1,4,192,1536]{3,2,1,0:T(8,128)(2,1)} %bitcast.188, ...), custom_call_target="tpu_custom_call" | custom-call | flops 23592 | bytes 23592 | tf_op jit(solution)/shard_map/pallas_call | solution.py:677
  898.1 10.0 shard_map.432
  924.9 11.5 %shard_map.434 = (f32[2,1,4,192,1536]{4,3,2,1,0:T(8,128)}, bf16[2,1,192,1536]{3,2,1,0:T(8,128)(2,1)}, bf16[2,1,192,1536]{3,2,1,0:T(8,128)(2,1)}) custom-call(s32[10]{0:T(128)} %stack.170.ids_ref, f32[1]{0:T(128)} %bitcast.36.inv_ref, f32[2,1,4,192,1536]{4,3,2,1,0:T(8,128)} %bitcast.178, bf16[1,4,192,1536]{3,2,1,0:T(8,128)(2,1)} %bitcast.187, ...), custom_call_target="tpu_custom_call" | custom-call | flops 23592 | bytes 23592 | tf_op jit(solution)/shard_map/pallas_call | solution.py:677
  953.3 16.2 %collective-permute-start.95 = (bf16[2,1,192,1536]{3,2,1,0:T(8,128)(2,1)}, bf16[2,1,192,1536]{3,2,1,0:T(8,128)(2,1)}, u32[]{:S(2)}, u32[]{:S(2)}) collective-permute-start(bf16[2,1,192,1536]{3,2,1,0:T(8,128)(2,1)} %get-tuple-element.566), channel_id=1, source_target_pairs={{0,8},{8,0},{16,24},{24,16},{1,9},{9,1},{17,25},{25,17},{2,10},{10... | collective-permute-start | bytes 3538952 | tf_op jit(solution)/shard_map/ppermute | solution.py:738
  (614 shorter events, 539.3 us)
Async XLA Ops:
  61.5 41.5 %collective-permute-start.14 = (bf16[2,96,1536]{2,1,0:T(8,128)(2,1)}, bf16[2,96,1536]{2,1,0:T(8,128)(2,1)S(1)}, u32[]{:S(2)}, u32[]{:S(2)}) collective-permute-start(bf16[2,96,1536]{2,1,0:T(8,128)(2,1)} %get-tuple-element.333), channel_id=1, source_target_pairs={{0,0},{1,1},{2,8},{3,9},{8,2},{9,3},{10,10},{11,11},{16,16},{17,17... | collective-permute-start | bytes 1769480 | tf_op jit(solution)/shard_map/ppermute | solution.py:750
  83.3 39.5 %collective-permute-start.15 = (bf16[1184,768]{1,0:T(8,128)(2,1)S(1)}, bf16[1184,768]{1,0:T(8,128)(2,1)}, u32[]{:S(2)}, u32[]{:S(2)}) collective-permute-start(bf16[1184,768]{1,0:T(8,128)(2,1)S(1)} %maximum_select_fusion.xm_ref), channel_id=1, source_target_pairs={{0,8},{8,0},{16,24},{24,16},{1,9},{9,1},{17,25},{25,17},{2,10},{10... | collective-permute-start | bytes 5455880 | tf_op jit(solution)/shard_map/ppermute | solution.py:738
  140.3 52.9 %collective-permute-start.25 = (bf16[1,384,1536]{2,1,0:T(8,128)(2,1)}, bf16[1,384,1536]{2,1,0:T(8,128)(2,1)S(1)}, u32[]{:S(2)}, u32[]{:S(2)}) collective-permute-start(bf16[1,384,1536]{2,1,0:T(8,128)(2,1)} %get-tuple-element.355), channel_id=1, source_target_pairs={{0,0},{1,1},{2,8},{3,9},{8,2},{9,3},{10,10},{11,11},{16,16},{17,17... | collective-permute-start | bytes 3538952 | tf_op jit(solution)/shard_map/ppermute | solution.py:750
  148.4 44.8 %collective-permute-start.23 = (bf16[1,384,1536]{2,1,0:T(8,128)(2,1)S(1)}, bf16[1,384,1536]{2,1,0:T(8,128)(2,1)S(1)}, u32[]{:S(2)}, u32[]{:S(2)}) collective-permute-start(bf16[1,384,1536]{2,1,0:T(8,128)(2,1)S(1)} %collective-permute-done.19.refs_0_), channel_id=1, source_target_pairs={{0,16},{8,24},{16,0},{24,8},{1,17},{9,25},{17,1},{25,9},{2,18},{10... | collective-permute-start | bytes 3538952 | tf_op jit(solution)/shard_map/ppermute | solution.py:741
  149.3 45.0 %collective-permute-start.24 = (bf16[1,384,1536]{2,1,0:T(8,128)(2,1)S(1)}, bf16[1,384,1536]{2,1,0:T(8,128)(2,1)}, u32[]{:S(2)}, u32[]{:S(2)}) collective-permute-start(bf16[1,384,1536]{2,1,0:T(8,128)(2,1)S(1)} %collective-permute-done.19.refs_0_), channel_id=1, source_target_pairs={{0,4},{4,0},{1,5},{5,1},{2,6},{6,2},{3,7},{7,3},{8,12},{12,8},{9,1... | collective-permute-start | bytes 3538952 | tf_op jit(solution)/shard_map/ppermute | solution.py:747
  151.5 41.7 %collective-permute-start.22 = (bf16[1184,384]{1,0:T(8,128)(2,1)}, bf16[1184,384]{1,0:T(8,128)(2,1)}, u32[]{:S(2)}, u32[]{:S(2)}) collective-permute-start(bf16[1184,384]{1,0:T(8,128)(2,1)} %fusion.34), channel_id=1, source_target_pairs={{0,0},{1,1},{2,8},{3,9},{8,2},{9,3},{10,10},{11,11},{16,16},{17,17... | collective-permute-start | bytes 2727944 | tf_op jit(solution)/shard_map/ppermute | solution.py:750
  194.2 38.8 %collective-permute-start.29 = (bf16[1,384,1536]{2,1,0:T(8,128)(2,1)}, bf16[1,384,1536]{2,1,0:T(8,128)(2,1)S(1)}, u32[]{:S(2)}, u32[]{:S(2)}) collective-permute-start(bf16[1,384,1536]{2,1,0:T(8,128)(2,1)} %get-tuple-element.361), channel_id=1, source_target_pairs={{0,0},{1,1},{2,8},{3,9},{8,2},{9,3},{10,10},{11,11},{16,16},{17,17... | collective-permute-start | bytes 3538952 | tf_op jit(solution)/shard_map/ppermute | solution.py:750
  241.3 71.4 %collective-permute-start.38 = (bf16[1184,768]{1,0:T(8,128)(2,1)}, bf16[1184,768]{1,0:T(8,128)(2,1)}, u32[]{:S(2)}, u32[]{:S(2)}) collective-permute-start(bf16[1184,768]{1,0:T(8,128)(2,1)} %add_convert_fusion.11), channel_id=1, source_target_pairs={{0,1},{1,0},{2,3},{3,2},{4,5},{5,4},{6,7},{7,6},{8,9},{9,8},{10,11... | collective-permute-start | bytes 5455880 | tf_op jit(solution)/shard_map/ppermute | solution.py:744
  268.2 44.6 %collective-permute-start.36 = (bf16[1,384,1536]{2,1,0:T(8,128)(2,1)S(1)}, bf16[1,384,1536]{2,1,0:T(8,128)(2,1)}, u32[]{:S(2)}, u32[]{:S(2)}) collective-permute-start(bf16[1,384,1536]{2,1,0:T(8,128)(2,1)S(1)} %collective-permute-done.29.refs_0_), channel_id=1, source_target_pairs={{0,16},{8,24},{16,0},{24,8},{1,17},{9,25},{17,1},{25,9},{2,18},{10... | collective-permute-start | bytes 3538952 | tf_op jit(solution)/shard_map/ppermute | solution.py:741
  269.0 43.8 %collective-permute-start.37 = (bf16[1,384,1536]{2,1,0:T(8,128)(2,1)S(1)}, bf16[1,384,1536]{2,1,0:T(8,128)(2,1)}, u32[]{:S(2)}, u32[]{:S(2)}) collective-permute-start(bf16[1,384,1536]{2,1,0:T(8,128)(2,1)S(1)} %collective-permute-done.29.refs_0_), channel_id=1, source_target_pairs={{0,4},{4,0},{1,5},{5,1},{2,6},{6,2},{3,7},{7,3},{8,12},{12,8},{9,1... | collective-permute-start | bytes 3538952 | tf_op jit(solution)/shard_map/ppermute | solution.py:747
  272.0 40.7 %collective-permute-start.35 = (bf16[1184,384]{1,0:T(8,128)(2,1)}, bf16[1184,384]{1,0:T(8,128)(2,1)}, u32[]{:S(2)}, u32[]{:S(2)}) collective-permute-start(bf16[1184,384]{1,0:T(8,128)(2,1)} %fusion.33), channel_id=1, source_target_pairs={{0,0},{1,1},{2,8},{3,9},{8,2},{9,3},{10,10},{11,11},{16,16},{17,17... | collective-permute-start | bytes 2727944 | tf_op jit(solution)/shard_map/ppermute | solution.py:750
  365.5 68.2 %collective-permute-start.48 = (bf16[1184,768]{1,0:T(8,128)(2,1)}, bf16[1184,768]{1,0:T(8,128)(2,1)}, u32[]{:S(2)}, u32[]{:S(2)}) collective-permute-start(bf16[1184,768]{1,0:T(8,128)(2,1)} %add_convert_fusion.9), channel_id=1, source_target_pairs={{0,1},{1,0},{2,3},{3,2},{4,5},{5,4},{6,7},{7,6},{8,9},{9,8},{10,11... | collective-permute-start | bytes 5455880 | tf_op jit(solution)/shard_map/ppermute | solution.py:744
  382.4 51.3 %collective-permute-start.49 = (bf16[1184,384]{1,0:T(8,128)(2,1)}, bf16[1184,384]{1,0:T(8,128)(2,1)}, u32[]{:S(2)}, u32[]{:S(2)}) collective-permute-start(bf16[1184,384]{1,0:T(8,128)(2,1)} %collective-permute-done.47), channel_id=1, source_target_pairs={{0,1},{1,0},{2,3},{3,2},{4,5},{5,4},{6,7},{7,6},{8,9},{9,8},{10,11... | collective-permute-start | bytes 2727944 | tf_op jit(solution)/shard_map/ppermute | solution.py:744
  442.5 61.0 %collective-permute-start.53 = (bf16[1184,768]{1,0:T(8,128)(2,1)}, bf16[1184,768]{1,0:T(8,128)(2,1)}, u32[]{:S(2)}, u32[]{:S(2)}) collective-permute-start(bf16[1184,768]{1,0:T(8,128)(2,1)} %add_convert_fusion.7), channel_id=1, source_target_pairs={{0,1},{1,0},{2,3},{3,2},{4,5},{5,4},{6,7},{7,6},{8,9},{9,8},{10,11... | collective-permute-start | bytes 5455880 | tf_op jit(solution)/shard_map/ppermute | solution.py:744
  461.8 41.6 %collective-permute-start.54 = (bf16[320,768]{1,0:T(8,128)(2,1)S(1)}, bf16[320,768]{1,0:T(8,128)(2,1)S(1)}, u32[]{:S(2)}, u32[]{:S(2)}) collective-permute-start(bf16[320,768]{1,0:T(8,128)(2,1)S(1)} %get-tuple-element.420), channel_id=1, source_target_pairs={{0,4},{4,0},{1,5},{5,1},{2,6},{6,2},{3,7},{7,3},{8,12},{12,8},{9,1... | collective-permute-start | bytes 1474568 | tf_op jit(solution)/shard_map/ppermute | solution.py:747
  514.3 43.5 %collective-permute-start.59 = (bf16[1184,768]{1,0:T(8,128)(2,1)S(1)}, bf16[1184,768]{1,0:T(8,128)(2,1)}, u32[]{:S(2)}, u32[]{:S(2)}) collective-permute-start(bf16[1184,768]{1,0:T(8,128)(2,1)S(1)} %add_convert_fusion.5), channel_id=1, source_target_pairs={{0,1},{1,0},{2,3},{3,2},{4,5},{5,4},{6,7},{7,6},{8,9},{9,8},{10,11... | collective-permute-start | bytes 5455880 | tf_op jit(solution)/shard_map/ppermute | solution.py:744
  515.8 42.0 %collective-permute-start.58 = (bf16[320,1536]{1,0:T(8,128)(2,1)}, bf16[320,1536]{1,0:T(8,128)(2,1)}, u32[]{:S(2)}, u32[]{:S(2)}) collective-permute-start(bf16[320,1536]{1,0:T(8,128)(2,1)} %pad_maximum_fusion.2.refs_2_), channel_id=1, source_target_pairs={{0,4},{4,0},{1,5},{5,1},{2,6},{6,2},{3,7},{7,3},{8,12},{12,8},{9,1... | collective-permute-start | bytes 2949128 | tf_op jit(solution)/shard_map/ppermute | solution.py:747
  516.8 41.0 %collective-permute-start.57 = (bf16[320,768]{1,0:T(8,128)(2,1)S(1)}, bf16[320,768]{1,0:T(8,128)(2,1)}, u32[]{:S(2)}, u32[]{:S(2)}) collective-permute-start(bf16[320,768]{1,0:T(8,128)(2,1)S(1)} %get-tuple-element.443), channel_id=1, source_target_pairs={{0,4},{4,0},{1,5},{5,1},{2,6},{6,2},{3,7},{7,3},{8,12},{12,8},{9,1... | collective-permute-start | bytes 1474568 | tf_op jit(solution)/shard_map/ppermute | solution.py:747
  566.8 42.9 %collective-permute-start.63 = (bf16[320,1536]{1,0:T(8,128)(2,1)}, bf16[320,1536]{1,0:T(8,128)(2,1)}, u32[]{:S(2)}, u32[]{:S(2)}) collective-permute-start(bf16[320,1536]{1,0:T(8,128)(2,1)} %pad_maximum_fusion.4.refs_2_), channel_id=1, source_target_pairs={{0,4},{4,0},{1,5},{5,1},{2,6},{6,2},{3,7},{7,3},{8,12},{12,8},{9,1... | collective-permute-start | bytes 2949128 | tf_op jit(solution)/shard_map/ppermute | solution.py:747
  568.7 41.0 %collective-permute-start.62 = (bf16[1,768,1536]{2,1,0:T(8,128)(2,1)}, bf16[1,768,1536]{2,1,0:T(8,128)(2,1)}, u32[]{:S(2)}, u32[]{:S(2)}) collective-permute-start(bf16[1,768,1536]{2,1,0:T(8,128)(2,1)} %shard_map.415), channel_id=1, source_target_pairs={{0,16},{1,17},{2,8},{3,9},{8,2},{9,3},{10,26},{11,27},{16,0},{17,1... | collective-permute-start | bytes 7077896 | tf_op jit(solution)/shard_map/ppermute | solution.py:753
  609.7 67.5 %collective-permute-start.67 = (bf16[1,768,1536]{2,1,0:T(8,128)(2,1)}, bf16[1,768,1536]{2,1,0:T(8,128)(2,1)}, u32[]{:S(2)}, u32[]{:S(2)}) collective-permute-start(bf16[1,768,1536]{2,1,0:T(8,128)(2,1)} %shard_map.413), channel_id=1, source_target_pairs={{0,4},{4,0},{1,5},{5,1},{2,6},{6,2},{3,7},{7,3},{8,12},{12,8},{9,1... | collective-permute-start | bytes 7077896 | tf_op jit(solution)/shard_map/ppermute | solution.py:747
  617.2 60.0 %collective-permute-start.68 = (bf16[1,768,1536]{2,1,0:T(8,128)(2,1)}, bf16[1,768,1536]{2,1,0:T(8,128)(2,1)}, u32[]{:S(2)}, u32[]{:S(2)}) collective-permute-start(bf16[1,768,1536]{2,1,0:T(8,128)(2,1)} %shard_map.417), channel_id=1, source_target_pairs={{0,16},{1,17},{2,8},{3,9},{8,2},{9,3},{10,26},{11,27},{16,0},{17,1... | collective-permute-start | bytes 7077896 | tf_op jit(solution)/shard_map/ppermute | solution.py:753
  632.0 45.3 %collective-permute-start.69 = (bf16[1184,384]{1,0:T(8,128)(2,1)}, bf16[1184,384]{1,0:T(8,128)(2,1)}, u32[]{:S(2)}, u32[]{:S(2)}) collective-permute-start(bf16[1184,384]{1,0:T(8,128)(2,1)} %get-tuple-element.475), channel_id=1, source_target_pairs={{0,1},{1,0},{2,3},{3,2},{4,5},{5,4},{6,7},{7,6},{8,9},{9,8},{10,11... | collective-permute-start | bytes 2727944 | tf_op jit(solution)/shard_map/ppermute | solution.py:744
  693.9 39.5 %collective-permute-start.72 = (bf16[1,768,1536]{2,1,0:T(8,128)(2,1)}, bf16[1,768,1536]{2,1,0:T(8,128)(2,1)}, u32[]{:S(2)}, u32[]{:S(2)}) collective-permute-start(bf16[1,768,1536]{2,1,0:T(8,128)(2,1)} %shard_map.421), channel_id=1, source_target_pairs={{0,16},{1,17},{2,8},{3,9},{8,2},{9,3},{10,26},{11,27},{16,0},{17,1... | collective-permute-start | bytes 7077896 | tf_op jit(solution)/shard_map/ppermute | solution.py:753
  697.3 53.6 %collective-permute-start.75 = (bf16[1,768,1536]{2,1,0:T(8,128)(2,1)}, bf16[1,768,1536]{2,1,0:T(8,128)(2,1)}, u32[]{:S(2)}, u32[]{:S(2)}) collective-permute-start(bf16[1,768,1536]{2,1,0:T(8,128)(2,1)} %shard_map.414), channel_id=1, source_target_pairs={{0,4},{4,0},{1,5},{5,1},{2,6},{6,2},{3,7},{7,3},{8,12},{12,8},{9,1... | collective-permute-start | bytes 7077896 | tf_op jit(solution)/shard_map/ppermute | solution.py:747
  761.6 63.7 %collective-permute-start.77 = (bf16[1,768,1536]{2,1,0:T(8,128)(2,1)}, bf16[1,768,1536]{2,1,0:T(8,128)(2,1)}, u32[]{:S(2)}, u32[]{:S(2)}) collective-permute-start(bf16[1,768,1536]{2,1,0:T(8,128)(2,1)} %shard_map.423), channel_id=1, source_target_pairs={{0,16},{1,17},{2,8},{3,9},{8,2},{9,3},{10,26},{11,27},{16,0},{17,1... | collective-permute-start | bytes 7077896 | tf_op jit(solution)/shard_map/ppermute | solution.py:753
  846.5 41.3 %collective-permute-start.86 = (bf16[3,768,384]{2,1,0:T(8,128)(2,1)}, bf16[3,768,384]{2,1,0:T(8,128)(2,1)}, u32[]{:S(2)}, u32[]{:S(2)}) collective-permute-start(bf16[3,768,384]{2,1,0:T(8,128)(2,1)} %shard_map.424), channel_id=1, source_target_pairs={{0,4},{4,0},{1,5},{5,1},{2,6},{6,2},{3,7},{7,3},{8,12},{12,8},{9,1... | collective-permute-start | bytes 5308424 | tf_op jit(solution)/shard_map/ppermute | solution.py:747
  847.7 40.1 %collective-permute-start.83 = (bf16[3,768,384]{2,1,0:T(8,128)(2,1)}, bf16[3,768,384]{2,1,0:T(8,128)(2,1)}, u32[]{:S(2)}, u32[]{:S(2)}) collective-permute-start(bf16[3,768,384]{2,1,0:T(8,128)(2,1)} %shard_map.428), channel_id=1, source_target_pairs={{0,16},{1,17},{2,8},{3,9},{8,2},{9,3},{10,26},{11,27},{16,0},{17,1... | collective-permute-start | bytes 5308424 | tf_op jit(solution)/shard_map/ppermute | solution.py:753
  854.9 42.2 %collective-permute-start.84 = (bf16[1184,384]{1,0:T(8,128)(2,1)}, bf16[1184,384]{1,0:T(8,128)(2,1)S(1)}, u32[]{:S(2)}, u32[]{:S(2)}) collective-permute-start(bf16[1184,384]{1,0:T(8,128)(2,1)} %get-tuple-element.533), channel_id=1, source_target_pairs={{0,1},{1,0},{2,3},{3,2},{4,5},{5,4},{6,7},{7,6},{8,9},{9,8},{10,11... | collective-permute-start | bytes 2727944 | tf_op jit(solution)/shard_map/ppermute | solution.py:744
  874.5 39.9 %collective-permute-start.88 = (bf16[1184,384]{1,0:T(8,128)(2,1)}, bf16[1184,384]{1,0:T(8,128)(2,1)}, u32[]{:S(2)}, u32[]{:S(2)}) collective-permute-start(bf16[1184,384]{1,0:T(8,128)(2,1)} %fusion.18), channel_id=1, source_target_pairs={{0,16},{1,17},{2,8},{3,9},{8,2},{9,3},{10,26},{11,27},{16,0},{17,1... | collective-permute-start | bytes 2727944 | tf_op jit(solution)/shard_map/ppermute | solution.py:753
  908.1 45.2 %collective-permute-start.93 = (bf16[3,768,384]{2,1,0:T(8,128)(2,1)}, bf16[3,768,384]{2,1,0:T(8,128)(2,1)}, u32[]{:S(2)}, u32[]{:S(2)}) collective-permute-start(bf16[3,768,384]{2,1,0:T(8,128)(2,1)} %shard_map.432), channel_id=1, source_target_pairs={{0,16},{1,17},{2,8},{3,9},{8,2},{9,3},{10,26},{11,27},{16,0},{17,1... | collective-permute-start | bytes 5308424 | tf_op jit(solution)/shard_map/ppermute | solution.py:753
  953.3 40.0 %collective-permute-start.95 = (bf16[2,1,192,1536]{3,2,1,0:T(8,128)(2,1)}, bf16[2,1,192,1536]{3,2,1,0:T(8,128)(2,1)}, u32[]{:S(2)}, u32[]{:S(2)}) collective-permute-start(bf16[2,1,192,1536]{3,2,1,0:T(8,128)(2,1)} %get-tuple-element.566), channel_id=1, source_target_pairs={{0,8},{8,0},{16,24},{24,16},{1,9},{9,1},{17,25},{25,17},{2,10},{10... | collective-permute-start | bytes 3538952 | tf_op jit(solution)/shard_map/ppermute | solution.py:738
  (177 other events, 2605.8 us)

commit v4 on v3

--- a/solution.py
+++ b/solution.py
@@ -1216,10 +1216,11 @@
             backward(1)
             out = step(lambda a: input_partial(ids, a, *wq, image_len), gqkvs[0])
             optimize(7)
-            sync(sent[3], grads[6], branch_mine[1])
+            sync(sent[3], branch_mine[1])
+            grads[3] = keep_half(3, sent[3])
+            sync(grads[6])
             half = half_start(*out)
             send_update(7)
-            grads[3] = keep_half(3, sent[3])
             gh1_mine.append(own_part(half()))
             small_sum(7)
             sent[2] = over_y(sent_two)
@@ -1235,7 +1236,7 @@
             fill_mixing()
             text_rights[0] = text_right(0)
             optimize(6)
-            sync(grads[2], totals[0], text_rights[0], results[0])
+            sync(grads[2], totals[0], text_rights[0])
             half = half_start(*out)
             send_update(6)
             totals[0] = row_total(*totals[0])
@@ -1246,7 +1247,7 @@
             row_grads(0, *totals[0])
             optimize(3)
             sent_text, sent_one = give_later(1, None, 1), give_later(1)
-            sync(grads[4], gh1_mine[1], waiting[6], sent[0])
+            sync(grads[4], gh1_mine[1], waiting[6], sent[0], results[0])
             send_update(3)
             grads[0] = keep_half(0, sent[0])
             results.append(owned(res[1]))
@@ -1255,29 +1256,31 @@
             small_sum(3)
             finish(6)
             optimize(2)
+            sync(totals[1], sent[5], sent[1], grads_x[0])
+            grads[5] = keep_half(1, sent[5], 1)
+            grads[1] = keep_half(1, sent[1])
             optimize(4)
-            sync(totals[1], sent[5], sent[1], grads[0], waiting[3], results[1], grads_x[0])
+            sync(grads[0], waiting[3], results[1], grads[5], grads[1])
             totals[1] = row_total(*totals[1])
             send_update(2)
             send_update(4)
-            grads[5] = keep_half(1, sent[5], 1)
-            grads[1] = keep_half(1, sent[1])
+            finish(3)
             small_sum(2)
             small_sum(4)
             row_grads(1, *totals[1])
-            finish(3)
             optimize(0)
-            sync(waiting[2], waiting[4], grads[5], grads[1])
-            send_update(0)
             optimize(5)
             optimize(1)
-            small_sum(0)
+            sync(waiting[2], waiting[4])
+            send_update(0)
             send_update(5)
             send_update(1)
+            small_sum(0)
+            small_sum(5)
+            small_sum(1)
             finish(2)
             finish(4)
-            small_sum(5)
-            small_sum(1)
+            sync(waiting[0], waiting[5], waiting[1])
             for i in (0, 5, 1):
                 finish(i)
         else:

time: 1110 us -> 1100 us (level)
  starting transfers between devices: 196 us -> 180 us
    ppermute x29, starting transfers between devices: 79.3 us -> 61.8 us  [core_swap(): return lax.ppermute(a, 'group', core_perm)]
    ppermute x15, waiting for transfers between devices: 75.7 us -> 88.5 us  [z_swap(): return lax.ppermute(a, 'mp', z_perm)]
    ppermute x19, waiting for transfers between devices: 47.8 us -> 36.7 us  [x_swap(): return lax.ppermute(a, 'group', x_perm)]
    unnamed x204 -> x242, local copies, waits for them, and re-layouts: 32.8 us -> 29.9 us
  transfers between devices with their start and end apart: 110 -> 110, of which waited for: 27 -> 28; matrix products, arithmetic and copies ran while one was open for 11% -> 12% of each run, Pallas kernels for 49% -> 48%
where the time goes in v4:
time: 1100 us; the launch traced here: 1090 us
  Pallas kernels  561 us (51%)
  starting transfers between devices  180 us (16%)
  waiting for transfers between devices  177 us (16%)
  other arithmetic  95.1 us (9%)
  local copies, waits for them, and re-layouts  68.8 us (6%)
    pallas_call x13, Pallas kernels, weight_grad(): call(kernel, (steps,), [left_spec] * n + [right_spec] * n + [out_spec] *...  102 us
    ppermute x15, waiting for transfers between devices, z_swap(): return lax.ppermute(a, 'mp', z_perm)  88.5 us
    pallas_call x2, Pallas kernels, mlp(): call(kernel, (steps,), [whole((rows, width)), whole((rows, width)), w1_sp...  81.4 us
    pallas_call x8, Pallas kernels, adam(): call(kernel, (4,), [pairs, grad, grad], [pairs, pl.BlockSpec((1, lead, pi...  75.9 us
    pallas_call x2, Pallas kernels, attend_back(): pl.pallas_call(kernel, grid=(pairs,), in_specs=[pl.BlockSpec((3, rows, 12...  65.9 us
    ppermute x29, starting transfers between devices, core_swap(): return lax.ppermute(a, 'group', core_perm)  61.8 us
    ppermute x13, starting transfers between devices, turn(): return lax.ppermute(a, ('group', 'mp'), turn_perm)  49.1 us
    pallas_call x2, Pallas kernels, attend(): pl.pallas_call(kernel, grid=(pairs,), in_specs=[pl.BlockSpec((3, rows, 12...  44.3 us
  transfers between devices with their start and end apart: 110, of which 28 were waited for; matrix products, arithmetic and copies ran while one was open for 12% of the time, Pallas kernels for 48%

profile of v4, /device:TPU:0, one launch (start us, length us, event | category | flops | bytes accessed | tf_op | source)
XLA Modules:
  0.0 1087.4 jit_solution(9936116567253946274)
XLA Ops:
  43.5 13.4 %collective-permute-done.8.refs_1_ = bf16[3,384,384]{2,1,0:T(8,128)(2,1)} collective-permute-done((bf16[3,384,384]{2,1,0:T(8,128)(2,1)S(1)}, bf16[3,384,384]{2,1,0:T(8,128)(2,1)}, u32[]{:S(2)}, u32[]{:S(2)}) %collective-permute-start.8) | collective-permute-done | bytes 884768 | tf_op jit(solution)/shard_map/ppermute | solution.py:741
  63.5 17.6 %collective-permute-done.13 = f32[32,384]{1,0:T(8,128)S(1)} collective-permute-done((f32[32,384]{1,0:T(8,128)S(1)}, f32[32,384]{1,0:T(8,128)S(1)}, u32[]{:S(2)}, u32[]{:S(2)}) %collective-permute-start.13) | collective-permute-done | bytes 49184 | tf_op jit(solution)/shard_map/ppermute | solution.py:744
  83.6 19.5 %collective-permute-start.15 = (bf16[1184,768]{1,0:T(8,128)(2,1)S(1)}, bf16[1184,768]{1,0:T(8,128)(2,1)}, u32[]{:S(2)}, u32[]{:S(2)}) collective-permute-start(bf16[1184,768]{1,0:T(8,128)(2,1)S(1)} %maximum_select_fusion.xm_ref), channel_id=1, source_target_pairs={{0,8},{8,0},{16,24},{24,16},{1,9},{9,1},{17,25},{25,17},{2,10},{10... | collective-permute-start | bytes 5455880 | tf_op jit(solution)/shard_map/ppermute | solution.py:738
  122.8 15.3 %shard_map.396 = (bf16[1184,1536]{1,0:T(8,128)(2,1)}, bf16[3,1184,384]{2,1,0:T(8,128)(2,1)}, f32[1184,384]{1,0:T(8,128)}, f32[1184,128]{1,0:T(8,128)}) custom-call(s32[10]{0:T(128)} %stack.170.ids_ref, bf16[1184,768]{1,0:T(8,128)(2,1)} %copy-done.25, bf16[1184,768]{1,0:T(8,128)(2,1)} %collective-permute-done.15.xo_ref, ...), custom_call_target="tpu_custom_call" | custom-call | flops 4190109 | bytes 17989 | tf_op jit(solution)/shard_map/pallas_call | solution.py:191
  163.8 22.2 %shard_map.399 = (bf16[1184,384]{1,0:T(8,128)(2,1)}, f32[3,8,1280]{2,1,0:T(8,128)}) custom-call(bf16[3,1184,384]{2,1,0:T(8,128)(2,1)} %get-tuple-element.456.qkv_ref), custom_call_target="tpu_custom_call" | custom-call | flops 8613003 | bytes 3637 | tf_op jit(solution)/shard_map/pallas_call | solution.py:248
  202.1 31.0 %collective-permute-done.30 = bf16[1184,384]{1,0:T(8,128)(2,1)S(1)} collective-permute-done((bf16[1184,384]{1,0:T(8,128)(2,1)}, bf16[1184,384]{1,0:T(8,128)(2,1)S(1)}, u32[]{:S(2)}, u32[]{:S(2)}) %collective-permute-start.30) | collective-permute-done | bytes 909344 | tf_op jit(solution)/shard_map/ppermute | solution.py:744
  242.6 15.4 %shard_map.401 = (bf16[1184,1536]{1,0:T(8,128)(2,1)}, bf16[3,1184,384]{2,1,0:T(8,128)(2,1)}, f32[1184,384]{1,0:T(8,128)}, f32[1184,128]{1,0:T(8,128)}) custom-call(s32[10]{0:T(128)} %stack.170.ids_ref, bf16[1184,768]{1,0:T(8,128)(2,1)} %copy-done.24, bf16[1184,768]{1,0:T(8,128)(2,1)} %collective-permute-done.31.xo_ref, ...), custom_call_target="tpu_custom_call" | custom-call | flops 4190109 | bytes 17989 | tf_op jit(solution)/shard_map/pallas_call | solution.py:191
  290.6 22.2 %shard_map.404 = (bf16[1184,384]{1,0:T(8,128)(2,1)}, f32[3,8,1280]{2,1,0:T(8,128)}) custom-call(bf16[3,1184,384]{2,1,0:T(8,128)(2,1)} %get-tuple-element.484.qkv_ref), custom_call_target="tpu_custom_call" | custom-call | flops 8613003 | bytes 3637 | tf_op jit(solution)/shard_map/pallas_call | solution.py:248
  327.8 17.1 %collective-permute-done.42 = bf16[1184,384]{1,0:T(8,128)(2,1)S(1)} collective-permute-done((bf16[1184,384]{1,0:T(8,128)(2,1)}, bf16[1184,384]{1,0:T(8,128)(2,1)S(1)}, u32[]{:S(2)}, u32[]{:S(2)}) %collective-permute-start.42) | collective-permute-done | bytes 909344 | tf_op jit(solution)/shard_map/ppermute | solution.py:744
  368.2 11.7 %shard_map.406 = (bf16[1184,1536]{1,0:T(8,128)(2,1)}, bf16[1184,1536]{1,0:T(8,128)(2,1)}, f32[1184,384]{1,0:T(8,128)}) custom-call(s32[10]{0:T(128)} %stack.170.ids_ref, f32[1]{0:T(128)} %bitcast.20.live_ref, bf16[1184,768]{1,0:T(8,128)(2,1)} %copy-done.25, bf16[1184,768]{1,0:T(8,128)(2,1)} %collective-permute-done.15.xo_ref, bf16[1184,768]{1,0:T(8,128)(2,1)} %copy-done.29, ...), custom_call_target="tpu_custom_call" | custom-call | flops 36372 | bytes 20004 | tf_op jit(solution)/shard_map/pallas_call | solution.py:426
  393.0 40.6 %shard_map.409 = (bf16[1184,1536]{1,0:T(8,128)(2,1)}, bf16[1184,1536]{1,0:T(8,128)(2,1)}, bf16[1184,768]{1,0:T(8,128)(2,1)}, bf16[1184,768]{1,0:T(8,128)(2,1)}, ...) custom-call(s32[10]{0:T(128)} %stack.170.ids_ref, bf16[1184,1536]{1,0:T(8,128)(2,1)} %get-tuple-element.491.h_ref.refs_0_, ...), custom_call_target="tpu_custom_call" | custom-call | flops 22347252 | bytes 40697 | tf_op jit(solution)/shard_map/pallas_call | solution.py:498
  446.8 11.7 %shard_map.410 = (bf16[1184,1536]{1,0:T(8,128)(2,1)}, bf16[1184,1536]{1,0:T(8,128)(2,1)}, f32[1184,384]{1,0:T(8,128)}) custom-call(s32[10]{0:T(128)} %stack.170.ids_ref, f32[1]{0:T(128)} %bitcast.35.live_ref, bf16[1184,768]{1,0:T(8,128)(2,1)} %copy-done.24, bf16[1184,768]{1,0:T(8,128)(2,1)} %collective-permute-done.31.xo_ref, ...), custom_call_target="tpu_custom_call" | custom-call | flops 36372 | bytes 20004 | tf_op jit(solution)/shard_map/pallas_call | solution.py:426
  462.5 40.8 %shard_map.411 = (bf16[1184,1536]{1,0:T(8,128)(2,1)}, bf16[1184,1536]{1,0:T(8,128)(2,1)}, bf16[1184,768]{1,0:T(8,128)(2,1)}, bf16[1184,768]{1,0:T(8,128)(2,1)}, ...) custom-call(s32[10]{0:T(128)} %stack.170.ids_ref, bf16[1184,1536]{1,0:T(8,128)(2,1)} %get-tuple-element.492.h_ref.refs_1_, ...), custom_call_target="tpu_custom_call" | custom-call | flops 22347252 | bytes 40697 | tf_op jit(solution)/shard_map/pallas_call | solution.py:498
  517.6 15.2 %shard_map.412 = (bf16[1184,1536]{1,0:T(8,128)(2,1)}, bf16[1184,384]{1,0:T(8,128)(2,1)}, f32[1184,384]{1,0:T(8,128)}, f32[2,24,384]{2,1,0:T(8,128)}) custom-call(s32[10]{0:T(128)} %stack.170.ids_ref, f32[1]{0:T(128)} %bitcast.20.live_ref, bf16[1184,768]{1,0:T(8,128)(2,1)} %copy-done.25, bf16[1184,768]{1,0:T(8,128)(2,1)} %collective-permute-done.15.xo_ref, ...), custom_call_target="tpu_custom_call" | custom-call | flops 1396703 | bytes 21823 | tf_op jit(solution)/shard_map/pallas_call | solution.py:570
  532.8 9.6 shard_map.413
  577.0 32.9 %shard_map.416.a_ref.refs_2_ = bf16[3,1184,384]{2,1,0:T(8,128)(2,1)} custom-call(bf16[3,1184,384]{2,1,0:T(8,128)(2,1)} %get-tuple-element.456.qkv_ref, bf16[1184,384]{1,0:T(8,128)(2,1)} %get-tuple-element.457.grad_ref, f32[3,8,1280]{2,1,0:T(8,128)} %get-tuple-element.458.lse_ref), custom_call_target="tpu_custom_call" | custom-call | flops 21532508 | bytes 6365 | tf_op jit(solution)/shard_map/pallas_call | solution.py:295
  618.5 11.7 %collective-permute-start.66 = (bf16[1184,768]{1,0:T(8,128)(2,1)S(1)}, bf16[1184,768]{1,0:T(8,128)(2,1)}, u32[]{:S(2)}, u32[]{:S(2)}) collective-permute-start(bf16[1184,768]{1,0:T(8,128)(2,1)S(1)} %add_convert_fusion.4.gm_ref), channel_id=1, source_target_pairs={{0,8},{8,0},{16,24},{24,16},{1,9},{9,1},{17,25},{25,17},{2,10},{10... | collective-permute-start | bytes 5455880 | tf_op jit(solution)/shard_map/ppermute | solution.py:738
  638.9 15.4 %shard_map.418 = (bf16[1184,1536]{1,0:T(8,128)(2,1)}, bf16[1184,384]{1,0:T(8,128)(2,1)}, f32[1184,384]{1,0:T(8,128)}, f32[2,24,384]{2,1,0:T(8,128)}) custom-call(s32[10]{0:T(128)} %stack.170.ids_ref, f32[1]{0:T(128)} %bitcast.35.live_ref, bf16[1184,768]{1,0:T(8,128)(2,1)} %copy-done.24, bf16[1184,768]{1,0:T(8,128)(2,1)} %collective-permute-done.31.xo_ref, ...), custom_call_target="tpu_custom_call" | custom-call | flops 1396703 | bytes 21823 | tf_op jit(solution)/shard_map/pallas_call | solution.py:570
  654.3 11.9 %shard_map.419 = (bf16[1184,768]{1,0:T(8,128)(2,1)}, bf16[1184,768]{1,0:T(8,128)(2,1)}) custom-call(s32[10]{0:T(128)} %stack.170.ids_ref, bf16[3,1184,384]{2,1,0:T(8,128)(2,1)} %shard_map.416.a_ref.refs_2_, bf16[3,1536,384]{2,1,0:T(8,128)(2,1)} %copy-done, bf16[3,1536,384]{2,1,0:T(8,128)(2,1)} %copy-done.1), custom_call_target="tpu_custom_call" | custom-call | flops 4190109 | bytes 16171 | tf_op jit(solution)/shard_map/pallas_call | solution.py:376
  666.2 11.5 %shard_map.420 = (f32[2,1,4,192,1536]{4,3,2,1,0:T(8,128)}, bf16[2,1,192,1536]{3,2,1,0:T(8,128)(2,1)}, bf16[2,1,192,1536]{3,2,1,0:T(8,128)(2,1)}) custom-call(s32[10]{0:T(128)} %stack.170.ids_ref, f32[1]{0:T(128)} %bitcast.36.inv_ref, f32[2,1,4,192,1536]{4,3,2,1,0:T(8,128)} %bitcast.175, bf16[1,4,192,1536]{3,2,1,0:T(8,128)(2,1)} %bitcast.190, ...), custom_call_target="tpu_custom_call" | custom-call | flops 23592 | bytes 23592 | tf_op jit(solution)/shard_map/pallas_call | solution.py:677
  677.8 10.5 shard_map.421
  700.1 33.0 %shard_map.422.refs_3_.a_ref = bf16[3,1184,384]{2,1,0:T(8,128)(2,1)} custom-call(bf16[3,1184,384]{2,1,0:T(8,128)(2,1)} %get-tuple-element.484.qkv_ref, bf16[1184,384]{1,0:T(8,128)(2,1)} %get-tuple-element.485.grad_ref, f32[3,8,1280]{2,1,0:T(8,128)} %get-tuple-element.486.lse_ref), custom_call_target="tpu_custom_call" | custom-call | flops 21532508 | bytes 6365 | tf_op jit(solution)/shard_map/pallas_call | solution.py:295
  733.1 12.6 %collective-permute-done.73 = bf16[1184,384]{1,0:T(8,128)(2,1)S(1)} collective-permute-done((bf16[1184,384]{1,0:T(8,128)(2,1)}, bf16[1184,384]{1,0:T(8,128)(2,1)S(1)}, u32[]{:S(2)}, u32[]{:S(2)}) %collective-permute-start.73) | collective-permute-done | bytes 909344 | tf_op jit(solution)/shard_map/ppermute | solution.py:744
  749.9 10.7 shard_map.423
  775.2 11.9 %shard_map.425 = (bf16[1184,768]{1,0:T(8,128)(2,1)}, bf16[1184,768]{1,0:T(8,128)(2,1)}) custom-call(s32[10]{0:T(128)} %stack.170.ids_ref, bf16[3,1184,384]{2,1,0:T(8,128)(2,1)} %shard_map.422.refs_3_.a_ref, bf16[3,1536,384]{2,1,0:T(8,128)(2,1)} %copy-done, bf16[3,1536,384]{2,1,0:T(8,128)(2,1)} %copy-done.1), custom_call_target="tpu_custom_call" | custom-call | flops 4190109 | bytes 16171 | tf_op jit(solution)/shard_map/pallas_call | solution.py:376
  808.3 11.5 %shard_map.427 = (f32[2,1,4,192,1536]{4,3,2,1,0:T(8,128)}, bf16[2,1,192,1536]{3,2,1,0:T(8,128)(2,1)}, bf16[2,1,192,1536]{3,2,1,0:T(8,128)(2,1)}) custom-call(s32[10]{0:T(128)} %stack.170.ids_ref, f32[1]{0:T(128)} %bitcast.36.inv_ref, f32[2,1,4,192,1536]{4,3,2,1,0:T(8,128)} %bitcast.176, bf16[1,4,192,1536]{3,2,1,0:T(8,128)(2,1)} %bitcast.189, ...), custom_call_target="tpu_custom_call" | custom-call | flops 23592 | bytes 23592 | tf_op jit(solution)/shard_map/pallas_call | solution.py:677
  851.4 11.7 %shard_map.429 = (f32[2,1,4,192,1536]{4,3,2,1,0:T(8,128)}, bf16[2,1,192,1536]{3,2,1,0:T(8,128)(2,1)}, bf16[2,1,192,1536]{3,2,1,0:T(8,128)(2,1)}) custom-call(s32[10]{0:T(128)} %stack.170.ids_ref, f32[1]{0:T(128)} %bitcast.36.inv_ref, f32[2,1,4,192,1536]{4,3,2,1,0:T(8,128)} %bitcast.177, bf16[1,4,192,1536]{3,2,1,0:T(8,128)(2,1)} %bitcast.188, ...), custom_call_target="tpu_custom_call" | custom-call | flops 23592 | bytes 23592 | tf_op jit(solution)/shard_map/pallas_call | solution.py:677
  881.0 10.2 collective-permute-done.84
  891.2 10.0 shard_map.432
  901.2 11.4 %collective-permute-start.89 = (bf16[2,1,192,1536]{3,2,1,0:T(8,128)(2,1)}, bf16[2,1,192,1536]{3,2,1,0:T(8,128)(2,1)}, u32[]{:S(2)}, u32[]{:S(2)}) collective-permute-start(bf16[2,1,192,1536]{3,2,1,0:T(8,128)(2,1)} %get-tuple-element.547), channel_id=1, source_target_pairs={{0,8},{8,0},{16,24},{24,16},{1,9},{9,1},{17,25},{25,17},{2,10},{10... | collective-permute-start | bytes 3538952 | tf_op jit(solution)/shard_map/ppermute | solution.py:738
  928.4 11.5 %shard_map.434 = (f32[2,1,4,192,1536]{4,3,2,1,0:T(8,128)}, bf16[2,1,192,1536]{3,2,1,0:T(8,128)(2,1)}, bf16[2,1,192,1536]{3,2,1,0:T(8,128)(2,1)}) custom-call(s32[10]{0:T(128)} %stack.170.ids_ref, f32[1]{0:T(128)} %bitcast.36.inv_ref, f32[2,1,4,192,1536]{4,3,2,1,0:T(8,128)} %bitcast.178, bf16[1,4,192,1536]{3,2,1,0:T(8,128)(2,1)} %bitcast.187, ...), custom_call_target="tpu_custom_call" | custom-call | flops 23592 | bytes 23592 | tf_op jit(solution)/shard_map/pallas_call | solution.py:677
  985.7 11.2 %collective-permute-start.97 = (bf16[2,1,192,1536]{3,2,1,0:T(8,128)(2,1)}, bf16[2,1,192,1536]{3,2,1,0:T(8,128)(2,1)}, u32[]{:S(2)}, u32[]{:S(2)}) collective-permute-start(bf16[2,1,192,1536]{3,2,1,0:T(8,128)(2,1)} %get-tuple-element.569), channel_id=1, source_target_pairs={{0,8},{8,0},{16,24},{24,16},{1,9},{9,1},{17,25},{25,17},{2,10},{10... | collective-permute-start | bytes 3538952 | tf_op jit(solution)/shard_map/ppermute | solution.py:738
  (652 shorter events, 539.5 us)
Async XLA Ops:
  61.6 41.4 %collective-permute-start.14 = (bf16[2,96,1536]{2,1,0:T(8,128)(2,1)}, bf16[2,96,1536]{2,1,0:T(8,128)(2,1)S(1)}, u32[]{:S(2)}, u32[]{:S(2)}) collective-permute-start(bf16[2,96,1536]{2,1,0:T(8,128)(2,1)} %get-tuple-element.333), channel_id=1, source_target_pairs={{0,0},{1,1},{2,8},{3,9},{8,2},{9,3},{10,10},{11,11},{16,16},{17,17... | collective-permute-start | bytes 1769480 | tf_op jit(solution)/shard_map/ppermute | solution.py:750
  140.3 52.9 %collective-permute-start.25 = (bf16[1,384,1536]{2,1,0:T(8,128)(2,1)}, bf16[1,384,1536]{2,1,0:T(8,128)(2,1)S(1)}, u32[]{:S(2)}, u32[]{:S(2)}) collective-permute-start(bf16[1,384,1536]{2,1,0:T(8,128)(2,1)} %get-tuple-element.355), channel_id=1, source_target_pairs={{0,0},{1,1},{2,8},{3,9},{8,2},{9,3},{10,10},{11,11},{16,16},{17,17... | collective-permute-start | bytes 3538952 | tf_op jit(solution)/shard_map/ppermute | solution.py:750
  148.5 44.8 %collective-permute-start.23 = (bf16[1,384,1536]{2,1,0:T(8,128)(2,1)S(1)}, bf16[1,384,1536]{2,1,0:T(8,128)(2,1)S(1)}, u32[]{:S(2)}, u32[]{:S(2)}) collective-permute-start(bf16[1,384,1536]{2,1,0:T(8,128)(2,1)S(1)} %collective-permute-done.19.refs_0_), channel_id=1, source_target_pairs={{0,16},{8,24},{16,0},{24,8},{1,17},{9,25},{17,1},{25,9},{2,18},{10... | collective-permute-start | bytes 3538952 | tf_op jit(solution)/shard_map/ppermute | solution.py:741
  149.4 44.9 %collective-permute-start.24 = (bf16[1,384,1536]{2,1,0:T(8,128)(2,1)S(1)}, bf16[1,384,1536]{2,1,0:T(8,128)(2,1)}, u32[]{:S(2)}, u32[]{:S(2)}) collective-permute-start(bf16[1,384,1536]{2,1,0:T(8,128)(2,1)S(1)} %collective-permute-done.19.refs_0_), channel_id=1, source_target_pairs={{0,4},{4,0},{1,5},{5,1},{2,6},{6,2},{3,7},{7,3},{8,12},{12,8},{9,1... | collective-permute-start | bytes 3538952 | tf_op jit(solution)/shard_map/ppermute | solution.py:747
  151.5 41.7 %collective-permute-start.22 = (bf16[1184,384]{1,0:T(8,128)(2,1)}, bf16[1184,384]{1,0:T(8,128)(2,1)}, u32[]{:S(2)}, u32[]{:S(2)}) collective-permute-start(bf16[1184,384]{1,0:T(8,128)(2,1)} %fusion.34), channel_id=1, source_target_pairs={{0,0},{1,1},{2,8},{3,9},{8,2},{9,3},{10,10},{11,11},{16,16},{17,17... | collective-permute-start | bytes 2727944 | tf_op jit(solution)/shard_map/ppermute | solution.py:750
  241.3 71.5 %collective-permute-start.38 = (bf16[1184,768]{1,0:T(8,128)(2,1)}, bf16[1184,768]{1,0:T(8,128)(2,1)}, u32[]{:S(2)}, u32[]{:S(2)}) collective-permute-start(bf16[1184,768]{1,0:T(8,128)(2,1)} %add_convert_fusion.11), channel_id=1, source_target_pairs={{0,1},{1,0},{2,3},{3,2},{4,5},{5,4},{6,7},{7,6},{8,9},{9,8},{10,11... | collective-permute-start | bytes 5455880 | tf_op jit(solution)/shard_map/ppermute | solution.py:744
  268.2 44.6 %collective-permute-start.36 = (bf16[1,384,1536]{2,1,0:T(8,128)(2,1)S(1)}, bf16[1,384,1536]{2,1,0:T(8,128)(2,1)}, u32[]{:S(2)}, u32[]{:S(2)}) collective-permute-start(bf16[1,384,1536]{2,1,0:T(8,128)(2,1)S(1)} %collective-permute-done.29.refs_0_), channel_id=1, source_target_pairs={{0,16},{8,24},{16,0},{24,8},{1,17},{9,25},{17,1},{25,9},{2,18},{10... | collective-permute-start | bytes 3538952 | tf_op jit(solution)/shard_map/ppermute | solution.py:741
  268.9 43.8 %collective-permute-start.37 = (bf16[1,384,1536]{2,1,0:T(8,128)(2,1)S(1)}, bf16[1,384,1536]{2,1,0:T(8,128)(2,1)}, u32[]{:S(2)}, u32[]{:S(2)}) collective-permute-start(bf16[1,384,1536]{2,1,0:T(8,128)(2,1)S(1)} %collective-permute-done.29.refs_0_), channel_id=1, source_target_pairs={{0,4},{4,0},{1,5},{5,1},{2,6},{6,2},{3,7},{7,3},{8,12},{12,8},{9,1... | collective-permute-start | bytes 3538952 | tf_op jit(solution)/shard_map/ppermute | solution.py:747
  272.1 40.6 %collective-permute-start.35 = (bf16[1184,384]{1,0:T(8,128)(2,1)}, bf16[1184,384]{1,0:T(8,128)(2,1)}, u32[]{:S(2)}, u32[]{:S(2)}) collective-permute-start(bf16[1184,384]{1,0:T(8,128)(2,1)} %fusion.33), channel_id=1, source_target_pairs={{0,0},{1,1},{2,8},{3,9},{8,2},{9,3},{10,10},{11,11},{16,16},{17,17... | collective-permute-start | bytes 2727944 | tf_op jit(solution)/shard_map/ppermute | solution.py:750
  365.4 68.1 %collective-permute-start.48 = (bf16[1184,768]{1,0:T(8,128)(2,1)}, bf16[1184,768]{1,0:T(8,128)(2,1)}, u32[]{:S(2)}, u32[]{:S(2)}) collective-permute-start(bf16[1184,768]{1,0:T(8,128)(2,1)} %add_convert_fusion.9), channel_id=1, source_target_pairs={{0,1},{1,0},{2,3},{3,2},{4,5},{5,4},{6,7},{7,6},{8,9},{9,8},{10,11... | collective-permute-start | bytes 5455880 | tf_op jit(solution)/shard_map/ppermute | solution.py:744
  382.4 51.2 %collective-permute-start.49 = (bf16[1184,384]{1,0:T(8,128)(2,1)}, bf16[1184,384]{1,0:T(8,128)(2,1)}, u32[]{:S(2)}, u32[]{:S(2)}) collective-permute-start(bf16[1184,384]{1,0:T(8,128)(2,1)} %collective-permute-done.47), channel_id=1, source_target_pairs={{0,1},{1,0},{2,3},{3,2},{4,5},{5,4},{6,7},{7,6},{8,9},{9,8},{10,11... | collective-permute-start | bytes 2727944 | tf_op jit(solution)/shard_map/ppermute | solution.py:744
  442.3 61.1 %collective-permute-start.53 = (bf16[1184,768]{1,0:T(8,128)(2,1)}, bf16[1184,768]{1,0:T(8,128)(2,1)}, u32[]{:S(2)}, u32[]{:S(2)}) collective-permute-start(bf16[1184,768]{1,0:T(8,128)(2,1)} %add_convert_fusion.7), channel_id=1, source_target_pairs={{0,1},{1,0},{2,3},{3,2},{4,5},{5,4},{6,7},{7,6},{8,9},{9,8},{10,11... | collective-permute-start | bytes 5455880 | tf_op jit(solution)/shard_map/ppermute | solution.py:744
  461.6 41.7 %collective-permute-start.54 = (bf16[320,768]{1,0:T(8,128)(2,1)S(1)}, bf16[320,768]{1,0:T(8,128)(2,1)S(1)}, u32[]{:S(2)}, u32[]{:S(2)}) collective-permute-start(bf16[320,768]{1,0:T(8,128)(2,1)S(1)} %get-tuple-element.420), channel_id=1, source_target_pairs={{0,4},{4,0},{1,5},{5,1},{2,6},{6,2},{3,7},{7,3},{8,12},{12,8},{9,1... | collective-permute-start | bytes 1474568 | tf_op jit(solution)/shard_map/ppermute | solution.py:747
  514.2 43.4 %collective-permute-start.59 = (bf16[1184,768]{1,0:T(8,128)(2,1)S(1)}, bf16[1184,768]{1,0:T(8,128)(2,1)}, u32[]{:S(2)}, u32[]{:S(2)}) collective-permute-start(bf16[1184,768]{1,0:T(8,128)(2,1)S(1)} %add_convert_fusion.5), channel_id=1, source_target_pairs={{0,1},{1,0},{2,3},{3,2},{4,5},{5,4},{6,7},{7,6},{8,9},{9,8},{10,11... | collective-permute-start | bytes 5455880 | tf_op jit(solution)/shard_map/ppermute | solution.py:744
  515.6 42.0 %collective-permute-start.58 = (bf16[320,1536]{1,0:T(8,128)(2,1)}, bf16[320,1536]{1,0:T(8,128)(2,1)}, u32[]{:S(2)}, u32[]{:S(2)}) collective-permute-start(bf16[320,1536]{1,0:T(8,128)(2,1)} %pad_maximum_fusion.2.refs_2_), channel_id=1, source_target_pairs={{0,4},{4,0},{1,5},{5,1},{2,6},{6,2},{3,7},{7,3},{8,12},{12,8},{9,1... | collective-permute-start | bytes 2949128 | tf_op jit(solution)/shard_map/ppermute | solution.py:747
  516.8 40.8 %collective-permute-start.57 = (bf16[320,768]{1,0:T(8,128)(2,1)S(1)}, bf16[320,768]{1,0:T(8,128)(2,1)}, u32[]{:S(2)}, u32[]{:S(2)}) collective-permute-start(bf16[320,768]{1,0:T(8,128)(2,1)S(1)} %get-tuple-element.443), channel_id=1, source_target_pairs={{0,4},{4,0},{1,5},{5,1},{2,6},{6,2},{3,7},{7,3},{8,12},{12,8},{9,1... | collective-permute-start | bytes 1474568 | tf_op jit(solution)/shard_map/ppermute | solution.py:747
  566.6 43.4 %collective-permute-start.63 = (bf16[320,1536]{1,0:T(8,128)(2,1)}, bf16[320,1536]{1,0:T(8,128)(2,1)}, u32[]{:S(2)}, u32[]{:S(2)}) collective-permute-start(bf16[320,1536]{1,0:T(8,128)(2,1)} %pad_maximum_fusion.4.refs_2_), channel_id=1, source_target_pairs={{0,4},{4,0},{1,5},{5,1},{2,6},{6,2},{3,7},{7,3},{8,12},{12,8},{9,1... | collective-permute-start | bytes 2949128 | tf_op jit(solution)/shard_map/ppermute | solution.py:747
  568.6 41.3 %collective-permute-start.62 = (bf16[1,768,1536]{2,1,0:T(8,128)(2,1)}, bf16[1,768,1536]{2,1,0:T(8,128)(2,1)}, u32[]{:S(2)}, u32[]{:S(2)}) collective-permute-start(bf16[1,768,1536]{2,1,0:T(8,128)(2,1)} %shard_map.415), channel_id=1, source_target_pairs={{0,16},{1,17},{2,8},{3,9},{8,2},{9,3},{10,26},{11,27},{16,0},{17,1... | collective-permute-start | bytes 7077896 | tf_op jit(solution)/shard_map/ppermute | solution.py:753
  610.0 67.8 %collective-permute-start.67 = (bf16[1,768,1536]{2,1,0:T(8,128)(2,1)}, bf16[1,768,1536]{2,1,0:T(8,128)(2,1)}, u32[]{:S(2)}, u32[]{:S(2)}) collective-permute-start(bf16[1,768,1536]{2,1,0:T(8,128)(2,1)} %shard_map.413), channel_id=1, source_target_pairs={{0,4},{4,0},{1,5},{5,1},{2,6},{6,2},{3,7},{7,3},{8,12},{12,8},{9,1... | collective-permute-start | bytes 7077896 | tf_op jit(solution)/shard_map/ppermute | solution.py:747
  617.2 71.1 %collective-permute-start.69 = (bf16[1,768,1536]{2,1,0:T(8,128)(2,1)}, bf16[1,768,1536]{2,1,0:T(8,128)(2,1)}, u32[]{:S(2)}, u32[]{:S(2)}) collective-permute-start(bf16[1,768,1536]{2,1,0:T(8,128)(2,1)} %shard_map.417), channel_id=1, source_target_pairs={{0,16},{1,17},{2,8},{3,9},{8,2},{9,3},{10,26},{11,27},{16,0},{17,1... | collective-permute-start | bytes 7077896 | tf_op jit(solution)/shard_map/ppermute | solution.py:753
  631.7 46.0 %collective-permute-start.68 = (bf16[1184,384]{1,0:T(8,128)(2,1)}, bf16[1184,384]{1,0:T(8,128)(2,1)}, u32[]{:S(2)}, u32[]{:S(2)}) collective-permute-start(bf16[1184,384]{1,0:T(8,128)(2,1)} %get-tuple-element.474), channel_id=1, source_target_pairs={{0,1},{1,0},{2,3},{3,2},{4,5},{5,4},{6,7},{7,6},{8,9},{9,8},{10,11... | collective-permute-start | bytes 2727944 | tf_op jit(solution)/shard_map/ppermute | solution.py:744
  688.8 44.3 %collective-permute-start.72 = (bf16[1,768,1536]{2,1,0:T(8,128)(2,1)}, bf16[1,768,1536]{2,1,0:T(8,128)(2,1)}, u32[]{:S(2)}, u32[]{:S(2)}) collective-permute-start(bf16[1,768,1536]{2,1,0:T(8,128)(2,1)} %shard_map.421), channel_id=1, source_target_pairs={{0,16},{1,17},{2,8},{3,9},{8,2},{9,3},{10,26},{11,27},{16,0},{17,1... | collective-permute-start | bytes 7077896 | tf_op jit(solution)/shard_map/ppermute | solution.py:753
  696.2 53.7 %collective-permute-start.75 = (bf16[1,768,1536]{2,1,0:T(8,128)(2,1)}, bf16[1,768,1536]{2,1,0:T(8,128)(2,1)}, u32[]{:S(2)}, u32[]{:S(2)}) collective-permute-start(bf16[1,768,1536]{2,1,0:T(8,128)(2,1)} %shard_map.414), channel_id=1, source_target_pairs={{0,4},{4,0},{1,5},{5,1},{2,6},{6,2},{3,7},{7,3},{8,12},{12,8},{9,1... | collective-permute-start | bytes 7077896 | tf_op jit(solution)/shard_map/ppermute | solution.py:747
  698.6 47.1 %collective-permute-start.73 = (bf16[1184,384]{1,0:T(8,128)(2,1)}, bf16[1184,384]{1,0:T(8,128)(2,1)S(1)}, u32[]{:S(2)}, u32[]{:S(2)}) collective-permute-start(bf16[1184,384]{1,0:T(8,128)(2,1)} %get-tuple-element.488), channel_id=1, source_target_pairs={{0,1},{1,0},{2,3},{3,2},{4,5},{5,4},{6,7},{7,6},{8,9},{9,8},{10,11... | collective-permute-start | bytes 2727944 | tf_op jit(solution)/shard_map/ppermute | solution.py:744
  760.6 63.6 %collective-permute-start.77 = (bf16[1,768,1536]{2,1,0:T(8,128)(2,1)}, bf16[1,768,1536]{2,1,0:T(8,128)(2,1)}, u32[]{:S(2)}, u32[]{:S(2)}) collective-permute-start(bf16[1,768,1536]{2,1,0:T(8,128)(2,1)} %shard_map.423), channel_id=1, source_target_pairs={{0,16},{1,17},{2,8},{3,9},{8,2},{9,3},{10,26},{11,27},{16,0},{17,1... | collective-permute-start | bytes 7077896 | tf_op jit(solution)/shard_map/ppermute | solution.py:753
  829.9 44.6 %collective-permute-start.76 = (bf16[1184,384]{1,0:T(8,128)(2,1)}, bf16[1184,384]{1,0:T(8,128)(2,1)}, u32[]{:S(2)}, u32[]{:S(2)}) collective-permute-start(bf16[1184,384]{1,0:T(8,128)(2,1)} %get-tuple-element.493), channel_id=1, source_target_pairs={{0,16},{1,17},{2,8},{3,9},{8,2},{9,3},{10,26},{11,27},{16,0},{17,1... | collective-permute-start | bytes 2727944 | tf_op jit(solution)/shard_map/ppermute | solution.py:753
  839.7 41.3 %collective-permute-start.86 = (bf16[3,768,384]{2,1,0:T(8,128)(2,1)}, bf16[3,768,384]{2,1,0:T(8,128)(2,1)}, u32[]{:S(2)}, u32[]{:S(2)}) collective-permute-start(bf16[3,768,384]{2,1,0:T(8,128)(2,1)} %shard_map.424), channel_id=1, source_target_pairs={{0,4},{4,0},{1,5},{5,1},{2,6},{6,2},{3,7},{7,3},{8,12},{12,8},{9,1... | collective-permute-start | bytes 5308424 | tf_op jit(solution)/shard_map/ppermute | solution.py:747
  840.7 40.2 %collective-permute-start.83 = (bf16[3,768,384]{2,1,0:T(8,128)(2,1)}, bf16[3,768,384]{2,1,0:T(8,128)(2,1)}, u32[]{:S(2)}, u32[]{:S(2)}) collective-permute-start(bf16[3,768,384]{2,1,0:T(8,128)(2,1)} %shard_map.428), channel_id=1, source_target_pairs={{0,16},{1,17},{2,8},{3,9},{8,2},{9,3},{10,26},{11,27},{16,0},{17,1... | collective-permute-start | bytes 5308424 | tf_op jit(solution)/shard_map/ppermute | solution.py:753
  848.3 42.9 %collective-permute-start.84 = (bf16[1184,384]{1,0:T(8,128)(2,1)}, bf16[1184,384]{1,0:T(8,128)(2,1)}, u32[]{:S(2)}, u32[]{:S(2)}) collective-permute-start(bf16[1184,384]{1,0:T(8,128)(2,1)} %get-tuple-element.533), channel_id=1, source_target_pairs={{0,1},{1,0},{2,3},{3,2},{4,5},{5,4},{6,7},{7,6},{8,9},{9,8},{10,11... | collective-permute-start | bytes 2727944 | tf_op jit(solution)/shard_map/ppermute | solution.py:744
  874.4 45.1 %collective-permute-start.88 = (bf16[1184,384]{1,0:T(8,128)(2,1)}, bf16[1184,384]{1,0:T(8,128)(2,1)}, u32[]{:S(2)}, u32[]{:S(2)}) collective-permute-start(bf16[1184,384]{1,0:T(8,128)(2,1)} %fusion.18), channel_id=1, source_target_pairs={{0,16},{1,17},{2,8},{3,9},{8,2},{9,3},{10,26},{11,27},{16,0},{17,1... | collective-permute-start | bytes 2727944 | tf_op jit(solution)/shard_map/ppermute | solution.py:753
  912.6 73.1 %collective-permute-start.93 = (bf16[3,768,384]{2,1,0:T(8,128)(2,1)}, bf16[3,768,384]{2,1,0:T(8,128)(2,1)}, u32[]{:S(2)}, u32[]{:S(2)}) collective-permute-start(bf16[3,768,384]{2,1,0:T(8,128)(2,1)} %shard_map.432), channel_id=1, source_target_pairs={{0,16},{1,17},{2,8},{3,9},{8,2},{9,3},{10,26},{11,27},{16,0},{17,1... | collective-permute-start | bytes 5308424 | tf_op jit(solution)/shard_map/ppermute | solution.py:753
  919.6 53.7 %collective-permute-start.87 = (bf16[1184,384]{1,0:T(8,128)(2,1)}, bf16[1184,384]{1,0:T(8,128)(2,1)}, u32[]{:S(2)}, u32[]{:S(2)}) collective-permute-start(bf16[1184,384]{1,0:T(8,128)(2,1)} %get-tuple-element.538), channel_id=1, source_target_pairs={{0,16},{1,17},{2,8},{3,9},{8,2},{9,3},{10,26},{11,27},{16,0},{17,1... | collective-permute-start | bytes 2727944 | tf_op jit(solution)/shard_map/ppermute | solution.py:753
  (196 other events, 2627.8 us)

commit v5 on v4

--- a/solution.py
+++ b/solution.py
@@ -1250,7 +1250,6 @@
             sync(grads[4], gh1_mine[1], waiting[6], sent[0], results[0])
             send_update(3)
             grads[0] = keep_half(0, sent[0])
-            results.append(owned(res[1]))
             totals.append(row_sums(1))
             sent[5], sent[1] = over_y(sent_text), over_y(sent_one)
             small_sum(3)
@@ -1260,18 +1259,19 @@
             grads[5] = keep_half(1, sent[5], 1)
             grads[1] = keep_half(1, sent[1])
             optimize(4)
-            sync(grads[0], waiting[3], results[1], grads[5], grads[1])
+            sync(grads[0], waiting[3], grads[5], grads[1])
             totals[1] = row_total(*totals[1])
             send_update(2)
             send_update(4)
             finish(3)
             small_sum(2)
             small_sum(4)
+            results.append(owned(res[1]))
             row_grads(1, *totals[1])
             optimize(0)
             optimize(5)
             optimize(1)
-            sync(waiting[2], waiting[4])
+            sync(waiting[2], waiting[4], results[1])
             send_update(0)
             send_update(5)
             send_update(1)

time: 1100 us -> 1090 us (level)
    ppermute x29, starting transfers between devices: 61.8 us -> 50.6 us  [core_swap(): return lax.ppermute(a, 'group', core_perm)]
    unnamed x242 -> x238, local copies, waits for them, and re-layouts: 29.9 us -> 28.4 us
  transfers between devices with their start and end apart: 110 -> 110, of which waited for: 28 -> 29; matrix products, arithmetic and copies ran while one was open for 12% -> 12% of each run, Pallas kernels for 48% -> 49%
where the time goes in v5:
time: 1090 us; the launch traced here: 1080 us
  Pallas kernels  561 us (51%)
  waiting for transfers between devices  181 us (17%)
  starting transfers between devices  170 us (16%)
  other arithmetic  95.5 us (9%)
  local copies, waits for them, and re-layouts  67.3 us (6%)
    pallas_call x13, Pallas kernels, weight_grad(): call(kernel, (steps,), [left_spec] * n + [right_spec] * n + [out_spec] *...  102 us
    ppermute x15, waiting for transfers between devices, z_swap(): return lax.ppermute(a, 'mp', z_perm)  88.1 us
    pallas_call x2, Pallas kernels, mlp(): call(kernel, (steps,), [whole((rows, width)), whole((rows, width)), w1_sp...  81.4 us
    pallas_call x8, Pallas kernels, adam(): call(kernel, (4,), [pairs, grad, grad], [pairs, pl.BlockSpec((1, lead, pi...  75.8 us
    pallas_call x2, Pallas kernels, attend_back(): pl.pallas_call(kernel, grid=(pairs,), in_specs=[pl.BlockSpec((3, rows, 12...  65.9 us
    ppermute x29, starting transfers between devices, core_swap(): return lax.ppermute(a, 'group', core_perm)  50.6 us
    ppermute x13, starting transfers between devices, turn(): return lax.ppermute(a, ('group', 'mp'), turn_perm)  49.1 us
    pallas_call x2, Pallas kernels, attend(): pl.pallas_call(kernel, grid=(pairs,), in_specs=[pl.BlockSpec((3, rows, 12...  44.3 us
  transfers between devices with their start and end apart: 110, of which 29 were waited for; matrix products, arithmetic and copies ran while one was open for 12% of the time, Pallas kernels for 49%

profile of v5, /device:TPU:0, one launch (start us, length us, event | category | flops | bytes accessed | tf_op | source)
XLA Modules:
  0.0 1079.9 jit_solution(15585491450260795148)
XLA Ops:
  43.5 13.4 %collective-permute-done.8.refs_1_ = bf16[3,384,384]{2,1,0:T(8,128)(2,1)} collective-permute-done((bf16[3,384,384]{2,1,0:T(8,128)(2,1)S(1)}, bf16[3,384,384]{2,1,0:T(8,128)(2,1)}, u32[]{:S(2)}, u32[]{:S(2)}) %collective-permute-start.8) | collective-permute-done | bytes 884768 | tf_op jit(solution)/shard_map/ppermute | solution.py:741
  63.4 17.6 %collective-permute-done.13 = f32[32,384]{1,0:T(8,128)S(1)} collective-permute-done((f32[32,384]{1,0:T(8,128)S(1)}, f32[32,384]{1,0:T(8,128)S(1)}, u32[]{:S(2)}, u32[]{:S(2)}) %collective-permute-start.13) | collective-permute-done | bytes 49184 | tf_op jit(solution)/shard_map/ppermute | solution.py:744
  83.6 19.5 %collective-permute-start.15 = (bf16[1184,768]{1,0:T(8,128)(2,1)S(1)}, bf16[1184,768]{1,0:T(8,128)(2,1)}, u32[]{:S(2)}, u32[]{:S(2)}) collective-permute-start(bf16[1184,768]{1,0:T(8,128)(2,1)S(1)} %maximum_select_fusion.xm_ref), channel_id=1, source_target_pairs={{0,8},{8,0},{16,24},{24,16},{1,9},{9,1},{17,25},{25,17},{2,10},{10... | collective-permute-start | bytes 5455880 | tf_op jit(solution)/shard_map/ppermute | solution.py:738
  122.9 15.4 %shard_map.396 = (bf16[1184,1536]{1,0:T(8,128)(2,1)}, bf16[3,1184,384]{2,1,0:T(8,128)(2,1)}, f32[1184,384]{1,0:T(8,128)}, f32[1184,128]{1,0:T(8,128)}) custom-call(s32[10]{0:T(128)} %stack.170.ids_ref, bf16[1184,768]{1,0:T(8,128)(2,1)} %copy-done.25, bf16[1184,768]{1,0:T(8,128)(2,1)} %collective-permute-done.15.xo_ref, ...), custom_call_target="tpu_custom_call" | custom-call | flops 4190109 | bytes 17989 | tf_op jit(solution)/shard_map/pallas_call | solution.py:191
  163.8 22.2 %shard_map.399 = (bf16[1184,384]{1,0:T(8,128)(2,1)}, f32[3,8,1280]{2,1,0:T(8,128)}) custom-call(bf16[3,1184,384]{2,1,0:T(8,128)(2,1)} %get-tuple-element.456.qkv_ref), custom_call_target="tpu_custom_call" | custom-call | flops 8613003 | bytes 3637 | tf_op jit(solution)/shard_map/pallas_call | solution.py:248
  202.3 30.8 %collective-permute-done.30 = bf16[1184,384]{1,0:T(8,128)(2,1)S(1)} collective-permute-done((bf16[1184,384]{1,0:T(8,128)(2,1)}, bf16[1184,384]{1,0:T(8,128)(2,1)S(1)}, u32[]{:S(2)}, u32[]{:S(2)}) %collective-permute-start.30) | collective-permute-done | bytes 909344 | tf_op jit(solution)/shard_map/ppermute | solution.py:744
  242.6 15.4 %shard_map.401 = (bf16[1184,1536]{1,0:T(8,128)(2,1)}, bf16[3,1184,384]{2,1,0:T(8,128)(2,1)}, f32[1184,384]{1,0:T(8,128)}, f32[1184,128]{1,0:T(8,128)}) custom-call(s32[10]{0:T(128)} %stack.170.ids_ref, bf16[1184,768]{1,0:T(8,128)(2,1)} %copy-done.24, bf16[1184,768]{1,0:T(8,128)(2,1)} %collective-permute-done.31.xo_ref, ...), custom_call_target="tpu_custom_call" | custom-call | flops 4190109 | bytes 17989 | tf_op jit(solution)/shard_map/pallas_call | solution.py:191
  290.6 22.2 %shard_map.404 = (bf16[1184,384]{1,0:T(8,128)(2,1)}, f32[3,8,1280]{2,1,0:T(8,128)}) custom-call(bf16[3,1184,384]{2,1,0:T(8,128)(2,1)} %get-tuple-element.484.qkv_ref), custom_call_target="tpu_custom_call" | custom-call | flops 8613003 | bytes 3637 | tf_op jit(solution)/shard_map/pallas_call | solution.py:248
  327.9 17.1 %collective-permute-done.42 = bf16[1184,384]{1,0:T(8,128)(2,1)S(1)} collective-permute-done((bf16[1184,384]{1,0:T(8,128)(2,1)}, bf16[1184,384]{1,0:T(8,128)(2,1)S(1)}, u32[]{:S(2)}, u32[]{:S(2)}) %collective-permute-start.42) | collective-permute-done | bytes 909344 | tf_op jit(solution)/shard_map/ppermute | solution.py:744
  368.3 11.7 %shard_map.406 = (bf16[1184,1536]{1,0:T(8,128)(2,1)}, bf16[1184,1536]{1,0:T(8,128)(2,1)}, f32[1184,384]{1,0:T(8,128)}) custom-call(s32[10]{0:T(128)} %stack.170.ids_ref, f32[1]{0:T(128)} %bitcast.20.live_ref, bf16[1184,768]{1,0:T(8,128)(2,1)} %copy-done.25, bf16[1184,768]{1,0:T(8,128)(2,1)} %collective-permute-done.15.xo_ref, bf16[1184,768]{1,0:T(8,128)(2,1)} %copy-done.29, ...), custom_call_target="tpu_custom_call" | custom-call | flops 36372 | bytes 20004 | tf_op jit(solution)/shard_map/pallas_call | solution.py:426
  393.0 40.5 %shard_map.409 = (bf16[1184,1536]{1,0:T(8,128)(2,1)}, bf16[1184,1536]{1,0:T(8,128)(2,1)}, bf16[1184,768]{1,0:T(8,128)(2,1)}, bf16[1184,768]{1,0:T(8,128)(2,1)}, ...) custom-call(s32[10]{0:T(128)} %stack.170.ids_ref, bf16[1184,1536]{1,0:T(8,128)(2,1)} %get-tuple-element.491.h_ref.refs_0_, ...), custom_call_target="tpu_custom_call" | custom-call | flops 22347252 | bytes 40697 | tf_op jit(solution)/shard_map/pallas_call | solution.py:498
  446.8 11.7 %shard_map.410 = (bf16[1184,1536]{1,0:T(8,128)(2,1)}, bf16[1184,1536]{1,0:T(8,128)(2,1)}, f32[1184,384]{1,0:T(8,128)}) custom-call(s32[10]{0:T(128)} %stack.170.ids_ref, f32[1]{0:T(128)} %bitcast.35.live_ref, bf16[1184,768]{1,0:T(8,128)(2,1)} %copy-done.24, bf16[1184,768]{1,0:T(8,128)(2,1)} %collective-permute-done.31.xo_ref, ...), custom_call_target="tpu_custom_call" | custom-call | flops 36372 | bytes 20004 | tf_op jit(solution)/shard_map/pallas_call | solution.py:426
  462.4 40.9 %shard_map.411 = (bf16[1184,1536]{1,0:T(8,128)(2,1)}, bf16[1184,1536]{1,0:T(8,128)(2,1)}, bf16[1184,768]{1,0:T(8,128)(2,1)}, bf16[1184,768]{1,0:T(8,128)(2,1)}, ...) custom-call(s32[10]{0:T(128)} %stack.170.ids_ref, bf16[1184,1536]{1,0:T(8,128)(2,1)} %get-tuple-element.492.h_ref.refs_1_, ...), custom_call_target="tpu_custom_call" | custom-call | flops 22347252 | bytes 40697 | tf_op jit(solution)/shard_map/pallas_call | solution.py:498
  517.6 15.2 %shard_map.412 = (bf16[1184,1536]{1,0:T(8,128)(2,1)}, bf16[1184,384]{1,0:T(8,128)(2,1)}, f32[1184,384]{1,0:T(8,128)}, f32[2,24,384]{2,1,0:T(8,128)}) custom-call(s32[10]{0:T(128)} %stack.170.ids_ref, f32[1]{0:T(128)} %bitcast.20.live_ref, bf16[1184,768]{1,0:T(8,128)(2,1)} %copy-done.25, bf16[1184,768]{1,0:T(8,128)(2,1)} %collective-permute-done.15.xo_ref, ...), custom_call_target="tpu_custom_call" | custom-call | flops 1396703 | bytes 21823 | tf_op jit(solution)/shard_map/pallas_call | solution.py:570
  532.8 9.6 shard_map.413
  542.4 9.6 shard_map.414
  576.9 32.8 %shard_map.416.a_ref.refs_2_ = bf16[3,1184,384]{2,1,0:T(8,128)(2,1)} custom-call(bf16[3,1184,384]{2,1,0:T(8,128)(2,1)} %get-tuple-element.456.qkv_ref, bf16[1184,384]{1,0:T(8,128)(2,1)} %get-tuple-element.457.grad_ref, f32[3,8,1280]{2,1,0:T(8,128)} %get-tuple-element.458.lse_ref), custom_call_target="tpu_custom_call" | custom-call | flops 21532508 | bytes 6365 | tf_op jit(solution)/shard_map/pallas_call | solution.py:295
  618.4 11.8 %collective-permute-start.66 = (bf16[1184,768]{1,0:T(8,128)(2,1)S(1)}, bf16[1184,768]{1,0:T(8,128)(2,1)}, u32[]{:S(2)}, u32[]{:S(2)}) collective-permute-start(bf16[1184,768]{1,0:T(8,128)(2,1)S(1)} %add_convert_fusion.4.gm_ref), channel_id=1, source_target_pairs={{0,8},{8,0},{16,24},{24,16},{1,9},{9,1},{17,25},{25,17},{2,10},{10... | collective-permute-start | bytes 5455880 | tf_op jit(solution)/shard_map/ppermute | solution.py:738
  638.9 15.4 %shard_map.418 = (bf16[1184,1536]{1,0:T(8,128)(2,1)}, bf16[1184,384]{1,0:T(8,128)(2,1)}, f32[1184,384]{1,0:T(8,128)}, f32[2,24,384]{2,1,0:T(8,128)}) custom-call(s32[10]{0:T(128)} %stack.170.ids_ref, f32[1]{0:T(128)} %bitcast.35.live_ref, bf16[1184,768]{1,0:T(8,128)(2,1)} %copy-done.24, bf16[1184,768]{1,0:T(8,128)(2,1)} %collective-permute-done.31.xo_ref, ...), custom_call_target="tpu_custom_call" | custom-call | flops 1396703 | bytes 21823 | tf_op jit(solution)/shard_map/pallas_call | solution.py:570
  654.3 11.9 %shard_map.419 = (bf16[1184,768]{1,0:T(8,128)(2,1)}, bf16[1184,768]{1,0:T(8,128)(2,1)}) custom-call(s32[10]{0:T(128)} %stack.170.ids_ref, bf16[3,1184,384]{2,1,0:T(8,128)(2,1)} %shard_map.416.a_ref.refs_2_, bf16[3,1536,384]{2,1,0:T(8,128)(2,1)} %copy-done, bf16[3,1536,384]{2,1,0:T(8,128)(2,1)} %copy-done.1), custom_call_target="tpu_custom_call" | custom-call | flops 4190109 | bytes 16171 | tf_op jit(solution)/shard_map/pallas_call | solution.py:376
  666.2 11.5 %shard_map.420 = (f32[2,1,4,192,1536]{4,3,2,1,0:T(8,128)}, bf16[2,1,192,1536]{3,2,1,0:T(8,128)(2,1)}, bf16[2,1,192,1536]{3,2,1,0:T(8,128)(2,1)}) custom-call(s32[10]{0:T(128)} %stack.170.ids_ref, f32[1]{0:T(128)} %bitcast.36.inv_ref, f32[2,1,4,192,1536]{4,3,2,1,0:T(8,128)} %bitcast.175, bf16[1,4,192,1536]{3,2,1,0:T(8,128)(2,1)} %bitcast.190, ...), custom_call_target="tpu_custom_call" | custom-call | flops 23592 | bytes 23592 | tf_op jit(solution)/shard_map/pallas_call | solution.py:677
  677.7 10.5 shard_map.421
  700.1 33.0 %shard_map.422.refs_3_.a_ref = bf16[3,1184,384]{2,1,0:T(8,128)(2,1)} custom-call(bf16[3,1184,384]{2,1,0:T(8,128)(2,1)} %get-tuple-element.484.qkv_ref, bf16[1184,384]{1,0:T(8,128)(2,1)} %get-tuple-element.485.grad_ref, f32[3,8,1280]{2,1,0:T(8,128)} %get-tuple-element.486.lse_ref), custom_call_target="tpu_custom_call" | custom-call | flops 21532508 | bytes 6365 | tf_op jit(solution)/shard_map/pallas_call | solution.py:295
  733.1 12.6 %collective-permute-done.73 = bf16[1184,384]{1,0:T(8,128)(2,1)S(1)} collective-permute-done((bf16[1184,384]{1,0:T(8,128)(2,1)}, bf16[1184,384]{1,0:T(8,128)(2,1)S(1)}, u32[]{:S(2)}, u32[]{:S(2)}) %collective-permute-start.73) | collective-permute-done | bytes 909344 | tf_op jit(solution)/shard_map/ppermute | solution.py:744
  749.8 10.7 shard_map.423
  775.1 11.9 %shard_map.425 = (bf16[1184,768]{1,0:T(8,128)(2,1)}, bf16[1184,768]{1,0:T(8,128)(2,1)}) custom-call(s32[10]{0:T(128)} %stack.170.ids_ref, bf16[3,1184,384]{2,1,0:T(8,128)(2,1)} %shard_map.422.refs_3_.a_ref, bf16[3,1536,384]{2,1,0:T(8,128)(2,1)} %copy-done, bf16[3,1536,384]{2,1,0:T(8,128)(2,1)} %copy-done.1), custom_call_target="tpu_custom_call" | custom-call | flops 4190109 | bytes 16171 | tf_op jit(solution)/shard_map/pallas_call | solution.py:376
  808.4 11.5 %shard_map.427 = (f32[2,1,4,192,1536]{4,3,2,1,0:T(8,128)}, bf16[2,1,192,1536]{3,2,1,0:T(8,128)(2,1)}, bf16[2,1,192,1536]{3,2,1,0:T(8,128)(2,1)}) custom-call(s32[10]{0:T(128)} %stack.170.ids_ref, f32[1]{0:T(128)} %bitcast.36.inv_ref, f32[2,1,4,192,1536]{4,3,2,1,0:T(8,128)} %bitcast.176, bf16[1,4,192,1536]{3,2,1,0:T(8,128)(2,1)} %bitcast.189, ...), custom_call_target="tpu_custom_call" | custom-call | flops 23592 | bytes 23592 | tf_op jit(solution)/shard_map/pallas_call | solution.py:677
  851.7 11.7 %shard_map.429 = (f32[2,1,4,192,1536]{4,3,2,1,0:T(8,128)}, bf16[2,1,192,1536]{3,2,1,0:T(8,128)(2,1)}, bf16[2,1,192,1536]{3,2,1,0:T(8,128)(2,1)}) custom-call(s32[10]{0:T(128)} %stack.170.ids_ref, f32[1]{0:T(128)} %bitcast.36.inv_ref, f32[2,1,4,192,1536]{4,3,2,1,0:T(8,128)} %bitcast.177, bf16[1,4,192,1536]{3,2,1,0:T(8,128)(2,1)} %bitcast.188, ...), custom_call_target="tpu_custom_call" | custom-call | flops 23592 | bytes 23592 | tf_op jit(solution)/shard_map/pallas_call | solution.py:677
  880.9 10.1 collective-permute-done.85
  891.0 10.0 shard_map.432
  901.0 11.4 %collective-permute-start.87 = (bf16[2,1,192,1536]{3,2,1,0:T(8,128)(2,1)}, bf16[2,1,192,1536]{3,2,1,0:T(8,128)(2,1)}, u32[]{:S(2)}, u32[]{:S(2)}) collective-permute-start(bf16[2,1,192,1536]{3,2,1,0:T(8,128)(2,1)} %get-tuple-element.543), channel_id=1, source_target_pairs={{0,8},{8,0},{16,24},{24,16},{1,9},{9,1},{17,25},{25,17},{2,10},{10... | collective-permute-start | bytes 3538952 | tf_op jit(solution)/shard_map/ppermute | solution.py:738
  927.2 11.5 %shard_map.434 = (f32[2,1,4,192,1536]{4,3,2,1,0:T(8,128)}, bf16[2,1,192,1536]{3,2,1,0:T(8,128)(2,1)}, bf16[2,1,192,1536]{3,2,1,0:T(8,128)(2,1)}) custom-call(s32[10]{0:T(128)} %stack.170.ids_ref, f32[1]{0:T(128)} %bitcast.36.inv_ref, f32[2,1,4,192,1536]{4,3,2,1,0:T(8,128)} %bitcast.178, bf16[1,4,192,1536]{3,2,1,0:T(8,128)(2,1)} %bitcast.187, ...), custom_call_target="tpu_custom_call" | custom-call | flops 23592 | bytes 23592 | tf_op jit(solution)/shard_map/pallas_call | solution.py:677
  (648 shorter events, 533.9 us)
Async XLA Ops:
  61.6 41.5 %collective-permute-start.14 = (bf16[2,96,1536]{2,1,0:T(8,128)(2,1)}, bf16[2,96,1536]{2,1,0:T(8,128)(2,1)S(1)}, u32[]{:S(2)}, u32[]{:S(2)}) collective-permute-start(bf16[2,96,1536]{2,1,0:T(8,128)(2,1)} %get-tuple-element.333), channel_id=1, source_target_pairs={{0,0},{1,1},{2,8},{3,9},{8,2},{9,3},{10,10},{11,11},{16,16},{17,17... | collective-permute-start | bytes 1769480 | tf_op jit(solution)/shard_map/ppermute | solution.py:750
  83.6 39.3 %collective-permute-start.15 = (bf16[1184,768]{1,0:T(8,128)(2,1)S(1)}, bf16[1184,768]{1,0:T(8,128)(2,1)}, u32[]{:S(2)}, u32[]{:S(2)}) collective-permute-start(bf16[1184,768]{1,0:T(8,128)(2,1)S(1)} %maximum_select_fusion.xm_ref), channel_id=1, source_target_pairs={{0,8},{8,0},{16,24},{24,16},{1,9},{9,1},{17,25},{25,17},{2,10},{10... | collective-permute-start | bytes 5455880 | tf_op jit(solution)/shard_map/ppermute | solution.py:738
  140.4 52.8 %collective-permute-start.25 = (bf16[1,384,1536]{2,1,0:T(8,128)(2,1)}, bf16[1,384,1536]{2,1,0:T(8,128)(2,1)S(1)}, u32[]{:S(2)}, u32[]{:S(2)}) collective-permute-start(bf16[1,384,1536]{2,1,0:T(8,128)(2,1)} %get-tuple-element.355), channel_id=1, source_target_pairs={{0,0},{1,1},{2,8},{3,9},{8,2},{9,3},{10,10},{11,11},{16,16},{17,17... | collective-permute-start | bytes 3538952 | tf_op jit(solution)/shard_map/ppermute | solution.py:750
  148.6 44.7 %collective-permute-start.23 = (bf16[1,384,1536]{2,1,0:T(8,128)(2,1)S(1)}, bf16[1,384,1536]{2,1,0:T(8,128)(2,1)S(1)}, u32[]{:S(2)}, u32[]{:S(2)}) collective-permute-start(bf16[1,384,1536]{2,1,0:T(8,128)(2,1)S(1)} %collective-permute-done.19.refs_0_), channel_id=1, source_target_pairs={{0,16},{8,24},{16,0},{24,8},{1,17},{9,25},{17,1},{25,9},{2,18},{10... | collective-permute-start | bytes 3538952 | tf_op jit(solution)/shard_map/ppermute | solution.py:741
  149.4 44.9 %collective-permute-start.24 = (bf16[1,384,1536]{2,1,0:T(8,128)(2,1)S(1)}, bf16[1,384,1536]{2,1,0:T(8,128)(2,1)}, u32[]{:S(2)}, u32[]{:S(2)}) collective-permute-start(bf16[1,384,1536]{2,1,0:T(8,128)(2,1)S(1)} %collective-permute-done.19.refs_0_), channel_id=1, source_target_pairs={{0,4},{4,0},{1,5},{5,1},{2,6},{6,2},{3,7},{7,3},{8,12},{12,8},{9,1... | collective-permute-start | bytes 3538952 | tf_op jit(solution)/shard_map/ppermute | solution.py:747
  151.5 41.7 %collective-permute-start.22 = (bf16[1184,384]{1,0:T(8,128)(2,1)}, bf16[1184,384]{1,0:T(8,128)(2,1)}, u32[]{:S(2)}, u32[]{:S(2)}) collective-permute-start(bf16[1184,384]{1,0:T(8,128)(2,1)} %fusion.34), channel_id=1, source_target_pairs={{0,0},{1,1},{2,8},{3,9},{8,2},{9,3},{10,10},{11,11},{16,16},{17,17... | collective-permute-start | bytes 2727944 | tf_op jit(solution)/shard_map/ppermute | solution.py:750
  241.3 71.4 %collective-permute-start.38 = (bf16[1184,768]{1,0:T(8,128)(2,1)}, bf16[1184,768]{1,0:T(8,128)(2,1)}, u32[]{:S(2)}, u32[]{:S(2)}) collective-permute-start(bf16[1184,768]{1,0:T(8,128)(2,1)} %add_convert_fusion.11), channel_id=1, source_target_pairs={{0,1},{1,0},{2,3},{3,2},{4,5},{5,4},{6,7},{7,6},{8,9},{9,8},{10,11... | collective-permute-start | bytes 5455880 | tf_op jit(solution)/shard_map/ppermute | solution.py:744
  268.2 44.6 %collective-permute-start.36 = (bf16[1,384,1536]{2,1,0:T(8,128)(2,1)S(1)}, bf16[1,384,1536]{2,1,0:T(8,128)(2,1)}, u32[]{:S(2)}, u32[]{:S(2)}) collective-permute-start(bf16[1,384,1536]{2,1,0:T(8,128)(2,1)S(1)} %collective-permute-done.29.refs_0_), channel_id=1, source_target_pairs={{0,16},{8,24},{16,0},{24,8},{1,17},{9,25},{17,1},{25,9},{2,18},{10... | collective-permute-start | bytes 3538952 | tf_op jit(solution)/shard_map/ppermute | solution.py:741
  269.0 43.7 %collective-permute-start.37 = (bf16[1,384,1536]{2,1,0:T(8,128)(2,1)S(1)}, bf16[1,384,1536]{2,1,0:T(8,128)(2,1)}, u32[]{:S(2)}, u32[]{:S(2)}) collective-permute-start(bf16[1,384,1536]{2,1,0:T(8,128)(2,1)S(1)} %collective-permute-done.29.refs_0_), channel_id=1, source_target_pairs={{0,4},{4,0},{1,5},{5,1},{2,6},{6,2},{3,7},{7,3},{8,12},{12,8},{9,1... | collective-permute-start | bytes 3538952 | tf_op jit(solution)/shard_map/ppermute | solution.py:747
  272.1 40.7 %collective-permute-start.35 = (bf16[1184,384]{1,0:T(8,128)(2,1)}, bf16[1184,384]{1,0:T(8,128)(2,1)}, u32[]{:S(2)}, u32[]{:S(2)}) collective-permute-start(bf16[1184,384]{1,0:T(8,128)(2,1)} %fusion.33), channel_id=1, source_target_pairs={{0,0},{1,1},{2,8},{3,9},{8,2},{9,3},{10,10},{11,11},{16,16},{17,17... | collective-permute-start | bytes 2727944 | tf_op jit(solution)/shard_map/ppermute | solution.py:750
  365.6 68.0 %collective-permute-start.48 = (bf16[1184,768]{1,0:T(8,128)(2,1)}, bf16[1184,768]{1,0:T(8,128)(2,1)}, u32[]{:S(2)}, u32[]{:S(2)}) collective-permute-start(bf16[1184,768]{1,0:T(8,128)(2,1)} %add_convert_fusion.9), channel_id=1, source_target_pairs={{0,1},{1,0},{2,3},{3,2},{4,5},{5,4},{6,7},{7,6},{8,9},{9,8},{10,11... | collective-permute-start | bytes 5455880 | tf_op jit(solution)/shard_map/ppermute | solution.py:744
  382.4 51.1 %collective-permute-start.49 = (bf16[1184,384]{1,0:T(8,128)(2,1)}, bf16[1184,384]{1,0:T(8,128)(2,1)}, u32[]{:S(2)}, u32[]{:S(2)}) collective-permute-start(bf16[1184,384]{1,0:T(8,128)(2,1)} %collective-permute-done.47), channel_id=1, source_target_pairs={{0,1},{1,0},{2,3},{3,2},{4,5},{5,4},{6,7},{7,6},{8,9},{9,8},{10,11... | collective-permute-start | bytes 2727944 | tf_op jit(solution)/shard_map/ppermute | solution.py:744
  442.2 61.0 %collective-permute-start.53 = (bf16[1184,768]{1,0:T(8,128)(2,1)}, bf16[1184,768]{1,0:T(8,128)(2,1)}, u32[]{:S(2)}, u32[]{:S(2)}) collective-permute-start(bf16[1184,768]{1,0:T(8,128)(2,1)} %add_convert_fusion.7), channel_id=1, source_target_pairs={{0,1},{1,0},{2,3},{3,2},{4,5},{5,4},{6,7},{7,6},{8,9},{9,8},{10,11... | collective-permute-start | bytes 5455880 | tf_op jit(solution)/shard_map/ppermute | solution.py:744
  461.5 41.7 %collective-permute-start.54 = (bf16[320,768]{1,0:T(8,128)(2,1)S(1)}, bf16[320,768]{1,0:T(8,128)(2,1)S(1)}, u32[]{:S(2)}, u32[]{:S(2)}) collective-permute-start(bf16[320,768]{1,0:T(8,128)(2,1)S(1)} %get-tuple-element.420), channel_id=1, source_target_pairs={{0,4},{4,0},{1,5},{5,1},{2,6},{6,2},{3,7},{7,3},{8,12},{12,8},{9,1... | collective-permute-start | bytes 1474568 | tf_op jit(solution)/shard_map/ppermute | solution.py:747
  514.1 43.5 %collective-permute-start.59 = (bf16[1184,768]{1,0:T(8,128)(2,1)S(1)}, bf16[1184,768]{1,0:T(8,128)(2,1)}, u32[]{:S(2)}, u32[]{:S(2)}) collective-permute-start(bf16[1184,768]{1,0:T(8,128)(2,1)S(1)} %add_convert_fusion.5), channel_id=1, source_target_pairs={{0,1},{1,0},{2,3},{3,2},{4,5},{5,4},{6,7},{7,6},{8,9},{9,8},{10,11... | collective-permute-start | bytes 5455880 | tf_op jit(solution)/shard_map/ppermute | solution.py:744
  515.6 42.0 %collective-permute-start.58 = (bf16[320,1536]{1,0:T(8,128)(2,1)}, bf16[320,1536]{1,0:T(8,128)(2,1)}, u32[]{:S(2)}, u32[]{:S(2)}) collective-permute-start(bf16[320,1536]{1,0:T(8,128)(2,1)} %pad_maximum_fusion.2.refs_2_), channel_id=1, source_target_pairs={{0,4},{4,0},{1,5},{5,1},{2,6},{6,2},{3,7},{7,3},{8,12},{12,8},{9,1... | collective-permute-start | bytes 2949128 | tf_op jit(solution)/shard_map/ppermute | solution.py:747
  516.7 40.8 %collective-permute-start.57 = (bf16[320,768]{1,0:T(8,128)(2,1)S(1)}, bf16[320,768]{1,0:T(8,128)(2,1)}, u32[]{:S(2)}, u32[]{:S(2)}) collective-permute-start(bf16[320,768]{1,0:T(8,128)(2,1)S(1)} %get-tuple-element.443), channel_id=1, source_target_pairs={{0,4},{4,0},{1,5},{5,1},{2,6},{6,2},{3,7},{7,3},{8,12},{12,8},{9,1... | collective-permute-start | bytes 1474568 | tf_op jit(solution)/shard_map/ppermute | solution.py:747
  566.6 43.2 %collective-permute-start.63 = (bf16[320,1536]{1,0:T(8,128)(2,1)}, bf16[320,1536]{1,0:T(8,128)(2,1)}, u32[]{:S(2)}, u32[]{:S(2)}) collective-permute-start(bf16[320,1536]{1,0:T(8,128)(2,1)} %pad_maximum_fusion.4.refs_2_), channel_id=1, source_target_pairs={{0,4},{4,0},{1,5},{5,1},{2,6},{6,2},{3,7},{7,3},{8,12},{12,8},{9,1... | collective-permute-start | bytes 2949128 | tf_op jit(solution)/shard_map/ppermute | solution.py:747
  568.6 41.1 %collective-permute-start.62 = (bf16[1,768,1536]{2,1,0:T(8,128)(2,1)}, bf16[1,768,1536]{2,1,0:T(8,128)(2,1)}, u32[]{:S(2)}, u32[]{:S(2)}) collective-permute-start(bf16[1,768,1536]{2,1,0:T(8,128)(2,1)} %shard_map.415), channel_id=1, source_target_pairs={{0,16},{1,17},{2,8},{3,9},{8,2},{9,3},{10,26},{11,27},{16,0},{17,1... | collective-permute-start | bytes 7077896 | tf_op jit(solution)/shard_map/ppermute | solution.py:753
  609.8 67.9 %collective-permute-start.67 = (bf16[1,768,1536]{2,1,0:T(8,128)(2,1)}, bf16[1,768,1536]{2,1,0:T(8,128)(2,1)}, u32[]{:S(2)}, u32[]{:S(2)}) collective-permute-start(bf16[1,768,1536]{2,1,0:T(8,128)(2,1)} %shard_map.413), channel_id=1, source_target_pairs={{0,4},{4,0},{1,5},{5,1},{2,6},{6,2},{3,7},{7,3},{8,12},{12,8},{9,1... | collective-permute-start | bytes 7077896 | tf_op jit(solution)/shard_map/ppermute | solution.py:747
  617.2 71.0 %collective-permute-start.69 = (bf16[1,768,1536]{2,1,0:T(8,128)(2,1)}, bf16[1,768,1536]{2,1,0:T(8,128)(2,1)}, u32[]{:S(2)}, u32[]{:S(2)}) collective-permute-start(bf16[1,768,1536]{2,1,0:T(8,128)(2,1)} %shard_map.417), channel_id=1, source_target_pairs={{0,16},{1,17},{2,8},{3,9},{8,2},{9,3},{10,26},{11,27},{16,0},{17,1... | collective-permute-start | bytes 7077896 | tf_op jit(solution)/shard_map/ppermute | solution.py:753
  631.7 46.0 %collective-permute-start.68 = (bf16[1184,384]{1,0:T(8,128)(2,1)}, bf16[1184,384]{1,0:T(8,128)(2,1)}, u32[]{:S(2)}, u32[]{:S(2)}) collective-permute-start(bf16[1184,384]{1,0:T(8,128)(2,1)} %get-tuple-element.474), channel_id=1, source_target_pairs={{0,1},{1,0},{2,3},{3,2},{4,5},{5,4},{6,7},{7,6},{8,9},{9,8},{10,11... | collective-permute-start | bytes 2727944 | tf_op jit(solution)/shard_map/ppermute | solution.py:744
  688.7 44.4 %collective-permute-start.72 = (bf16[1,768,1536]{2,1,0:T(8,128)(2,1)}, bf16[1,768,1536]{2,1,0:T(8,128)(2,1)}, u32[]{:S(2)}, u32[]{:S(2)}) collective-permute-start(bf16[1,768,1536]{2,1,0:T(8,128)(2,1)} %shard_map.421), channel_id=1, source_target_pairs={{0,16},{1,17},{2,8},{3,9},{8,2},{9,3},{10,26},{11,27},{16,0},{17,1... | collective-permute-start | bytes 7077896 | tf_op jit(solution)/shard_map/ppermute | solution.py:753
  696.2 53.7 %collective-permute-start.75 = (bf16[1,768,1536]{2,1,0:T(8,128)(2,1)}, bf16[1,768,1536]{2,1,0:T(8,128)(2,1)}, u32[]{:S(2)}, u32[]{:S(2)}) collective-permute-start(bf16[1,768,1536]{2,1,0:T(8,128)(2,1)} %shard_map.414), channel_id=1, source_target_pairs={{0,4},{4,0},{1,5},{5,1},{2,6},{6,2},{3,7},{7,3},{8,12},{12,8},{9,1... | collective-permute-start | bytes 7077896 | tf_op jit(solution)/shard_map/ppermute | solution.py:747
  698.6 47.1 %collective-permute-start.73 = (bf16[1184,384]{1,0:T(8,128)(2,1)}, bf16[1184,384]{1,0:T(8,128)(2,1)S(1)}, u32[]{:S(2)}, u32[]{:S(2)}) collective-permute-start(bf16[1184,384]{1,0:T(8,128)(2,1)} %get-tuple-element.488), channel_id=1, source_target_pairs={{0,1},{1,0},{2,3},{3,2},{4,5},{5,4},{6,7},{7,6},{8,9},{9,8},{10,11... | collective-permute-start | bytes 2727944 | tf_op jit(solution)/shard_map/ppermute | solution.py:744
  760.5 63.6 %collective-permute-start.77 = (bf16[1,768,1536]{2,1,0:T(8,128)(2,1)}, bf16[1,768,1536]{2,1,0:T(8,128)(2,1)}, u32[]{:S(2)}, u32[]{:S(2)}) collective-permute-start(bf16[1,768,1536]{2,1,0:T(8,128)(2,1)} %shard_map.423), channel_id=1, source_target_pairs={{0,16},{1,17},{2,8},{3,9},{8,2},{9,3},{10,26},{11,27},{16,0},{17,1... | collective-permute-start | bytes 7077896 | tf_op jit(solution)/shard_map/ppermute | solution.py:753
  830.0 44.7 %collective-permute-start.76 = (bf16[1184,384]{1,0:T(8,128)(2,1)}, bf16[1184,384]{1,0:T(8,128)(2,1)}, u32[]{:S(2)}, u32[]{:S(2)}) collective-permute-start(bf16[1184,384]{1,0:T(8,128)(2,1)} %get-tuple-element.493), channel_id=1, source_target_pairs={{0,16},{1,17},{2,8},{3,9},{8,2},{9,3},{10,26},{11,27},{16,0},{17,1... | collective-permute-start | bytes 2727944 | tf_op jit(solution)/shard_map/ppermute | solution.py:753
  839.5 41.3 %collective-permute-start.86 = (bf16[3,768,384]{2,1,0:T(8,128)(2,1)}, bf16[3,768,384]{2,1,0:T(8,128)(2,1)}, u32[]{:S(2)}, u32[]{:S(2)}) collective-permute-start(bf16[3,768,384]{2,1,0:T(8,128)(2,1)} %shard_map.424), channel_id=1, source_target_pairs={{0,4},{4,0},{1,5},{5,1},{2,6},{6,2},{3,7},{7,3},{8,12},{12,8},{9,1... | collective-permute-start | bytes 5308424 | tf_op jit(solution)/shard_map/ppermute | solution.py:747
  840.7 40.1 %collective-permute-start.84 = (bf16[3,768,384]{2,1,0:T(8,128)(2,1)}, bf16[3,768,384]{2,1,0:T(8,128)(2,1)}, u32[]{:S(2)}, u32[]{:S(2)}) collective-permute-start(bf16[3,768,384]{2,1,0:T(8,128)(2,1)} %shard_map.428), channel_id=1, source_target_pairs={{0,16},{1,17},{2,8},{3,9},{8,2},{9,3},{10,26},{11,27},{16,0},{17,1... | collective-permute-start | bytes 5308424 | tf_op jit(solution)/shard_map/ppermute | solution.py:753
  848.2 42.8 %collective-permute-start.85 = (bf16[1184,384]{1,0:T(8,128)(2,1)}, bf16[1184,384]{1,0:T(8,128)(2,1)}, u32[]{:S(2)}, u32[]{:S(2)}) collective-permute-start(bf16[1184,384]{1,0:T(8,128)(2,1)} %get-tuple-element.535), channel_id=1, source_target_pairs={{0,1},{1,0},{2,3},{3,2},{4,5},{5,4},{6,7},{7,6},{8,9},{9,8},{10,11... | collective-permute-start | bytes 2727944 | tf_op jit(solution)/shard_map/ppermute | solution.py:744
  874.7 64.0 %collective-permute-start.91 = (bf16[1184,384]{1,0:T(8,128)(2,1)}, bf16[1184,384]{1,0:T(8,128)(2,1)}, u32[]{:S(2)}, u32[]{:S(2)}) collective-permute-start(bf16[1184,384]{1,0:T(8,128)(2,1)} %fusion.18), channel_id=1, source_target_pairs={{0,16},{1,17},{2,8},{3,9},{8,2},{9,3},{10,26},{11,27},{16,0},{17,1... | collective-permute-start | bytes 2727944 | tf_op jit(solution)/shard_map/ppermute | solution.py:753
  912.4 73.2 %collective-permute-start.93 = (bf16[3,768,384]{2,1,0:T(8,128)(2,1)}, bf16[3,768,384]{2,1,0:T(8,128)(2,1)}, u32[]{:S(2)}, u32[]{:S(2)}) collective-permute-start(bf16[3,768,384]{2,1,0:T(8,128)(2,1)} %shard_map.432), channel_id=1, source_target_pairs={{0,16},{1,17},{2,8},{3,9},{8,2},{9,3},{10,26},{11,27},{16,0},{17,1... | collective-permute-start | bytes 5308424 | tf_op jit(solution)/shard_map/ppermute | solution.py:753
  (194 other events, 2599.6 us)
